TPU v7x, 512 devices: a whole 4x8x8 slice. The times are simulated.
512 devices in a mesh: grp: 32 (over x, z_lo, core), fsdp: 8 (over y), rep: 2 (over z_hi).
Axes of the slice: x: 4, y: 8, z: 8 (z_hi: 2, z_lo: 4; z = z_hi * 4 + z_lo), core: 2. Of those that a mesh axis runs over, the one named last changes fastest.
Arguments:
- grad_parts: bfloat16 [2, 4608, 4608], P('rep', 'grp', 'fsdp'), may hold values from -6 to 6
- basis_in: float32 [4608, 4608], P('grp', 'fsdp'), may hold values from -0.09375 to 0.09375
- basis_out: float32 [4608, 4608], P('grp', 'fsdp'), may hold values from -0.09375 to 0.09375
- eig_in: float32 [4608], replicated, may hold values from 0.3 to 3
- eig_out: float32 [4608], replicated, may hold values from 0.3 to 3
Outputs:
- preconditioned: bfloat16 [4608, 4608], P('grp', ('fsdp', 'rep'))
All inputs are finite; a program needn't handle non-finite values.
Results may differ from a plain program's by a relative error of at most 0.03.
Values may be sent and summed in bfloat16 or wider, within the bound.
No kernel may reach another device: no remote copies, remote signals or barrier semaphores. Data moves between devices by JAX's collectives and lax.ppermute only.
A program may use at most 64 MiB of HBM per device.

v0:
```python
import jax
import jax.numpy as jnp
from jax import lax
from jax.sharding import PartitionSpec as P

DAMPING = 0.1


def contract_last(left, right):
    return lax.dot_general(
        left, right, (((1,), (1,)), ((), ())), preferred_element_type=jnp.float32
    )


def contract_first(left, right):
    return lax.dot_general(
        left, right, (((0,), (0,)), ((), ())), preferred_element_type=jnp.float32
    )


def body(grad_parts, basis_in, basis_out, eig_in, eig_out):
    rep_index = lax.axis_index("rep")
    grp_index = lax.axis_index("grp")
    block_index = lax.axis_index("fsdp") * lax.axis_size("rep") + rep_index
    local_grad = grad_parts[0]
    partial_rows = lax.all_gather(local_grad, "fsdp", axis=1, tiled=True)
    grad_rows = lax.psum(partial_rows.astype(jnp.float32).astype(jnp.bfloat16), "rep")
    half_width = basis_in.shape[1] // lax.axis_size("rep")
    in_half = lax.dynamic_slice_in_dim(basis_in, rep_index * half_width, half_width, 1).astype(
        jnp.bfloat16
    )
    columns = grad_rows
    rotated_in = jnp.dot(
        columns,
        lax.all_gather(in_half, "grp", axis=0, tiled=True),
        preferred_element_type=jnp.float32,
    )
    rotated_in = rotated_in.astype(jnp.bfloat16)
    out_rows = lax.all_gather(basis_out.astype(jnp.bfloat16), "fsdp", axis=1, tiled=True)
    out_count = out_rows.shape[0]
    columns = out_rows
    rotated = jnp.dot(
        columns,
        lax.all_gather(rotated_in, "grp", axis=0, tiled=True),
        preferred_element_type=jnp.float32,
    )
    out_scale = lax.dynamic_slice_in_dim(eig_out, grp_index * out_count, out_count, 0)
    in_scale = lax.dynamic_slice_in_dim(eig_in, block_index * half_width, half_width, 0)
    scaled = (rotated / (out_scale[:, None] * in_scale[None, :] + DAMPING)).astype(jnp.bfloat16)
    back_terms = contract_last(scaled, lax.all_gather(in_half, "grp", axis=0, tiled=True))
    back_in = lax.psum_scatter(
        back_terms.astype(jnp.bfloat16), ("fsdp", "rep"), scatter_dimension=1, tiled=True
    )
    return lax.psum_scatter(
        contract_first(out_rows, back_in).astype(jnp.bfloat16),
        "grp",
        scatter_dimension=0,
        tiled=True,
    )


def solution(mesh):
    in_specs = (P("rep", "grp", "fsdp"), P("grp", "fsdp"), P("grp", "fsdp"), P(), P())
    out_specs = P("grp", ("fsdp", "rep"))
    return jax.shard_map(body, mesh=mesh, in_specs=in_specs, out_specs=out_specs, check_vma=False)
```

profile of v0, /device:TPU:1, one launch (start us, length us, event | category | flops | bytes accessed | tf_op | source)
XLA Modules:
  0.0 716.1 jit_solution(1511349153323516137)
XLA Ops:
  7.4 2.1 copy.12
  9.5 0.0 all-gather.11.cloned.1.call-update
  9.5 0.0 all-reduce.2.cloned.1.call-start
  9.6 68.2 %all-gather.11.cloned.1.call-done = bf16[1,144,4608]{1,0,2:T(2,128)(2,1)} async-done(((bf16[1,144,576]{1,0,2:T(2,128)(2,1)}), bf16[1,144,4608]{1,0,2:T(2,128)(2,1)}) %all-gather.11.cloned.1.call-update) | async-done | bytes 1327120 | tf_op jit(solution)/shard_map/all_gather | solution.py:26
  77.8 10.7 %copy.13 = bf16[1,144,4608]{2,1,0:T(8,128)(2,1)} copy(bf16[1,144,4608]{1,0,2:T(2,128)(2,1)} %all-gather.11.cloned.1.call-done) | data formatting | bytes 2654208 | tf_op jit(solution)/shard_map/all_gather | solution.py:26
  88.5 0.0 all-reduce.2.cloned.1.call-update
  88.5 0.0 all-gather.7.cloned.1.call-start
  88.6 0.8 dynamic-slice_convert_fusion
  89.4 0.0 all-gather.7.cloned.1.call-update
  89.4 0.0 all-gather.13.cloned.1.call-start
  89.5 0.7 convert_bitcast_fusion
  90.1 0.0 all-gather.13.cloned.1.call-update
  90.2 0.0 all-gather.9.cloned.1.call-start
  90.2 95.3 %all-reduce.2.cloned.1.call-done = bf16[144,4608]{1,0:T(8,128)(2,1)} async-done(((bf16[144,4608]{1,0:T(8,128)(2,1)}), bf16[144,4608]{1,0:T(8,128)(2,1)}) %all-reduce.2.cloned.1.call-update) | async-done | bytes 1327120 | tf_op jit(solution)/shard_map/psum | solution.py:27
  185.5 22.8 %all-gather.7.cloned.1.call-done = bf16[4608,288]{1,0:T(8,128)(2,1)} async-done(((bf16[144,288]{1,0:T(8,128)(2,1)}), bf16[4608,288]{1,0:T(8,128)(2,1)}) %all-gather.7.cloned.1.call-update) | async-done | bytes 2654224 | tf_op jit(solution)/shard_map/all_gather | solution.py:35
  208.4 3.9 fusion.3
  212.3 0.0 all-gather.9.cloned.1.call-update
  212.3 0.0 reduce-scatter.7.cloned.1.call-start
  212.3 0.8 dynamic_slice.11
  213.1 0.8 dynamic_slice.10
  213.9 33.0 %all-gather.13.cloned.1.call-done = bf16[8,576,144]{1,2,0:T(8,128)(2,1)} async-done(((bf16[1,576,144]{1,2,0:T(8,128)(2,1)}), bf16[8,576,144]{1,2,0:T(8,128)(2,1)}) %all-gather.13.cloned.1.call-update) | async-done | bytes 1327120 | tf_op jit(solution)/shard_map/all_gather | solution.py:39
  246.8 1.7 copy.14
  248.5 1.0 reshape.4
  249.6 68.5 %all-gather.9.cloned.1.call-done = bf16[4608,288]{1,0:T(8,128)(2,1)} async-done(((bf16[144,288]{1,0:T(8,128)(2,1)}), bf16[4608,288]{1,0:T(8,128)(2,1)}) %all-gather.9.cloned.1.call-update) | async-done | bytes 2654224 | tf_op jit(solution)/shard_map/all_gather | solution.py:44
  318.1 5.2 convolution_convert_fusion.1
  323.3 2.4 copy.16
  325.7 0.0 reduce-scatter.9.cloned.1.call-start
  325.8 229.6 %reduce-scatter.7.cloned.1.call-done = bf16[288,144]{1,0:T(8,128)(2,1)} async-done(((bf16[4608,144]{1,0:T(8,128)(2,1)}), bf16[288,144]{1,0:T(8,128)(2,1)}) %reduce-scatter.7.cloned.1.call-update) | async-done | bytes 82960
  555.4 2.2 fusion
  557.7 3.0 copy.18
  560.7 0.0 reduce-scatter.9.cloned.1.call-update
  560.7 148.1 %reduce-scatter.9.cloned.1.call-done = bf16[144,288]{1,0:T(8,128)(2,1)} async-done(((bf16[4608,288]{1,0:T(8,128)(2,1)}), bf16[144,288]{1,0:T(8,128)(2,1)}) %reduce-scatter.9.cloned.1.call-update) | async-done | bytes 82960 | tf_op jit(solution)/shard_map/reduce_scatter | solution.py:54
  (8 shorter events, 0.0 us)
Async XLA Ops:
  7.4 81.2 %copy-start = (f32[144,576]{1,0:T(8,128)S(1)}, f32[144,576]{1,0:T(8,128)}, u32[]{:S(2)}) copy-start(f32[144,576]{1,0:T(8,128)} %param.6) | copy-start | bytes 995332
  7.4 70.5 %all-gather.11.cloned.1.call-start = ((), (), s32[]{:S(2)}) async-start(), calls=%async_computation.5 | async-start | bytes 5308416 | tf_op jit(solution)/shard_map/all_gather | solution.py:26
  9.5 79.9 %copy-start.2 = (f32[144,576]{1,0:T(8,128)S(1)}, f32[144,576]{1,0:T(8,128)}, u32[]{:S(2)}) copy-start(f32[144,576]{1,0:T(8,128)} %param.7) | copy-start | bytes 995332
  9.5 176.0 %all-reduce.2.cloned.1.call-start = ((), (), s32[]{:S(2)}) async-start(), calls=%async_computation.3 | async-start | bytes 2654208 | tf_op jit(solution)/shard_map/psum | solution.py:27
  88.5 119.8 %all-gather.7.cloned.1.call-start = ((), (), s32[]{:S(2)}) async-start(), calls=%async_computation.2 | async-start | bytes 3649536 | tf_op jit(solution)/shard_map/all_gather | solution.py:35
  89.4 157.5 %all-gather.13.cloned.1.call-start = ((), (), s32[]{:S(2)}) async-start(), calls=%async_computation.6 | async-start | bytes 1658880 | tf_op jit(solution)/shard_map/all_gather | solution.py:39
  90.2 227.9 %all-gather.9.cloned.1.call-start = ((), (), s32[]{:S(2)}) async-start(), calls=%async_computation.4 | async-start | bytes 3649536 | tf_op jit(solution)/shard_map/all_gather | solution.py:44
  212.3 343.1 %reduce-scatter.7.cloned.1.call-start = ((), (), s32[]{:S(2)}) async-start(), calls=%async_computation.7 | async-start | bytes 2506752
  249.5 73.7 %copy-start.1 = (bf16[4608,144]{0,1:T(8,128)(2,1)}, bf16[4608,144]{0,1:T(8,128)(2,1)S(1)}, u32[]{:S(2)}) copy-start(bf16[4608,144]{0,1:T(8,128)(2,1)S(1)} %reshape.4) | copy-start | bytes 3981316
  325.7 383.0 %reduce-scatter.9.cloned.1.call-start = ((), (), s32[]{:S(2)}) async-start(), calls=%async_computation.8 | async-start | bytes 3649536 | tf_op jit(solution)/shard_map/reduce_scatter | solution.py:54
Sparse Core Ops, SparseCore 0:
  10.3 67.5 all-gather.10
  88.7 96.8 all-reduce.1
  325.8 229.5 reduce-scatter.6
Sparse Core Ops, SparseCore 1:
  91.2 117.1 all-gather.6
  210.3 36.5 all-gather.12
  249.1 68.9 all-gather.8
  560.8 147.9 reduce-scatter.8
where the time goes:
time: 721 us; the launch traced here: 716 us
  waiting for transfers between devices  666 us (92%)
  local copies, waits for them, and re-layouts  23.2 us (3%)
  between operations  14.9 us (2%)
  matrix products  11.3 us (2%)
    unnamed x8, waiting for transfers between devices  230 us
    reduce_scatter x1, waiting for transfers between devices, body(): lax.psum_scatter(contract_first(out_rows, back_in).astype(jnp.bfloat16),...  148 us
    psum x1, waiting for transfers between devices, body(): lax.psum(partial_rows.astype(jnp.float32).astype(jnp.bfloat16), 'rep')  95.3 us
    all_gather x1, waiting for transfers between devices, body(): lax.all_gather(rotated_in, 'grp', axis=0, tiled=True)  68.5 us
    all_gather x1, waiting for transfers between devices, body(): partial_rows = lax.all_gather(local_grad, 'fsdp', axis=1, tiled=True)  68.2 us
    all_gather x1, waiting for transfers between devices, body(): lax.all_gather(basis_out.astype(jnp.bfloat16), 'fsdp', axis=1, tiled=True)  33 us
    all_gather x1, waiting for transfers between devices, body(): lax.all_gather(in_half, 'grp', axis=0, tiled=True)  22.8 us
  transfers between devices with their start and end apart: 7, of which 7 were waited for; matrix products, arithmetic and copies ran while one was open for 1% of the time, Pallas kernels for 0%

commit v1 on v0

v1 whole, which is shorter than its diff:
```python
import jax
import jax.numpy as jnp
from jax import lax
from jax.sharding import Mesh, PartitionSpec as P

DAMPING = 0.1
AXES = ("x", "z1", "z0", "c", "y", "z2")
ROWS = ("x", "z1", "z0", "c")
RING = ("x", "z0")
PART = ("z1", "z2")


def gather(block, axes, count):
    return lax.all_to_all(
        jnp.broadcast_to(block[None], (count,) + block.shape), axes, 0, 0, tiled=True
    )


def scatter_sum(blocks, axes):
    got = lax.all_to_all(blocks, axes, 0, 0, tiled=True)
    return jnp.sum(got.astype(jnp.float32), axis=0)


def pack(rows):
    q = rows.shape[0] // 4
    return jnp.concatenate([rows[i * q : (i + 1) * q] for i in range(4)], axis=1)


def dot(left, right, left_dim, right_dim):
    return lax.dot_general(
        left, right, (((left_dim,), (right_dim,)), ((), ())), preferred_element_type=jnp.float32
    )


def pairs_z1z0_cz2():
    out = []
    for z1 in range(2):
        for z0 in range(2):
            for c in range(2):
                for z2 in range(2):
                    out.append((z1 * 8 + z0 * 4 + c * 2 + z2, z0 * 8 + z1 * 4 + z2 * 2 + c))
    return out


def pairs_z1y0():
    out = []
    for z1 in range(2):
        for y in range(8):
            out.append((z1 * 8 + y, (y % 2) * 8 + (y // 2) * 2 + z1))
    return out


SWAP = [(0, 1), (1, 0)]


def body(grad_parts, basis_in, basis_out, eig_in, eig_out):
    bf16, f32 = jnp.bfloat16, jnp.float32
    x, z1, z0, c, y, z2 = (lax.axis_index(a) for a in AXES)
    rows, cols = basis_in.shape
    half, quarter = rows // 2, cols // 4
    wide = 2 * rows

    bi = basis_in.astype(bf16)
    bi = jnp.where(z2 == 0, bi[:half], bi[half:])
    bi = lax.ppermute(bi, ("z1", "z0", "c", "z2"), pairs_z1z0_cz2())
    bi = gather(bi, RING, 8)
    bi_other = lax.ppermute(bi, "c", SWAP)
    bi = jnp.where(
        c == 0, jnp.concatenate([bi, bi_other], axis=1), jnp.concatenate([bi_other, bi], axis=1)
    ).reshape(8 * rows, cols)

    bo = basis_out.astype(bf16)
    lo = jnp.concatenate([bo[:, i * quarter : i * quarter + half] for i in range(4)], axis=1)
    hi = jnp.concatenate([bo[:, i * quarter + half : (i + 1) * quarter] for i in range(4)], axis=1)
    bo = jnp.where(z2 == 0, lo, hi)
    bo = jnp.concatenate([bo[:half], bo[half:]], axis=1)
    bo = lax.ppermute(bo, ("z1", "y"), pairs_z1y0())
    bo = gather(bo, "y", 8)
    bo = bo.reshape(4, 2, half, 2, wide).transpose(1, 3, 2, 0, 4).reshape(wide, 4 * wide)

    grad = grad_parts[0]
    parts = jnp.stack([grad[:, i * quarter : (i + 1) * quarter] for i in range(4)])
    got = lax.all_to_all(parts, PART, 0, 0, tiled=True).astype(f32)
    got = got.reshape(2, 2, rows, quarter)
    grad = (got[:, 0] + got[:, 1]).astype(bf16).reshape(wide, quarter)
    grad = gather(pack(grad), "y", 8)
    grad = grad.reshape(8, half, 4, quarter).transpose(2, 1, 0, 3).reshape(wide, 8 * quarter)

    part = dot(grad, bi, 1, 0).astype(bf16).reshape(4, half, cols)
    turned = scatter_sum(part, PART).astype(bf16)
    turned = gather(turned, RING, 8)
    other = lax.ppermute(turned, "c", SWAP)
    turned = jnp.where(
        c == 0, jnp.stack([turned, other], axis=1), jnp.stack([other, turned], axis=1)
    ).reshape(16 * half, cols)

    part = dot(bo, turned, 1, 0).astype(bf16).reshape(4, half, cols)
    rotated = scatter_sum(part, PART)
    first = (((x * 2 + z1) * 2 + z0) * 2 + c) * rows + z2 * half
    out_scale = lax.dynamic_slice_in_dim(eig_out, first, half, 0)
    in_scale = lax.dynamic_slice_in_dim(eig_in, y * cols, cols, 0)
    scaled = (rotated / (out_scale[:, None] * in_scale[None, :] + DAMPING)).astype(bf16)
    scaled = gather(scaled, PART, 4).reshape(wide, cols)

    part = dot(scaled, bi, 1, 1).astype(bf16)
    part = part.reshape(4, half, 8, quarter).transpose(2, 1, 0, 3).reshape(8, half, cols)
    back = scatter_sum(part, "y").astype(bf16)
    back = gather(back, PART, 4)
    back = back.reshape(4, half, 4, quarter).transpose(2, 1, 0, 3).reshape(wide, cols)

    part = dot(bo, back, 0, 0).reshape(8, 2, half, cols)
    keep = jnp.where(c == 0, part[:, 0], part[:, 1])
    give = jnp.where(c == 0, part[:, 1], part[:, 0]).astype(bf16)
    part = (keep + lax.ppermute(give, "c", SWAP).astype(f32)).astype(bf16)
    out = scatter_sum(part, RING).astype(bf16)

    keep = jnp.where(z2 == 0, out[:, : cols // 2], out[:, cols // 2 :])
    give = jnp.where(z2 == 0, out[:, cols // 2 :], out[:, : cols // 2])
    other = lax.ppermute(give, "z2", SWAP)
    return jnp.where(
        z2 == 0, jnp.concatenate([keep, other], axis=0), jnp.concatenate([other, keep], axis=0)
    )


def solution(mesh):
    fine = Mesh(mesh.devices.reshape(4, 2, 2, 2, 8, 2), AXES)
    in_specs = (P("z2", ROWS, "y"), P(ROWS, "y"), P(ROWS, "y"), P(), P())
    out_specs = P(ROWS, ("y", "z2"))
    return jax.shard_map(body, mesh=fine, in_specs=in_specs, out_specs=out_specs, check_vma=False)
```

time: 721 us -> 253 us (0.35)
  waiting for transfers between devices: 666 us -> 88 us
  blocking collectives: 0 us -> 71.4 us
  starting transfers between devices: 0.26 us -> 64.8 us
  between operations: 14.9 us -> 0.38 us
  matrix products: 11.3 us -> 4.02 us
    unnamed x8 -> x0, waiting for transfers between devices: 230 us -> none
    all_gather x4 -> x0, waiting for transfers between devices: 193 us -> none  [the longest x1 68.5 us: body(): lax.all_gather(rotated_in, 'grp', axis=0, tiled=True)]
    reduce_scatter x1 -> x0, waiting for transfers between devices: 148 us -> none  [body(): lax.psum_scatter(contract_first(out_rows, back_in).astype(jnp.bfloat16),...]
    psum x1 -> x0, waiting for transfers between devices: 95.3 us -> none  [body(): lax.psum(partial_rows.astype(jnp.float32).astype(jnp.bfloat16), 'rep')]
    all_to_all x0 -> x7, waiting for transfers between devices: none -> 73.1 us  [the longest x5 66.2 us: gather(): lax.all_to_all(jnp.broadcast_to(block[None], (count,) + block.shape), axe...]
    all_to_all x0 -> x4, blocking collectives: none -> 71.4 us  [the longest x3 56.7 us: scatter_sum(): got = lax.all_to_all(blocks, axes, 0, 0, tiled=True)]
    all_to_all x0 -> x7, starting transfers between devices: none -> 39.4 us  [the longest x5 23.2 us: gather(): lax.all_to_all(jnp.broadcast_to(block[None], (count,) + block.shape), axe...]
    ppermute x0 -> x6, starting transfers between devices: none -> 25.4 us  [the longest x1 8.4 us: body(): bi = lax.ppermute(bi, ('z1', 'z0', 'c', 'z2'), pairs_z1z0_cz2())]
  transfers between devices with their start and end apart: 7 -> 13, of which waited for: 7 -> 9; matrix products, arithmetic and copies ran while one was open for 1% -> 3% of each run, Pallas kernels for 0% -> 0%
where the time goes in v1:
time: 253 us; the launch traced here: 251 us
  waiting for transfers between devices  88 us (35%)
  blocking collectives  71.4 us (28%)
  starting transfers between devices  64.8 us (26%)
  local copies, waits for them, and re-layouts  17.5 us (7%)
  other arithmetic  5.18 us (2%)
  matrix products  4.02 us (2%)
    all_to_all x5, waiting for transfers between devices, gather(): lax.all_to_all(jnp.broadcast_to(block[None], (count,) + block.shape), axe...  66.2 us
    all_to_all x3, blocking collectives, scatter_sum(): got = lax.all_to_all(blocks, axes, 0, 0, tiled=True)  56.7 us
    all_to_all x5, starting transfers between devices, gather(): lax.all_to_all(jnp.broadcast_to(block[None], (count,) + block.shape), axe...  23.2 us
    all_to_all x1, blocking collectives, gather(): lax.all_to_all(jnp.broadcast_to(block[None], (count,) + block.shape), axe...  14.7 us
    all_to_all x1, starting transfers between devices, body(): got = lax.all_to_all(parts, PART, 0, 0, tiled=True).astype(f32)  10.8 us
    ppermute x1, starting transfers between devices, body(): bi = lax.ppermute(bi, ('z1', 'z0', 'c', 'z2'), pairs_z1z0_cz2())  8.4 us
    all_to_all x1, waiting for transfers between devices, scatter_sum(): got = lax.all_to_all(blocks, axes, 0, 0, tiled=True)  6.84 us
    ppermute x1, waiting for transfers between devices, body(): other = lax.ppermute(give, 'z2', SWAP)  6.73 us
  transfers between devices with their start and end apart: 13, of which 9 were waited for; matrix products, arithmetic and copies ran while one was open for 3% of the time, Pallas kernels for 0%

profile of v1, /device:TPU:1, one launch (start us, length us, event | category | flops | bytes accessed | tf_op | source)
XLA Modules:
  0.0 251.3 jit_solution(10173887016067197297)
XLA Ops:
  0.0 1.2 slice_bitcast_fusion.3
  2.0 10.8 %all-to-all-start.1 = ((bf16[4,144,144]{2,1,0:T(8,128)(2,1)}), bf16[4,144,144]{2,1,0:T(8,128)(2,1)S(1)}, u32[]{:S(2)}, u32[]{:S(2)}) async-start(bf16[4,144,144]{2,1,0:T(8,128)(2,1)} %pad_maximum_fusion), calls=%async_computation.1 | async-start | bytes 589824 | tf_op jit(solution)/shard_map/all_to_all | solution.py:83
  12.9 8.4 %collective-permute-start.1 = (bf16[72,576]{1,0:T(8,128)(2,1)S(1)}, bf16[72,576]{1,0:T(8,128)(2,1)S(1)}, u32[]{:S(2)}, u32[]{:S(2)}) collective-permute-start(bf16[72,576]{1,0:T(8,128)(2,1)S(1)} %slice_select_fusion), channel_id=1, source_target_pairs={{0,0},{1,16},{16,1},{17,17},{32,64},{33,80},{48,65},{49,81},{64,32... | collective-permute-start | bytes 248840 | tf_op jit(solution)/shard_map/ppermute | solution.py:65
  21.3 6.4 %collective-permute-done.1 = bf16[72,576]{1,0:T(8,128)(2,1)S(1)} collective-permute-done((bf16[72,576]{1,0:T(8,128)(2,1)S(1)}, bf16[72,576]{1,0:T(8,128)(2,1)S(1)}, u32[]{:S(2)}, u32[]{:S(2)}) %collective-permute-start.1) | collective-permute-done | bytes 82976 | tf_op jit(solution)/shard_map/ppermute | solution.py:65
  27.7 0.9 broadcast_in_dim.14
  28.6 4.0 %all-to-all-start.3 = ((bf16[8,72,576]{2,1,0:T(8,128)(2,1)}), bf16[8,72,576]{2,1,0:T(8,128)(2,1)S(1)}, u32[]{:S(2)}, u32[]{:S(2)}) async-start(bf16[8,72,576]{2,1,0:T(8,128)(2,1)} %broadcast_in_dim.14), calls=%async_computation.3 | async-start | bytes 1474560 | tf_op jit(solution)/shard_map/all_to_all | solution.py:14
  32.9 12.2 %all-to-all-done.3 = bf16[8,72,576]{2,1,0:T(8,128)(2,1)S(1)} async-done(((bf16[8,72,576]{2,1,0:T(8,128)(2,1)}), bf16[8,72,576]{2,1,0:T(8,128)(2,1)S(1)}, u32[]{:S(2)}, u32[]{:S(2)}) %all-to-all-start.3) | async-done | bytes 663584 | tf_op jit(solution)/shard_map/all_to_all | solution.py:14
  46.0 6.8 %all-to-all-start.2 = ((bf16[8,72,576]{2,1,0:T(8,128)(2,1)}), bf16[8,72,576]{2,1,0:T(8,128)(2,1)S(1)}, u32[]{:S(2)}, u32[]{:S(2)}) async-start(bf16[8,72,576]{2,1,0:T(8,128)(2,1)} %broadcast_in_dim.13), calls=%async_computation.2 | async-start | bytes 1474560 | tf_op jit(solution)/shard_map/all_to_all | solution.py:14
  52.8 3.1 %collective-permute-start.2 = (bf16[8,72,576]{2,1,0:T(8,128)(2,1)S(1)}, bf16[8,72,576]{2,1,0:T(8,128)(2,1)}, u32[]{:S(2)}, u32[]{:S(2)}) collective-permute-start(bf16[8,72,576]{2,1,0:T(8,128)(2,1)S(1)} %all-to-all-done.3), channel_id=1, source_target_pairs={{0,16},{16,0},{1,17},{17,1},{2,18},{18,2},{3,19},{19,3},{4,20},{20... | collective-permute-start | bytes 1990664 | tf_op jit(solution)/shard_map/ppermute | solution.py:67
  56.0 19.4 %all-to-all-done.2 = bf16[8,72,576]{2,1,0:T(8,128)(2,1)S(1)} async-done(((bf16[8,72,576]{2,1,0:T(8,128)(2,1)}), bf16[8,72,576]{2,1,0:T(8,128)(2,1)S(1)}, u32[]{:S(2)}, u32[]{:S(2)}) %all-to-all-start.2) | async-done | bytes 663584 | tf_op jit(solution)/shard_map/all_to_all | solution.py:14
  76.8 1.2 reshape.123
  78.0 1.9 maximum_select_fusion
  81.0 14.4 %all_to_all.55 = bf16[4,72,576]{2,1,0:T(8,128)(2,1)S(1)} all-to-all(bf16[4,72,576]{2,1,0:T(8,128)(2,1)S(1)} %bitcast.78), channel_id=1, replica_groups=mesh['x'=4,'z1'=2,'z0'=2,'c'=2,'y'=8,'z2'=2] {'z1','z2'}, dimensions={0} | all-to-all | bytes 663552 | tf_op jit(solution)/shard_map/all_to_all | solution.py:20
  96.5 4.0 %all-to-all-start.5 = ((bf16[8,72,576]{2,1,0:T(8,128)(2,1)}), bf16[8,72,576]{2,1,0:T(8,128)(2,1)S(1)}, u32[]{:S(2)}, u32[]{:S(2)}) async-start(bf16[8,72,576]{2,1,0:T(8,128)(2,1)} %broadcast_in_dim.15), calls=%async_computation.5 | async-start | bytes 1474560 | tf_op jit(solution)/shard_map/all_to_all | solution.py:14
  101.7 9.8 %all-to-all-done.5 = bf16[8,72,576]{2,1,0:T(8,128)(2,1)S(1)} async-done(((bf16[8,72,576]{2,1,0:T(8,128)(2,1)}), bf16[8,72,576]{2,1,0:T(8,128)(2,1)S(1)}, u32[]{:S(2)}, u32[]{:S(2)}) %all-to-all-start.5) | async-done | bytes 663584 | tf_op jit(solution)/shard_map/all_to_all | solution.py:14
  112.3 3.5 %all-to-all-start = ((bf16[8,72,576]{2,1,0:T(8,128)(2,1)}), bf16[8,72,576]{2,1,0:T(8,128)(2,1)S(1)}, u32[]{:S(2)}, u32[]{:S(2)}) async-start(bf16[8,72,576]{2,1,0:T(8,128)(2,1)} %broadcast_in_dim.12), calls=%async_computation | async-start | bytes 1474560 | tf_op jit(solution)/shard_map/all_to_all | solution.py:14
  115.9 4.3 %collective-permute-start.3 = (bf16[8,72,576]{2,1,0:T(8,128)(2,1)S(1)}, bf16[8,72,576]{2,1,0:T(8,128)(2,1)S(1)}, u32[]{:S(2)}, u32[]{:S(2)}) collective-permute-start(bf16[8,72,576]{2,1,0:T(8,128)(2,1)S(1)} %all-to-all-done.5), channel_id=1, source_target_pairs={{0,16},{16,0},{1,17},{17,1},{2,18},{18,2},{3,19},{19,3},{4,20},{20... | collective-permute-start | bytes 1990664 | tf_op jit(solution)/shard_map/ppermute | solution.py:92
  120.2 15.8 %all-to-all-done = bf16[8,72,576]{2,1,0:T(8,128)(2,1)S(1)} async-done(((bf16[8,72,576]{2,1,0:T(8,128)(2,1)}), bf16[8,72,576]{2,1,0:T(8,128)(2,1)S(1)}, u32[]{:S(2)}, u32[]{:S(2)}) %all-to-all-start) | async-done | bytes 663584 | tf_op jit(solution)/shard_map/all_to_all | solution.py:14
  138.8 1.5 convolution_convert_fusion.1
  140.2 5.3 %all-to-all-start.6 = ((bf16[4,72,576]{2,1,0:T(8,128)(2,1)}), bf16[4,72,576]{2,1,0:T(8,128)(2,1)S(1)}, u32[]{:S(2)}, u32[]{:S(2)}) async-start(bf16[4,72,576]{2,1,0:T(8,128)(2,1)} %bitcast.17), calls=%async_computation.6 | async-start | bytes 737280 | tf_op jit(solution)/shard_map/all_to_all | solution.py:20
  147.1 6.8 %all-to-all-done.6 = bf16[4,72,576]{2,1,0:T(8,128)(2,1)S(1)} async-done(((bf16[4,72,576]{2,1,0:T(8,128)(2,1)}), bf16[4,72,576]{2,1,0:T(8,128)(2,1)S(1)}, u32[]{:S(2)}, u32[]{:S(2)}) %all-to-all-start.6) | async-done | bytes 331808 | tf_op jit(solution)/shard_map/all_to_all | solution.py:20
  154.2 14.7 %all_to_all.56 = bf16[4,72,576]{2,1,0:T(8,128)(2,1)S(1)} all-to-all(bf16[4,72,576]{2,1,0:T(8,128)(2,1)S(1)} %broadcast_in_dim.16), channel_id=1, replica_groups=mesh['x'=4,'z1'=2,'z0'=2,'c'=2,'y'=8,'z2'=2] {'z1','z2'}, dimensions={0} | all-to-all | bytes 663552 | tf_op jit(solution)/shard_map/all_to_all | solution.py:14
  169.6 1.5 reshape.127
  172.8 20.2 %all_to_all.57 = bf16[8,72,576]{2,1,0:T(8,128)(2,1)S(1)} all-to-all(bf16[8,72,576]{2,1,0:T(8,128)(2,1)S(1)} %reshape.128), channel_id=1, replica_groups=mesh['x'=4,'z1'=2,'z0'=2,'c'=2,'y'=8,'z2'=2] {'y'}, dimensions={0} | all-to-all | bytes 1327104 | tf_op jit(solution)/shard_map/all_to_all | solution.py:20
  193.8 4.8 %all-to-all-start.9 = ((bf16[4,72,576]{2,1,0:T(8,128)(2,1)}), bf16[4,72,576]{2,1,0:T(8,128)(2,1)S(1)}, u32[]{:S(2)}, u32[]{:S(2)}) async-start(bf16[4,72,576]{2,1,0:T(8,128)(2,1)} %broadcast_in_dim.17), calls=%async_computation.9 | async-start | bytes 737280 | tf_op jit(solution)/shard_map/all_to_all | solution.py:14
  199.1 9.1 %all-to-all-done.9 = bf16[4,72,576]{2,1,0:T(8,128)(2,1)S(1)} async-done(((bf16[4,72,576]{2,1,0:T(8,128)(2,1)}), bf16[4,72,576]{2,1,0:T(8,128)(2,1)S(1)}, u32[]{:S(2)}, u32[]{:S(2)}) %all-to-all-start.9) | async-done | bytes 331808 | tf_op jit(solution)/shard_map/all_to_all | solution.py:14
  209.4 1.1 fusion.4
  210.6 6.7 %collective-permute-start.4 = (bf16[8,72,576]{2,1,0:T(8,128)(2,1)S(1)}, bf16[8,72,576]{2,1,0:T(8,128)(2,1)S(1)}, u32[]{:S(2)}, u32[]{:S(2)}) collective-permute-start(bf16[8,72,576]{2,1,0:T(8,128)(2,1)S(1)} %fusion.3), channel_id=1, source_target_pairs={{0,16},{16,0},{1,17},{17,1},{2,18},{18,2},{3,19},{19,3},{4,20},{20... | collective-permute-start | bytes 1990664 | tf_op jit(solution)/shard_map/ppermute | solution.py:114
  217.4 1.8 collective-permute-done.4
  219.4 22.1 %all_to_all.58 = bf16[8,72,576]{2,1,0:T(8,128)(2,1)S(1)} all-to-all(bf16[8,72,576]{2,1,0:T(8,128)(2,1)S(1)} %fusion.2), channel_id=1, replica_groups=mesh['x'=4,'z1'=2,'z0'=2,'c'=2,'y'=8,'z2'=2] {'x','z0'}, dimensions={0} | all-to-all | bytes 1327104 | tf_op jit(solution)/shard_map/all_to_all | solution.py:20
  241.7 2.1 collective-permute-start.5
  243.9 6.7 %collective-permute-done.5 = bf16[72,288]{1,0:T(8,128)(2,1)S(1)} collective-permute-done((bf16[72,288]{1,0:T(8,128)(2,1)S(1)}, bf16[72,288]{1,0:T(8,128)(2,1)S(1)}, u32[]{:S(2)}, u32[]{:S(2)}) %collective-permute-start.5) | collective-permute-done | bytes 41504 | tf_op jit(solution)/shard_map/ppermute | solution.py:119
  (59 shorter events, 18.1 us)
Async XLA Ops:
  0.0 12.8 %copy-start.4 = (f32[144,576]{1,0:T(8,128)S(1)}, f32[144,576]{1,0:T(8,128)}, u32[]{:S(2)}) copy-start(f32[144,576]{1,0:T(8,128)} %param.6) | copy-start | bytes 995332
  2.0 25.7 %all-to-all-start.1 = ((bf16[4,144,144]{2,1,0:T(8,128)(2,1)}), bf16[4,144,144]{2,1,0:T(8,128)(2,1)S(1)}, u32[]{:S(2)}, u32[]{:S(2)}) async-start(bf16[4,144,144]{2,1,0:T(8,128)(2,1)} %pad_maximum_fusion), calls=%async_computation.1 | async-start | bytes 589824 | tf_op jit(solution)/shard_map/all_to_all | solution.py:83
  12.9 14.8 %collective-permute-start.1 = (bf16[72,576]{1,0:T(8,128)(2,1)S(1)}, bf16[72,576]{1,0:T(8,128)(2,1)S(1)}, u32[]{:S(2)}, u32[]{:S(2)}) collective-permute-start(bf16[72,576]{1,0:T(8,128)(2,1)S(1)} %slice_select_fusion), channel_id=1, source_target_pairs={{0,0},{1,16},{16,1},{17,17},{32,64},{33,80},{48,65},{49,81},{64,32... | collective-permute-start | bytes 248840 | tf_op jit(solution)/shard_map/ppermute | solution.py:65
  28.6 16.4 %all-to-all-start.3 = ((bf16[8,72,576]{2,1,0:T(8,128)(2,1)}), bf16[8,72,576]{2,1,0:T(8,128)(2,1)S(1)}, u32[]{:S(2)}, u32[]{:S(2)}) async-start(bf16[8,72,576]{2,1,0:T(8,128)(2,1)} %broadcast_in_dim.14), calls=%async_computation.3 | async-start | bytes 1474560 | tf_op jit(solution)/shard_map/all_to_all | solution.py:14
  46.0 29.3 %all-to-all-start.2 = ((bf16[8,72,576]{2,1,0:T(8,128)(2,1)}), bf16[8,72,576]{2,1,0:T(8,128)(2,1)S(1)}, u32[]{:S(2)}, u32[]{:S(2)}) async-start(bf16[8,72,576]{2,1,0:T(8,128)(2,1)} %broadcast_in_dim.13), calls=%async_computation.2 | async-start | bytes 1474560 | tf_op jit(solution)/shard_map/all_to_all | solution.py:14
  52.8 25.2 %collective-permute-start.2 = (bf16[8,72,576]{2,1,0:T(8,128)(2,1)S(1)}, bf16[8,72,576]{2,1,0:T(8,128)(2,1)}, u32[]{:S(2)}, u32[]{:S(2)}) collective-permute-start(bf16[8,72,576]{2,1,0:T(8,128)(2,1)S(1)} %all-to-all-done.3), channel_id=1, source_target_pairs={{0,16},{16,0},{1,17},{17,1},{2,18},{18,2},{3,19},{19,3},{4,20},{20... | collective-permute-start | bytes 1990664 | tf_op jit(solution)/shard_map/ppermute | solution.py:67
  79.9 1.1 copy-start.2
  95.5 5.0 %copy-start.5 = (f32[144,576]{1,0:T(8,128)S(1)}, f32[144,576]{1,0:T(8,128)}, u32[]{:S(2)}) copy-start(f32[144,576]{1,0:T(8,128)} %param.7) | copy-start | bytes 995332
  96.5 14.9 %all-to-all-start.5 = ((bf16[8,72,576]{2,1,0:T(8,128)(2,1)}), bf16[8,72,576]{2,1,0:T(8,128)(2,1)S(1)}, u32[]{:S(2)}, u32[]{:S(2)}) async-start(bf16[8,72,576]{2,1,0:T(8,128)(2,1)} %broadcast_in_dim.15), calls=%async_computation.5 | async-start | bytes 1474560 | tf_op jit(solution)/shard_map/all_to_all | solution.py:14
  101.0 0.7 collective-permute-start
  112.3 23.7 %all-to-all-start = ((bf16[8,72,576]{2,1,0:T(8,128)(2,1)}), bf16[8,72,576]{2,1,0:T(8,128)(2,1)S(1)}, u32[]{:S(2)}, u32[]{:S(2)}) async-start(bf16[8,72,576]{2,1,0:T(8,128)(2,1)} %broadcast_in_dim.12), calls=%async_computation | async-start | bytes 1474560 | tf_op jit(solution)/shard_map/all_to_all | solution.py:14
  115.9 22.0 %collective-permute-start.3 = (bf16[8,72,576]{2,1,0:T(8,128)(2,1)S(1)}, bf16[8,72,576]{2,1,0:T(8,128)(2,1)S(1)}, u32[]{:S(2)}, u32[]{:S(2)}) collective-permute-start(bf16[8,72,576]{2,1,0:T(8,128)(2,1)S(1)} %all-to-all-done.5), channel_id=1, source_target_pairs={{0,16},{16,0},{1,17},{17,1},{2,18},{18,2},{3,19},{19,3},{4,20},{20... | collective-permute-start | bytes 1990664 | tf_op jit(solution)/shard_map/ppermute | solution.py:92
  137.9 0.9 copy-start
  140.2 28.6 %copy-start.3 = (bf16[8,144,576]{2,1,0:T(8,128)(2,1)S(1)}, bf16[8,144,576]{2,1,0:T(8,128)(2,1)}, u32[]{:S(2)}) copy-start(bf16[8,144,576]{2,1,0:T(8,128)(2,1)} %copy-done.2) | copy-start | bytes 3981316
  140.2 13.7 %all-to-all-start.6 = ((bf16[4,72,576]{2,1,0:T(8,128)(2,1)}), bf16[4,72,576]{2,1,0:T(8,128)(2,1)S(1)}, u32[]{:S(2)}, u32[]{:S(2)}) async-start(bf16[4,72,576]{2,1,0:T(8,128)(2,1)} %bitcast.17), calls=%async_computation.6 | async-start | bytes 737280 | tf_op jit(solution)/shard_map/all_to_all | solution.py:20
  172.8 25.9 %copy-start.1 = (bf16[288,1152]{1,0:T(8,128)(2,1)S(1)}, bf16[288,1152]{1,0:T(8,128)(2,1)}, u32[]{:S(2)}) copy-start(bf16[288,1152]{1,0:T(8,128)(2,1)} %copy-done) | copy-start | bytes 1990660
  193.8 14.3 %all-to-all-start.9 = ((bf16[4,72,576]{2,1,0:T(8,128)(2,1)}), bf16[4,72,576]{2,1,0:T(8,128)(2,1)S(1)}, u32[]{:S(2)}, u32[]{:S(2)}) async-start(bf16[4,72,576]{2,1,0:T(8,128)(2,1)} %broadcast_in_dim.17), calls=%async_computation.9 | async-start | bytes 737280 | tf_op jit(solution)/shard_map/all_to_all | solution.py:14
  210.6 8.5 %collective-permute-start.4 = (bf16[8,72,576]{2,1,0:T(8,128)(2,1)S(1)}, bf16[8,72,576]{2,1,0:T(8,128)(2,1)S(1)}, u32[]{:S(2)}, u32[]{:S(2)}) collective-permute-start(bf16[8,72,576]{2,1,0:T(8,128)(2,1)S(1)} %fusion.3), channel_id=1, source_target_pairs={{0,16},{16,0},{1,17},{17,1},{2,18},{18,2},{3,19},{19,3},{4,20},{20... | collective-permute-start | bytes 1990664 | tf_op jit(solution)/shard_map/ppermute | solution.py:114
  241.7 8.9 %collective-permute-start.5 = (bf16[72,288]{1,0:T(8,128)(2,1)S(1)}, bf16[72,288]{1,0:T(8,128)(2,1)S(1)}, u32[]{:S(2)}, u32[]{:S(2)}) collective-permute-start(bf16[72,288]{1,0:T(8,128)(2,1)S(1)} %get-tuple-element.24), channel_id=1, source_target_pairs={{0,1},{1,0},{2,3},{3,2},{4,5},{5,4},{6,7},{7,6},{8,9},{9,8},{10,11... | collective-permute-start | bytes 124424 | tf_op jit(solution)/shard_map/ppermute | solution.py:119

commit v2 on v1

v2 whole, which is shorter than its diff:
```python
import jax
import jax.numpy as jnp
from jax import lax
from jax.sharding import Mesh, PartitionSpec as P

DAMPING = 0.1
AXES = ("x", "z1", "z0", "c", "y", "z2")
ROWS = ("x", "z1", "z0", "c")
RING = ("x", "z0")
PART = ("z1", "z2")
SWAP = [(0, 1), (1, 0)]


def gather(block, axes, count):
    return lax.all_to_all(
        jnp.broadcast_to(block[None], (count,) + block.shape), axes, 0, 0, tiled=True
    )


def scatter_sum(blocks, axes):
    got = lax.all_to_all(blocks, axes, 0, 0, tiled=True)
    return jnp.sum(got.astype(jnp.float32), axis=0)


def dot(left, right, left_dim, right_dim):
    return lax.dot_general(
        left, right, (((left_dim,), (right_dim,)), ((), ())), preferred_element_type=jnp.float32
    )


def in_order(first, mine, other, axis):
    return jnp.where(
        first,
        jnp.concatenate([mine, other], axis=axis),
        jnp.concatenate([other, mine], axis=axis),
    )


def pairs_z1y0():
    return [(z1 * 8 + y, (y % 2) * 8 + (y // 2) * 2 + z1) for z1 in range(2) for y in range(8)]


def body(grad_parts, basis_in, basis_out, eig_in, eig_out):
    bf16, f32 = jnp.bfloat16, jnp.float32
    x, z1, z0, c, y, z2 = (lax.axis_index(a) for a in AXES)
    rows, cols = basis_in.shape
    half, quarter = rows // 2, cols // 4
    wide = 2 * rows
    low_core, low_rep = c == 0, z2 == 0

    bi = lax.all_gather(basis_in.astype(bf16), ("x", "z1", "z0"), axis=0, tiled=True)

    bo = lax.ppermute(basis_out.astype(bf16), ("z1", "y"), pairs_z1y0())
    bo = lax.all_gather(bo, ("c", "y"), axis=0, tiled=True).reshape(2, 4, 2, rows, cols)

    grad = grad_parts[0]
    keep = jnp.where(low_rep, grad[:half], grad[half:])
    give = jnp.where(low_rep, grad[half:], grad[:half])
    got = lax.ppermute(give, "z2", SWAP)
    grad = (keep.astype(f32) + got.astype(f32)).astype(bf16)
    even = jnp.concatenate([grad[:, :quarter], grad[:, 2 * quarter : 3 * quarter]], axis=1)
    odd = jnp.concatenate([grad[:, quarter : 2 * quarter], grad[:, 3 * quarter :]], axis=1)
    keep, give = jnp.where(low_core, even, odd), jnp.where(low_core, odd, even)
    grad = in_order(low_core, keep, lax.ppermute(give, "c", SWAP), 1)
    grad = gather(grad, "y", 8)
    grad = grad.reshape(8, half, 2, wide).transpose(2, 1, 0, 3).reshape(rows, 8 * wide)

    part = dot(grad, bi, 1, 0)
    keep = jnp.where(low_core, part[:half], part[half:])
    give = jnp.where(low_core, part[half:], part[:half]).astype(bf16)
    turned = (keep + lax.ppermute(give, "c", SWAP).astype(f32)).astype(bf16)
    turned = gather(turned, RING, 8)
    other = lax.ppermute(turned, "c", SWAP)
    turned = in_order(low_core, turned[:, None], other[:, None], 1).reshape(16 * half, cols)

    mine = lax.dynamic_index_in_dim(bo, c, 0, keepdims=False).reshape(4, wide, 4, 2, half)
    mine = lax.dynamic_index_in_dim(mine, z2, 3, keepdims=False)
    mine = mine.transpose(1, 0, 2, 3).reshape(wide, 4 * wide)
    part = dot(mine, turned, 1, 0).astype(bf16).reshape(4, half, cols)
    rotated = scatter_sum(part, PART)
    first = (((x * 2 + z1) * 2 + z0) * 2 + c) * rows + z2 * half
    out_scale = lax.dynamic_slice_in_dim(eig_out, first, half, 0)
    in_scale = lax.dynamic_slice_in_dim(eig_in, y * cols, cols, 0)
    scaled = (rotated / (out_scale[:, None] * in_scale[None, :] + DAMPING)).astype(bf16)
    scaled = in_order(low_core, scaled, lax.ppermute(scaled, "c", SWAP), 0)

    part = dot(scaled, bi, 1, 1).astype(bf16)
    part = part.reshape(2, half, 8, wide).transpose(2, 1, 0, 3).reshape(8, half, cols)
    back = scatter_sum(part, "y").astype(bf16)
    low = jnp.concatenate([back[:, :quarter], back[:, 2 * quarter : 3 * quarter]], axis=1)
    high = jnp.concatenate([back[:, quarter : 2 * quarter], back[:, 3 * quarter :]], axis=1)
    back = lax.all_to_all(jnp.stack([low, high, low, high]), PART, 0, 0, tiled=True)
    back = back.reshape(4 * half, 2, quarter).transpose(1, 0, 2).reshape(8 * half, quarter)

    left = bo.transpose(0, 2, 3, 1, 4).reshape(8 * half, 4 * cols)
    part = dot(left, back, 0, 0).astype(bf16).reshape(8, 4, half, quarter)
    part = part.transpose(0, 2, 1, 3).reshape(8, half, cols)
    out = scatter_sum(part, RING).astype(bf16)
    keep = jnp.where(low_core, out[:, :wide], out[:, wide:])
    give = jnp.where(low_core, out[:, wide:], out[:, :wide])
    got = lax.ppermute(give, "c", SWAP)
    mine = jnp.concatenate([keep[:, :quarter], keep[:, quarter:]], axis=0)
    got = jnp.concatenate([got[:, :quarter], got[:, quarter:]], axis=0)
    return in_order(low_core, mine, got, 1)


def solution(mesh):
    fine = Mesh(mesh.devices.reshape(4, 2, 2, 2, 8, 2), AXES)
    in_specs = (P("z2", ROWS, "y"), P(ROWS, "y"), P(ROWS, "y"), P(), P())
    out_specs = P(ROWS, ("y", "z2"))
    return jax.shard_map(body, mesh=fine, in_specs=in_specs, out_specs=out_specs, check_vma=False)
```

time: 253 us -> 285 us (1.13)
  local copies, waits for them, and re-layouts: 17.5 us -> 43.7 us
  waiting for transfers between devices: 88 us -> 69.4 us
  blocking collectives: 71.4 us -> 88.1 us
  between operations: 0.38 us -> 13.7 us
  starting transfers between devices: 64.8 us -> 52.2 us
  matrix products: 4.02 us -> 8.28 us
  other arithmetic: 5.18 us -> 8.73 us
    all_to_all x6 -> x1, waiting for transfers between devices: 66.2 us -> 1.08 us  [body(): lax.all_to_all(jnp.stack([low, high, low, high]), PART, 0, 0, tiled=True)]
    all_gather x0 -> x2, waiting for transfers between devices: none -> 46.7 us  [the longest x1 27.7 us: body(): lax.all_gather(basis_in.astype(bf16), ('x', 'z1', 'z0'), axis=0, tiled=True)]
    all_to_all x1 -> x2, blocking collectives: 14.7 us -> 47.9 us  [gather(): lax.all_to_all(jnp.broadcast_to(block[None], (count,) + block.shape), axe...]
    all_to_all x6 -> x1, starting transfers between devices: 34.1 us -> 3.48 us  [body(): lax.all_to_all(jnp.stack([low, high, low, high]), PART, 0, 0, tiled=True)]
    reshape x9 -> x13, local copies, waits for them, and re-layouts: 7.32 us -> 27.7 us  [the longest x1 10.4 us: body(): lax.dynamic_index_in_dim(bo, c, 0, keepdims=False)]
    ppermute x5 -> x6, starting transfers between devices: 21 us -> 38.2 us  [the longest x1 11.5 us: body(): got = lax.ppermute(give, 'z2', SWAP)]
    all_to_all x3 -> x2, blocking collectives: 56.7 us -> 40.3 us  [scatter_sum(): got = lax.all_to_all(blocks, axes, 0, 0, tiled=True)]
    dynamic_slice x0 -> x3, local copies, waits for them, and re-layouts: none -> 12.4 us  [the longest x2 9.77 us: body(): mine = lax.dynamic_index_in_dim(mine, z2, 3, keepdims=False)]
  transfers between devices with their start and end apart: 13 -> 11, of which waited for: 9 -> 9; matrix products, arithmetic and copies ran while one was open for 3% -> 14% of each run, Pallas kernels for 0% -> 0%
where the time goes in v2:
time: 285 us; the launch traced here: 284 us
  blocking collectives  88.1 us (31%)
  waiting for transfers between devices  69.4 us (24%)
  starting transfers between devices  52.2 us (18%)
  local copies, waits for them, and re-layouts  43.7 us (15%)
  between operations  13.7 us (5%)
  other arithmetic  8.73 us (3%)
  matrix products  8.28 us (3%)
    all_to_all x2, blocking collectives, gather(): lax.all_to_all(jnp.broadcast_to(block[None], (count,) + block.shape), axe...  47.9 us
    all_to_all x2, blocking collectives, scatter_sum(): got = lax.all_to_all(blocks, axes, 0, 0, tiled=True)  40.3 us
    all_gather x1, waiting for transfers between devices, body(): lax.all_gather(basis_in.astype(bf16), ('x', 'z1', 'z0'), axis=0, tiled=True)  27.7 us
    all_gather x1, waiting for transfers between devices, body(): lax.all_gather(bo, ('c', 'y'), axis=0, tiled=True)  19.1 us
    ppermute x1, starting transfers between devices, body(): got = lax.ppermute(give, 'z2', SWAP)  11.5 us
    ppermute x1, starting transfers between devices, body(): turned = (keep + lax.ppermute(give, 'c', SWAP).astype(f32)).astype(bf16)  11.1 us
    reshape x1, local copies, waits for them, and re-layouts, body(): lax.dynamic_index_in_dim(bo, c, 0, keepdims=False)  10.4 us
    ppermute x1, waiting for transfers between devices, body(): got = lax.ppermute(give, 'z2', SWAP)  9.98 us
  transfers between devices with their start and end apart: 11, of which 9 were waited for; matrix products, arithmetic and copies ran while one was open for 14% of the time, Pallas kernels for 0%

profile of v2, /device:TPU:1, one launch (start us, length us, event | category | flops | bytes accessed | tf_op | source)
XLA Modules:
  0.0 284.2 jit_solution(10451100637544899038)
XLA Ops:
  6.5 1.7 convert_element_type.54
  11.7 11.5 %collective-permute-start.1 = (bf16[72,576]{1,0:T(8,128)(2,1)S(1)}, bf16[72,576]{1,0:T(8,128)(2,1)S(1)}, u32[]{:S(2)}, u32[]{:S(2)}) collective-permute-start(bf16[72,576]{1,0:T(8,128)(2,1)S(1)} %select_bitcast_fusion), channel_id=1, source_target_pairs={{0,1},{1,0},{2,3},{3,2},{4,5},{5,4},{6,7},{7,6},{8,9},{9,8},{10,11... | collective-permute-start | bytes 248840 | tf_op jit(solution)/shard_map/ppermute | solution.py:59
  23.1 10.0 %collective-permute-done.1 = bf16[72,576]{1,0:T(8,128)(2,1)S(1)} collective-permute-done((bf16[72,576]{1,0:T(8,128)(2,1)S(1)}, bf16[72,576]{1,0:T(8,128)(2,1)S(1)}, u32[]{:S(2)}, u32[]{:S(2)}) %collective-permute-start.1) | collective-permute-done | bytes 82976 | tf_op jit(solution)/shard_map/ppermute | solution.py:59
  34.3 3.4 %collective-permute-start.2 = (bf16[72,288]{1,0:T(8,128)(2,1)S(1)}, bf16[72,288]{1,0:T(8,128)(2,1)S(1)}, u32[]{:S(2)}, u32[]{:S(2)}) collective-permute-start(bf16[72,288]{1,0:T(8,128)(2,1)S(1)} %get-tuple-element.6), channel_id=1, source_target_pairs={{0,16},{16,0},{1,17},{17,1},{2,18},{18,2},{3,19},{19,3},{4,20},{20... | collective-permute-start | bytes 124424 | tf_op jit(solution)/shard_map/ppermute | solution.py:64
  38.8 33.6 %all_to_all.30 = bf16[8,72,576]{2,1,0:T(8,128)(2,1)S(1)} all-to-all(bf16[8,72,576]{2,1,0:T(8,128)(2,1)S(1)} %broadcast_in_dim.8), channel_id=1, replica_groups=mesh['x'=4,'z1'=2,'z0'=2,'c'=2,'y'=8,'z2'=2] {'y'}, dimensions={0} | all-to-all | bytes 1327104 | tf_op jit(solution)/shard_map/all_to_all | solution.py:15
  74.1 27.7 %all-gather.5.cloned.1.call-done = bf16[2304,576]{1,0:T(8,128)(2,1)} async-done(((bf16[144,576]{1,0:T(8,128)(2,1)}), bf16[2304,576]{1,0:T(8,128)(2,1)}) %all-gather.5.cloned.1.call-update) | async-done | bytes 2654224 | tf_op jit(solution)/shard_map/all_gather | solution.py:51
  101.8 2.5 fusion.13
  104.3 11.1 %collective-permute-start.3 = (bf16[72,576]{1,0:T(8,128)(2,1)S(1)}, bf16[72,576]{1,0:T(8,128)(2,1)S(1)}, u32[]{:S(2)}, u32[]{:S(2)}) collective-permute-start(bf16[72,576]{1,0:T(8,128)(2,1)S(1)} %select_convert_fusion), channel_id=1, source_target_pairs={{0,16},{16,0},{1,17},{17,1},{2,18},{18,2},{3,19},{19,3},{4,20},{20... | collective-permute-start | bytes 248840 | tf_op jit(solution)/shard_map/ppermute | solution.py:71
  116.4 14.2 %all_to_all.31 = bf16[8,72,576]{2,1,0:T(8,128)(2,1)S(1)} all-to-all(bf16[8,72,576]{2,1,0:T(8,128)(2,1)S(1)} %broadcast_in_dim.9), channel_id=1, replica_groups=mesh['x'=4,'z1'=2,'z0'=2,'c'=2,'y'=8,'z2'=2] {'x','z0'}, dimensions={0} | all-to-all | bytes 1327104 | tf_op jit(solution)/shard_map/all_to_all | solution.py:15
  130.7 3.4 %collective-permute-start.4 = (bf16[8,72,576]{2,1,0:T(8,128)(2,1)S(1)}, bf16[8,72,576]{2,1,0:T(8,128)(2,1)}, u32[]{:S(2)}, u32[]{:S(2)}) collective-permute-start(bf16[8,72,576]{2,1,0:T(8,128)(2,1)S(1)} %all_to_all.31), channel_id=1, source_target_pairs={{0,16},{16,0},{1,17},{17,1},{2,18},{18,2},{3,19},{19,3},{4,20},{20... | collective-permute-start | bytes 1990664 | tf_op jit(solution)/shard_map/ppermute | solution.py:73
  134.1 19.1 %all-gather.3.cloned.1.call-done = bf16[2304,576]{1,0:T(8,128)(2,1)} async-done(((bf16[144,576]{1,0:T(8,128)(2,1)}), bf16[2304,576]{1,0:T(8,128)(2,1)}) %all-gather.3.cloned.1.call-update) | async-done | bytes 2654224 | tf_op jit(solution)/shard_map/all_gather | solution.py:54
  153.1 2.6 constant_dynamic-slice_fusion.1
  155.8 10.4 %reshape.110 = bf16[4,288,4,2,72]{4,3,2,1,0:T(2,128)(2,1)S(1)} reshape(bf16[1,4,2,144,576]{4,3,2,1,0:T(8,128)(2,1)} %constant_dynamic-slice_fusion.1) | data formatting | bytes 2654208 | tf_op jit(solution)/shard_map/reshape | solution.py:76
  166.2 3.9 %constant_dynamic-slice_fusion = bf16[4,288,4,1,72]{4,3,2,1,0:T(2,128)(2,1)} fusion(bf16[4,288,4,2,72]{4,3,2,1,0:T(2,128)(2,1)S(1)} %reshape.110, s32[]{:T(128)S(6)} %select_n.111), kind=kLoop, calls=%fused_computation.32 | loop fusion | bytes 1327108 | tf_op jit(solution)/shard_map/jit(dynamic_index_in_dim)/dynamic_slice | solution.py:77
  170.0 5.9 %copy.11 = bf16[4,288,4,1,72]{1,4,3,2,0:T(8,128)(2,1)} copy(bf16[4,288,4,1,72]{4,3,2,1,0:T(2,128)(2,1)} %constant_dynamic-slice_fusion) | data formatting | bytes 1327104 | tf_op jit(solution)/shard_map/jit(dynamic_index_in_dim)/dynamic_slice | solution.py:77
  175.9 1.8 maximum_select_fusion
  177.8 1.5 convolution_convert_fusion.2
  179.3 7.1 %all-to-all-start.2 = ((bf16[4,72,576]{2,1,0:T(8,128)(2,1)}), bf16[4,72,576]{2,1,0:T(8,128)(2,1)S(1)}, u32[]{:S(2)}, u32[]{:S(2)}) async-start(bf16[4,72,576]{2,1,0:T(8,128)(2,1)} %bitcast.55), calls=%async_computation.2 | async-start | bytes 737280 | tf_op jit(solution)/shard_map/all_to_all | solution.py:21
  187.9 8.3 %all-to-all-done.2 = bf16[4,72,576]{2,1,0:T(8,128)(2,1)S(1)} async-done(((bf16[4,72,576]{2,1,0:T(8,128)(2,1)}), bf16[4,72,576]{2,1,0:T(8,128)(2,1)S(1)}, u32[]{:S(2)}, u32[]{:S(2)}) %all-to-all-start.2) | async-done | bytes 331808 | tf_op jit(solution)/shard_map/all_to_all | solution.py:21
  196.3 5.5 %collective-permute-start.5 = (bf16[72,576]{1,0:T(8,128)(2,1)S(1)}, bf16[72,576]{1,0:T(8,128)(2,1)S(1)}, u32[]{:S(2)}, u32[]{:S(2)}) collective-permute-start(bf16[72,576]{1,0:T(8,128)(2,1)S(1)} %divide_convert_fusion), channel_id=1, source_target_pairs={{0,16},{16,0},{1,17},{17,1},{2,18},{18,2},{3,19},{19,3},{4,20},{20... | collective-permute-start | bytes 248840 | tf_op jit(solution)/shard_map/ppermute | solution.py:85
  202.6 1.8 convolution_convert_fusion.1
  204.4 2.5 reshape.115
  208.4 25.1 %all_to_all.32 = bf16[8,72,576]{2,1,0:T(8,128)(2,1)S(1)} all-to-all(bf16[8,72,576]{2,1,0:T(8,128)(2,1)S(1)} %reshape.116), channel_id=1, replica_groups=mesh['x'=4,'z1'=2,'z0'=2,'c'=2,'y'=8,'z2'=2] {'y'}, dimensions={0} | all-to-all | bytes 1327104 | tf_op jit(solution)/shard_map/all_to_all | solution.py:21
  234.6 3.5 %all-to-all-start.4 = ((bf16[4,72,288]{2,1,0:T(8,128)(2,1)}), bf16[4,72,288]{2,1,0:T(8,128)(2,1)S(1)}, u32[]{:S(2)}, u32[]{:S(2)}) async-start(bf16[4,72,288]{2,1,0:T(8,128)(2,1)} %pad_maximum_fusion), calls=%async_computation.4 | async-start | bytes 442368 | tf_op jit(solution)/shard_map/all_to_all | solution.py:92
  238.1 3.3 %copy.19 = bf16[2,4,2,144,576]{4,1,3,2,0:T(4,128)(2,1)S(1)} copy(bf16[2,4,2,144,576]{4,3,2,1,0:T(8,128)(2,1)} %bitcast.47) | data formatting | bytes 5308416 | tf_op jit(solution)/shard_map/reshape | solution.py:54
  241.5 3.4 %reshape.119 = bf16[576,2304]{1,0:T(8,128)(2,1)} reshape(bf16[2,2,144,4,576]{4,3,2,1,0:T(4,128)(2,1)S(1)} %bitcast.45) | data formatting | bytes 5308416 | tf_op jit(solution)/shard_map/reshape | solution.py:95
  244.9 1.1 all-to-all-done.4
  247.1 2.4 fusion
  249.5 2.6 reshape.120
  252.1 1.4 copy.16
  254.3 15.1 %all_to_all.33 = bf16[8,72,576]{2,1,0:T(8,128)(2,1)S(1)} all-to-all(bf16[8,72,576]{2,1,0:T(8,128)(2,1)S(1)} %reshape.121), channel_id=1, replica_groups=mesh['x'=4,'z1'=2,'z0'=2,'c'=2,'y'=8,'z2'=2] {'x','z0'}, dimensions={0} | all-to-all | bytes 1327104 | tf_op jit(solution)/shard_map/all_to_all | solution.py:21
  269.6 6.0 %collective-permute-start.6 = (bf16[72,288]{1,0:T(8,128)(2,1)S(1)}, bf16[72,288]{1,0:T(8,128)(2,1)S(1)}, u32[]{:S(2)}, u32[]{:S(2)}) collective-permute-start(bf16[72,288]{1,0:T(8,128)(2,1)S(1)} %get-tuple-element.8), channel_id=1, source_target_pairs={{0,16},{16,0},{1,17},{17,1},{2,18},{18,2},{3,19},{19,3},{4,20},{20... | collective-permute-start | bytes 124424 | tf_op jit(solution)/shard_map/ppermute | solution.py:101
  (49 shorter events, 17.1 us)
Async XLA Ops:
  6.5 95.2 %all-gather.5.cloned.1.call-start = ((), (), s32[]{:S(2)}) async-start(), calls=%async_computation.7 | async-start | bytes 3133440 | tf_op jit(solution)/shard_map/all_gather | solution.py:51
  8.2 144.9 %all-gather.3.cloned.1.call-start = ((), (), s32[]{:S(2)}) async-start(), calls=%async_computation.6 | async-start | bytes 3133440 | tf_op jit(solution)/shard_map/all_gather | solution.py:54
  9.3 0.7 collective-permute-start
  10.0 0.7 copy-start.2
  11.7 21.5 %collective-permute-start.1 = (bf16[72,576]{1,0:T(8,128)(2,1)S(1)}, bf16[72,576]{1,0:T(8,128)(2,1)S(1)}, u32[]{:S(2)}, u32[]{:S(2)}) collective-permute-start(bf16[72,576]{1,0:T(8,128)(2,1)S(1)} %select_bitcast_fusion), channel_id=1, source_target_pairs={{0,1},{1,0},{2,3},{3,2},{4,5},{5,4},{6,7},{7,6},{8,9},{9,8},{10,11... | collective-permute-start | bytes 248840 | tf_op jit(solution)/shard_map/ppermute | solution.py:59
  34.3 4.3 %collective-permute-start.2 = (bf16[72,288]{1,0:T(8,128)(2,1)S(1)}, bf16[72,288]{1,0:T(8,128)(2,1)S(1)}, u32[]{:S(2)}, u32[]{:S(2)}) collective-permute-start(bf16[72,288]{1,0:T(8,128)(2,1)S(1)} %get-tuple-element.6), channel_id=1, source_target_pairs={{0,16},{16,0},{1,17},{17,1},{2,18},{18,2},{3,19},{19,3},{4,20},{20... | collective-permute-start | bytes 124424 | tf_op jit(solution)/shard_map/ppermute | solution.py:64
  104.3 12.0 %collective-permute-start.3 = (bf16[72,576]{1,0:T(8,128)(2,1)S(1)}, bf16[72,576]{1,0:T(8,128)(2,1)S(1)}, u32[]{:S(2)}, u32[]{:S(2)}) collective-permute-start(bf16[72,576]{1,0:T(8,128)(2,1)S(1)} %select_convert_fusion), channel_id=1, source_target_pairs={{0,16},{16,0},{1,17},{17,1},{2,18},{18,2},{3,19},{19,3},{4,20},{20... | collective-permute-start | bytes 248840 | tf_op jit(solution)/shard_map/ppermute | solution.py:71
  130.7 45.2 %collective-permute-start.4 = (bf16[8,72,576]{2,1,0:T(8,128)(2,1)S(1)}, bf16[8,72,576]{2,1,0:T(8,128)(2,1)}, u32[]{:S(2)}, u32[]{:S(2)}) collective-permute-start(bf16[8,72,576]{2,1,0:T(8,128)(2,1)S(1)} %all_to_all.31), channel_id=1, source_target_pairs={{0,16},{16,0},{1,17},{17,1},{2,18},{18,2},{3,19},{19,3},{4,20},{20... | collective-permute-start | bytes 1990664 | tf_op jit(solution)/shard_map/ppermute | solution.py:73
  175.9 1.8 copy-start.1
  177.8 24.9 %copy-start = (bf16[2304,576]{1,0:T(8,128)(2,1)S(1)}, bf16[2304,576]{1,0:T(8,128)(2,1)}, u32[]{:S(2)}) copy-start(bf16[2304,576]{1,0:T(8,128)(2,1)} %all-gather.5.cloned.1.call-done) | copy-start | bytes 7962628
  179.3 16.9 %all-to-all-start.2 = ((bf16[4,72,576]{2,1,0:T(8,128)(2,1)}), bf16[4,72,576]{2,1,0:T(8,128)(2,1)S(1)}, u32[]{:S(2)}, u32[]{:S(2)}) async-start(bf16[4,72,576]{2,1,0:T(8,128)(2,1)} %bitcast.55), calls=%async_computation.2 | async-start | bytes 737280 | tf_op jit(solution)/shard_map/all_to_all | solution.py:21
  196.3 6.3 %collective-permute-start.5 = (bf16[72,576]{1,0:T(8,128)(2,1)S(1)}, bf16[72,576]{1,0:T(8,128)(2,1)S(1)}, u32[]{:S(2)}, u32[]{:S(2)}) collective-permute-start(bf16[72,576]{1,0:T(8,128)(2,1)S(1)} %divide_convert_fusion), channel_id=1, source_target_pairs={{0,16},{16,0},{1,17},{17,1},{2,18},{18,2},{3,19},{19,3},{4,20},{20... | collective-permute-start | bytes 248840 | tf_op jit(solution)/shard_map/ppermute | solution.py:85
  234.6 11.3 %all-to-all-start.4 = ((bf16[4,72,288]{2,1,0:T(8,128)(2,1)}), bf16[4,72,288]{2,1,0:T(8,128)(2,1)S(1)}, u32[]{:S(2)}, u32[]{:S(2)}) async-start(bf16[4,72,288]{2,1,0:T(8,128)(2,1)} %pad_maximum_fusion), calls=%async_computation.4 | async-start | bytes 442368 | tf_op jit(solution)/shard_map/all_to_all | solution.py:92
  269.6 6.9 %collective-permute-start.6 = (bf16[72,288]{1,0:T(8,128)(2,1)S(1)}, bf16[72,288]{1,0:T(8,128)(2,1)S(1)}, u32[]{:S(2)}, u32[]{:S(2)}) collective-permute-start(bf16[72,288]{1,0:T(8,128)(2,1)S(1)} %get-tuple-element.8), channel_id=1, source_target_pairs={{0,16},{16,0},{1,17},{17,1},{2,18},{18,2},{3,19},{19,3},{4,20},{20... | collective-permute-start | bytes 124424 | tf_op jit(solution)/shard_map/ppermute | solution.py:101
Sparse Core Ops, SparseCore 0:
  9.4 92.2 all-gather.4
  103.9 49.2 all-gather.2

commit v3 on v2

v3 whole, which is shorter than its diff:
```python
import jax
import jax.numpy as jnp
from jax import lax
from jax.sharding import Mesh, PartitionSpec as P

DAMPING = 0.1
AXES = ("x", "z1", "z0", "c", "y", "z2")
ROWS = ("x", "z1", "z0", "c")
RING = ("x", "z0")
PART = ("z1", "z2")
SWAP = [(0, 1), (1, 0)]


def gather(block, axes, count):
    return lax.all_to_all(
        jnp.broadcast_to(block[None], (count,) + block.shape), axes, 0, 0, tiled=True
    )


def scatter_sum(blocks, axes):
    got = lax.all_to_all(blocks, axes, 0, 0, tiled=True)
    return jnp.sum(got.astype(jnp.float32), axis=0)


def dot(left, right, left_dim, right_dim):
    return lax.dot_general(
        left, right, (((left_dim,), (right_dim,)), ((), ())), preferred_element_type=jnp.float32
    )


def in_order(first, mine, other, axis):
    return jnp.where(
        first,
        jnp.concatenate([mine, other], axis=axis),
        jnp.concatenate([other, mine], axis=axis),
    )


def pairs_z1y0():
    return [(z1 * 8 + y, (y % 2) * 8 + (y // 2) * 2 + z1) for z1 in range(2) for y in range(8)]


def pairs_part(d1, d2):
    return [(i, i ^ (2 * d1 + d2)) for i in range(4)]


def pairs_rows():
    return [
        (z1 * 8 + z0 * 4 + c * 2 + z2, c * 8 + z1 * 4 + z2 * 2 + z0)
        for z1 in range(2)
        for z0 in range(2)
        for c in range(2)
        for z2 in range(2)
    ]


def pack(rows):
    q = rows.shape[0] // 2
    return jnp.concatenate([rows[:q], rows[q:]], axis=1)


def body(grad_parts, basis_in, basis_out, eig_in, eig_out):
    bf16, f32 = jnp.bfloat16, jnp.float32
    x, z1, z0, c, y, z2 = (lax.axis_index(a) for a in AXES)
    rows, cols = basis_in.shape
    half, quarter = rows // 2, cols // 4
    wide = 2 * rows
    low_core, low_rep, low_z1 = c == 0, z2 == 0, z1 == 0


    grad = grad_parts[0]
    parts = jnp.stack([pack(grad[:, i * quarter : (i + 1) * quarter]) for i in range(4)])

    def piece(d1, d2):
        which = 2 * (z2 ^ d2) + (z1 ^ d1)
        return lax.dynamic_index_in_dim(parts, which, 0, keepdims=False)

    def from_part(d1, d2):
        return lax.ppermute(piece(d1, d2), PART, pairs_part(d1, d2)).astype(f32)

    mine = (piece(0, 0).astype(f32) + from_part(0, 1)).astype(bf16)
    other = (from_part(1, 0) + from_part(1, 1)).astype(bf16)
    grad = in_order(low_z1, mine, other, 1)

    bi = basis_in.astype(bf16)
    bi = jnp.where(low_rep, bi[:half], bi[half:])
    bi = lax.ppermute(bi, ("z1", "z0", "c", "z2"), pairs_rows())
    bi = gather(bi, RING, 8)
    bi = in_order(low_core, bi, lax.ppermute(bi, "c", SWAP), 1).reshape(8 * rows, cols)

    bo = basis_out.astype(bf16)
    low = jnp.concatenate([bo[:, i * quarter : i * quarter + half] for i in range(4)], axis=1)
    high = jnp.concatenate([bo[:, i * quarter + half : (i + 1) * quarter] for i in range(4)], axis=1)
    low, high = pack(low), pack(high)
    bo = jnp.stack([jnp.where(low_rep, low, high), jnp.where(low_rep, high, low)])
    bo = lax.ppermute(bo, ("z1", "y"), pairs_z1y0())
    bo = lax.all_gather(bo, "y", axis=0)
    bo = bo.reshape(4, 2, 2, half, 2, wide).transpose(2, 1, 4, 3, 0, 5)
    near, far = bo.reshape(2, wide, 4 * wide)

    grad = gather(grad, "y", 8)
    grad = grad.reshape(8, half, 4, quarter).transpose(2, 1, 0, 3).reshape(wide, 8 * quarter)
    part = dot(grad, bi, 1, 0).astype(bf16).reshape(4, half, cols)
    turned = scatter_sum(part, PART).astype(bf16)
    turned = gather(turned, RING, 8)
    other = lax.ppermute(turned, "c", SWAP)
    turned = in_order(low_core, turned[:, None], other[:, None], 1).reshape(16 * half, cols)

    part = dot(near, turned, 1, 0).astype(bf16).reshape(4, half, cols)
    rotated = scatter_sum(part, PART)
    first = (((x * 2 + z1) * 2 + z0) * 2 + c) * rows + z2 * half
    out_scale = lax.dynamic_slice_in_dim(eig_out, first, half, 0)
    in_scale = lax.dynamic_slice_in_dim(eig_in, y * cols, cols, 0)
    scaled = (rotated / (out_scale[:, None] * in_scale[None, :] + DAMPING)).astype(bf16)
    scaled = gather(scaled, PART, 4).reshape(wide, cols)

    part = dot(scaled, bi, 1, 1).astype(bf16)
    part = part.reshape(4, half, 8, quarter).transpose(2, 1, 0, 3).reshape(8, half, cols)
    back = scatter_sum(part, "y").astype(bf16)
    other = lax.ppermute(back, "z1", SWAP)
    first, second = jnp.where(low_z1, back, other), jnp.where(low_z1, other, back)
    back = jnp.concatenate(
        [
            jnp.concatenate(
                [first[:, i * quarter : (i + 1) * quarter], second[:, i * quarter : (i + 1) * quarter]],
                axis=1,
            )
            for i in range(4)
        ],
        axis=0,
    )

    part = jnp.concatenate([dot(near, back, 0, 0), dot(far, back, 0, 0)], axis=1)
    part = part.reshape(8, 2, half, cols)
    keep = jnp.where(low_core, part[:, 0], part[:, 1])
    give = jnp.where(low_core, part[:, 1], part[:, 0]).astype(bf16)
    part = (keep + lax.ppermute(give, "c", SWAP).astype(f32)).astype(bf16)
    out = scatter_sum(part, RING).astype(bf16)
    return in_order(low_rep, out[:, :wide], out[:, wide:], 0)


def solution(mesh):
    fine = Mesh(mesh.devices.reshape(4, 2, 2, 2, 8, 2), AXES)
    in_specs = (P("z2", ROWS, "y"), P(ROWS, "y"), P(ROWS, "y"), P(), P())
    out_specs = P(ROWS, ("y", "z2"))
    return jax.shard_map(body, mesh=fine, in_specs=in_specs, out_specs=out_specs, check_vma=False)
```

time: 285 us -> 229 us (0.80)
  waiting for transfers between devices: 69.4 us -> 43.1 us
  local copies, waits for them, and re-layouts: 43.7 us -> 21.8 us
  blocking collectives: 88.1 us -> 71.3 us
  starting transfers between devices: 52.2 us -> 64 us
  matrix products: 8.28 us -> 4.2 us
    all_gather x2 -> x1, waiting for transfers between devices: 46.7 us -> 0.02 us  [body(): bo = lax.all_gather(bo, 'y', axis=0)]
    all_to_all x2, blocking collectives: 47.9 us -> 25.2 us  [gather(): lax.all_to_all(jnp.broadcast_to(block[None], (count,) + block.shape), axe...]
    all_to_all x1 -> x2, waiting for transfers between devices: 1.08 us -> 17.7 us  [gather(): lax.all_to_all(jnp.broadcast_to(block[None], (count,) + block.shape), axe...]
    reshape x13 -> x7, local copies, waits for them, and re-layouts: 27.7 us -> 11.5 us  [the longest x2 5.49 us: body(): bo = bo.reshape(4, 2, 2, half, 2, wide).transpose(2, 1, 4, 3, 0, 5)]
    dynamic_slice x3 -> x0, local copies, waits for them, and re-layouts: 12.4 us -> none  [the longest x2 9.77 us: body(): mine = lax.dynamic_index_in_dim(mine, z2, 3, keepdims=False)]
    all_to_all x1 -> x2, starting transfers between devices: 3.48 us -> 12.8 us  [gather(): lax.all_to_all(jnp.broadcast_to(block[None], (count,) + block.shape), axe...]
    ppermute x1, starting transfers between devices: 3.38 us -> 9.32 us  [body(): other = lax.ppermute(turned, 'c', SWAP)]
    all_to_all x2 -> x3, blocking collectives: 40.3 us -> 46 us  [scatter_sum(): got = lax.all_to_all(blocks, axes, 0, 0, tiled=True)]
  transfers between devices with their start and end apart: 11 -> 13, of which waited for: 9 -> 6; matrix products, arithmetic and copies ran while one was open for 14% -> 7% of each run, Pallas kernels for 0% -> 0%
where the time goes in v3:
time: 229 us; the launch traced here: 228 us
  blocking collectives  71.3 us (31%)
  starting transfers between devices  64 us (28%)
  waiting for transfers between devices  43.1 us (19%)
  local copies, waits for them, and re-layouts  21.8 us (10%)
  between operations  13.9 us (6%)
  other arithmetic  9.35 us (4%)
  matrix products  4.2 us (2%)
    all_to_all x3, blocking collectives, scatter_sum(): got = lax.all_to_all(blocks, axes, 0, 0, tiled=True)  46 us
    all_to_all x2, blocking collectives, gather(): lax.all_to_all(jnp.broadcast_to(block[None], (count,) + block.shape), axe...  25.2 us
    all_to_all x2, waiting for transfers between devices, gather(): lax.all_to_all(jnp.broadcast_to(block[None], (count,) + block.shape), axe...  17.7 us
    all_to_all x2, starting transfers between devices, gather(): lax.all_to_all(jnp.broadcast_to(block[None], (count,) + block.shape), axe...  12.8 us
    ppermute x1, starting transfers between devices, body(): part = (keep + lax.ppermute(give, 'c', SWAP).astype(f32)).astype(bf16)  11.7 us
    ppermute x3, starting transfers between devices, from_part(): return lax.ppermute(piece(d1, d2), PART, pairs_part(d1, d2)).astype(f32)  11.4 us
    ppermute x1, starting transfers between devices, body(): other = lax.ppermute(turned, 'c', SWAP)  9.32 us
    ppermute x1, starting transfers between devices, body(): bi = lax.ppermute(bi, ('z1', 'z0', 'c', 'z2'), pairs_rows())  7.2 us
  transfers between devices with their start and end apart: 13, of which 6 were waited for; matrix products, arithmetic and copies ran while one was open for 7% of the time, Pallas kernels for 0%

profile of v3, /device:TPU:1, one launch (start us, length us, event | category | flops | bytes accessed | tf_op | source)
XLA Modules:
  0.0 227.6 jit_solution(8706353359624625120)
XLA Ops:
  7.6 7.2 %collective-permute-start.4 = (bf16[72,576]{1,0:T(8,128)(2,1)S(1)}, bf16[72,576]{1,0:T(8,128)(2,1)S(1)}, u32[]{:S(2)}, u32[]{:S(2)}) collective-permute-start(bf16[72,576]{1,0:T(8,128)(2,1)S(1)} %slice_select_fusion), channel_id=1, source_target_pairs={{0,0},{1,16},{16,64},{17,80},{32,1},{33,17},{48,65},{49,81},{64,32... | collective-permute-start | bytes 248840 | tf_op jit(solution)/shard_map/ppermute | solution.py:87
  14.8 7.1 %collective-permute-done.4 = bf16[72,576]{1,0:T(8,128)(2,1)S(1)} collective-permute-done((bf16[72,576]{1,0:T(8,128)(2,1)S(1)}, bf16[72,576]{1,0:T(8,128)(2,1)S(1)}, u32[]{:S(2)}, u32[]{:S(2)}) %collective-permute-start.4) | collective-permute-done | bytes 82976 | tf_op jit(solution)/shard_map/ppermute | solution.py:87
  22.9 5.9 %all-to-all-start.1 = ((bf16[8,72,576]{2,1,0:T(8,128)(2,1)}), bf16[8,72,576]{2,1,0:T(8,128)(2,1)S(1)}, u32[]{:S(2)}, u32[]{:S(2)}) async-start(bf16[8,72,576]{2,1,0:T(8,128)(2,1)} %broadcast_in_dim.13), calls=%async_computation.1 | async-start | bytes 1474560 | tf_op jit(solution)/shard_map/all_to_all | solution.py:15
  29.3 3.0 %collective-permute-start.1 = (bf16[72,288]{1,0:T(8,128)(2,1)S(1)}, bf16[72,288]{1,0:T(8,128)(2,1)S(1)}, u32[]{:S(2)}, u32[]{:S(2)}) collective-permute-start(bf16[72,288]{1,0:T(8,128)(2,1)S(1)} %get-tuple-element.7), channel_id=1, source_target_pairs={{0,1},{1,0},{64,65},{65,64},{2,3},{3,2},{66,67},{67,66},{4,5},{5,4... | collective-permute-start | bytes 124424 | tf_op jit(solution)/shard_map/ppermute | solution.py:79
  32.3 4.5 %collective-permute-start.3 = (bf16[72,288]{1,0:T(8,128)(2,1)S(1)}, bf16[72,288]{1,0:T(8,128)(2,1)S(1)}, u32[]{:S(2)}, u32[]{:S(2)}) collective-permute-start(bf16[72,288]{1,0:T(8,128)(2,1)S(1)} %get-tuple-element.8), channel_id=1, source_target_pairs={{0,65},{1,64},{64,1},{65,0},{2,67},{3,66},{66,3},{67,2},{4,69},{5,... | collective-permute-start | bytes 124424 | tf_op jit(solution)/shard_map/ppermute | solution.py:79
  36.9 3.8 %collective-permute-start.2 = (bf16[72,288]{1,0:T(8,128)(2,1)S(1)}, bf16[72,288]{1,0:T(8,128)(2,1)S(1)}, u32[]{:S(2)}, u32[]{:S(2)}) collective-permute-start(bf16[72,288]{1,0:T(8,128)(2,1)S(1)} %get-tuple-element.9), channel_id=1, source_target_pairs={{0,64},{1,65},{64,0},{65,1},{2,66},{3,67},{66,2},{67,3},{4,68},{5,... | collective-permute-start | bytes 124424 | tf_op jit(solution)/shard_map/ppermute | solution.py:79
  40.8 4.3 %collective-permute-done.2 = bf16[72,288]{1,0:T(8,128)(2,1)S(1)} collective-permute-done((bf16[72,288]{1,0:T(8,128)(2,1)S(1)}, bf16[72,288]{1,0:T(8,128)(2,1)S(1)}, u32[]{:S(2)}, u32[]{:S(2)}) %collective-permute-start.2) | collective-permute-done | bytes 41504 | tf_op jit(solution)/shard_map/ppermute | solution.py:79
  46.2 6.8 %all-to-all-start = ((bf16[8,72,576]{2,1,0:T(8,128)(2,1)}), bf16[8,72,576]{2,1,0:T(8,128)(2,1)S(1)}, u32[]{:S(2)}, u32[]{:S(2)}) async-start(bf16[8,72,576]{2,1,0:T(8,128)(2,1)} %broadcast_in_dim.12), calls=%async_computation | async-start | bytes 1474560 | tf_op jit(solution)/shard_map/all_to_all | solution.py:15
  53.4 2.8 %collective-permute-start.5 = (bf16[8,72,576]{2,1,0:T(8,128)(2,1)S(1)}, bf16[8,72,576]{2,1,0:T(8,128)(2,1)}, u32[]{:S(2)}, u32[]{:S(2)}) collective-permute-start(bf16[8,72,576]{2,1,0:T(8,128)(2,1)S(1)} %all-to-all-done.1), channel_id=1, source_target_pairs={{0,16},{16,0},{1,17},{17,1},{2,18},{18,2},{3,19},{19,3},{4,20},{20... | collective-permute-start | bytes 1990664 | tf_op jit(solution)/shard_map/ppermute | solution.py:89
  57.9 17.7 %all-to-all-done = bf16[8,72,576]{2,1,0:T(8,128)(2,1)S(1)} async-done(((bf16[8,72,576]{2,1,0:T(8,128)(2,1)}), bf16[8,72,576]{2,1,0:T(8,128)(2,1)S(1)}, u32[]{:S(2)}, u32[]{:S(2)}) %all-to-all-start) | async-done | bytes 663584 | tf_op jit(solution)/shard_map/all_to_all | solution.py:15
  77.0 1.2 reshape.244
  78.2 1.9 maximum_select_fusion
  81.3 12.1 %all_to_all.40 = bf16[4,72,576]{2,1,0:T(8,128)(2,1)S(1)} all-to-all(bf16[4,72,576]{2,1,0:T(8,128)(2,1)S(1)} %bitcast.67), channel_id=1, replica_groups=mesh['x'=4,'z1'=2,'z0'=2,'c'=2,'y'=8,'z2'=2] {'z1','z2'}, dimensions={0} | all-to-all | bytes 663552 | tf_op jit(solution)/shard_map/all_to_all | solution.py:21
  93.5 11.8 %all_to_all.41 = bf16[8,72,576]{2,1,0:T(8,128)(2,1)} all-to-all(bf16[8,72,576]{2,1,0:T(8,128)(2,1)S(1)} %broadcast_in_dim.14), channel_id=1, replica_groups=mesh['x'=4,'z1'=2,'z0'=2,'c'=2,'y'=8,'z2'=2] {'x','z0'}, dimensions={0} | all-to-all | bytes 1327104 | tf_op jit(solution)/shard_map/all_to_all | solution.py:15
  105.3 9.3 %collective-permute-start.6 = (bf16[8,72,576]{2,1,0:T(8,128)(2,1)}, bf16[8,72,576]{2,1,0:T(8,128)(2,1)}, u32[]{:S(2)}, u32[]{:S(2)}) collective-permute-start(bf16[8,72,576]{2,1,0:T(8,128)(2,1)} %all_to_all.41), channel_id=1, source_target_pairs={{0,16},{16,0},{1,17},{17,1},{2,18},{18,2},{3,19},{19,3},{4,20},{20... | collective-permute-start | bytes 1990664 | tf_op jit(solution)/shard_map/ppermute | solution.py:106
  114.6 4.1 %reshape.242 = bf16[4,2,2,72,2,288]{5,4,3,2,1,0:T(2,128)(2,1)S(1)} reshape(bf16[16,72,576]{2,1,0:T(8,128)(2,1)} %all-gather.3.cloned.1.call-done) | data formatting | bytes 2654208 | tf_op jit(solution)/shard_map/reshape | solution.py:98
  118.7 1.4 copy.23
  121.3 2.4 %maximum_select_fusion.1 = bf16[8,2,72,576]{3,2,1,0:T(8,128)(2,1)S(1)} fusion(bf16[8,1,72,576]{3,2,1,0:T(8,128)(2,1)} %bitcast.18, bf16[8,1,72,576]{3,2,1,0:T(8,128)(2,1)} %bitcast.17, pred[]{:T(512)S(6)} %eq.10), kind=kLoop, calls=%fused_computation.4 | loop fusion | flops 1990656 | bytes 2654209 | tf_op jit(solution)/shard_map/jit(_where)/select_n | solution.py:32
  123.7 1.5 convolution_convert_fusion.1
  125.2 6.0 %all-to-all-start.4 = ((bf16[4,72,576]{2,1,0:T(8,128)(2,1)}), bf16[4,72,576]{2,1,0:T(8,128)(2,1)S(1)}, u32[]{:S(2)}, u32[]{:S(2)}) async-start(bf16[4,72,576]{2,1,0:T(8,128)(2,1)} %bitcast.20), calls=%async_computation.4 | async-start | bytes 737280 | tf_op jit(solution)/shard_map/all_to_all | solution.py:21
  132.7 7.1 %all-to-all-done.4 = bf16[4,72,576]{2,1,0:T(8,128)(2,1)S(1)} async-done(((bf16[4,72,576]{2,1,0:T(8,128)(2,1)}), bf16[4,72,576]{2,1,0:T(8,128)(2,1)S(1)}, u32[]{:S(2)}, u32[]{:S(2)}) %all-to-all-start.4) | async-done | bytes 331808 | tf_op jit(solution)/shard_map/all_to_all | solution.py:21
  140.1 13.4 %all_to_all.42 = bf16[4,72,576]{2,1,0:T(8,128)(2,1)S(1)} all-to-all(bf16[4,72,576]{2,1,0:T(8,128)(2,1)S(1)} %broadcast_in_dim.17), channel_id=1, replica_groups=mesh['x'=4,'z1'=2,'z0'=2,'c'=2,'y'=8,'z2'=2] {'z1','z2'}, dimensions={0} | all-to-all | bytes 663552 | tf_op jit(solution)/shard_map/all_to_all | solution.py:15
  154.2 1.5 reshape.248
  156.7 1.6 reshape.249
  158.3 18.3 %all_to_all.43 = bf16[8,72,576]{2,1,0:T(8,128)(2,1)S(1)} all-to-all(bf16[8,72,576]{2,1,0:T(8,128)(2,1)} %reshape.249), channel_id=1, replica_groups=mesh['x'=4,'z1'=2,'z0'=2,'c'=2,'y'=8,'z2'=2] {'y'}, dimensions={0} | all-to-all | bytes 1327104 | tf_op jit(solution)/shard_map/all_to_all | solution.py:21
  176.8 2.1 collective-permute-start.7
  179.4 5.0 %collective-permute-done.7 = bf16[72,576]{1,0:T(8,128)(2,1)S(1)} collective-permute-done((bf16[72,576]{1,0:T(8,128)(2,1)S(1)}, bf16[72,576]{1,0:T(8,128)(2,1)S(1)}, u32[]{:S(2)}, u32[]{:S(2)}) %collective-permute-start.7) | collective-permute-done | bytes 82976 | tf_op jit(solution)/shard_map/ppermute | solution.py:120
  185.9 1.7 pad_maximum_fusion
  187.6 2.7 %copy.20 = f32[1152,576]{1,0:T(8,128)S(1)} copy(f32[1152,576]{0,1:T(8,128)} %pad_maximum_fusion) | data formatting | bytes 5308416 | tf_op jit(solution)/shard_map/concatenate | solution.py:133
  190.5 11.7 %collective-permute-start.8 = (bf16[8,72,576]{2,1,0:T(8,128)(2,1)S(1)}, bf16[8,72,576]{2,1,0:T(8,128)(2,1)S(1)}, u32[]{:S(2)}, u32[]{:S(2)}) collective-permute-start(bf16[8,72,576]{2,1,0:T(8,128)(2,1)S(1)} %fusion.1), channel_id=1, source_target_pairs={{0,16},{16,0},{1,17},{17,1},{2,18},{18,2},{3,19},{19,3},{4,20},{20... | collective-permute-start | bytes 1990664 | tf_op jit(solution)/shard_map/ppermute | solution.py:137
  202.2 1.8 collective-permute-done.8
  204.2 15.6 %all_to_all.44 = bf16[8,72,576]{2,1,0:T(8,128)(2,1)S(1)} all-to-all(bf16[8,72,576]{2,1,0:T(8,128)(2,1)S(1)} %fusion), channel_id=1, replica_groups=mesh['x'=4,'z1'=2,'z0'=2,'c'=2,'y'=8,'z2'=2] {'x','z0'}, dimensions={0} | all-to-all | bytes 1327104 | tf_op jit(solution)/shard_map/all_to_all | solution.py:21
  (69 shorter events, 16.1 us)
Async XLA Ops:
  6.5 22.3 %copy-start.4 = (bf16[1,144,576]{2,1,0:T(8,128)(2,1)S(1)}, bf16[1,144,576]{2,1,0:T(8,128)(2,1)}, u32[]{:S(2)}) copy-start(bf16[1,144,576]{2,1,0:T(8,128)(2,1)} %param.5) | copy-start | bytes 497668
  7.6 14.4 %collective-permute-start.4 = (bf16[72,576]{1,0:T(8,128)(2,1)S(1)}, bf16[72,576]{1,0:T(8,128)(2,1)S(1)}, u32[]{:S(2)}, u32[]{:S(2)}) collective-permute-start(bf16[72,576]{1,0:T(8,128)(2,1)S(1)} %slice_select_fusion), channel_id=1, source_target_pairs={{0,0},{1,16},{16,64},{17,80},{32,1},{33,17},{48,65},{49,81},{64,32... | collective-permute-start | bytes 248840 | tf_op jit(solution)/shard_map/ppermute | solution.py:87
  22.9 17.8 %copy-start.5 = (f32[144,576]{1,0:T(8,128)S(1)}, f32[144,576]{1,0:T(8,128)}, u32[]{:S(2)}) copy-start(f32[144,576]{1,0:T(8,128)} %param.7) | copy-start | bytes 995332
  22.9 22.4 %all-to-all-start.1 = ((bf16[8,72,576]{2,1,0:T(8,128)(2,1)}), bf16[8,72,576]{2,1,0:T(8,128)(2,1)S(1)}, u32[]{:S(2)}, u32[]{:S(2)}) async-start(bf16[8,72,576]{2,1,0:T(8,128)(2,1)} %broadcast_in_dim.13), calls=%async_computation.1 | async-start | bytes 1474560 | tf_op jit(solution)/shard_map/all_to_all | solution.py:15
  29.3 11.5 %collective-permute-start.1 = (bf16[72,288]{1,0:T(8,128)(2,1)S(1)}, bf16[72,288]{1,0:T(8,128)(2,1)S(1)}, u32[]{:S(2)}, u32[]{:S(2)}) collective-permute-start(bf16[72,288]{1,0:T(8,128)(2,1)S(1)} %get-tuple-element.7), channel_id=1, source_target_pairs={{0,1},{1,0},{64,65},{65,64},{2,3},{3,2},{66,67},{67,66},{4,5},{5,4... | collective-permute-start | bytes 124424 | tf_op jit(solution)/shard_map/ppermute | solution.py:79
  32.3 8.5 %collective-permute-start.3 = (bf16[72,288]{1,0:T(8,128)(2,1)S(1)}, bf16[72,288]{1,0:T(8,128)(2,1)S(1)}, u32[]{:S(2)}, u32[]{:S(2)}) collective-permute-start(bf16[72,288]{1,0:T(8,128)(2,1)S(1)} %get-tuple-element.8), channel_id=1, source_target_pairs={{0,65},{1,64},{64,1},{65,0},{2,67},{3,66},{66,3},{67,2},{4,69},{5,... | collective-permute-start | bytes 124424 | tf_op jit(solution)/shard_map/ppermute | solution.py:79
  36.9 8.2 %collective-permute-start.2 = (bf16[72,288]{1,0:T(8,128)(2,1)S(1)}, bf16[72,288]{1,0:T(8,128)(2,1)S(1)}, u32[]{:S(2)}, u32[]{:S(2)}) collective-permute-start(bf16[72,288]{1,0:T(8,128)(2,1)S(1)} %get-tuple-element.9), channel_id=1, source_target_pairs={{0,64},{1,65},{64,0},{65,1},{2,66},{3,67},{66,2},{67,3},{4,68},{5,... | collective-permute-start | bytes 124424 | tf_op jit(solution)/shard_map/ppermute | solution.py:79
  46.2 29.3 %all-to-all-start = ((bf16[8,72,576]{2,1,0:T(8,128)(2,1)}), bf16[8,72,576]{2,1,0:T(8,128)(2,1)S(1)}, u32[]{:S(2)}, u32[]{:S(2)}) async-start(bf16[8,72,576]{2,1,0:T(8,128)(2,1)} %broadcast_in_dim.12), calls=%async_computation | async-start | bytes 1474560 | tf_op jit(solution)/shard_map/all_to_all | solution.py:15
  53.0 61.6 %all-gather.3.cloned.1.call-start = ((), (), s32[]{:S(2)}) async-start(), calls=%async_computation.8 | async-start | bytes 1658880 | tf_op jit(solution)/shard_map/all_gather | solution.py:97
  53.4 24.8 %collective-permute-start.5 = (bf16[8,72,576]{2,1,0:T(8,128)(2,1)S(1)}, bf16[8,72,576]{2,1,0:T(8,128)(2,1)}, u32[]{:S(2)}, u32[]{:S(2)}) collective-permute-start(bf16[8,72,576]{2,1,0:T(8,128)(2,1)S(1)} %all-to-all-done.1), channel_id=1, source_target_pairs={{0,16},{16,0},{1,17},{17,1},{2,18},{18,2},{3,19},{19,3},{4,20},{20... | collective-permute-start | bytes 1990664 | tf_op jit(solution)/shard_map/ppermute | solution.py:89
  56.4 0.7 collective-permute-start
  57.1 0.7 copy-start.6
  80.1 1.1 copy-start
  105.3 16.1 %collective-permute-start.6 = (bf16[8,72,576]{2,1,0:T(8,128)(2,1)}, bf16[8,72,576]{2,1,0:T(8,128)(2,1)}, u32[]{:S(2)}, u32[]{:S(2)}) collective-permute-start(bf16[8,72,576]{2,1,0:T(8,128)(2,1)} %all_to_all.41), channel_id=1, source_target_pairs={{0,16},{16,0},{1,17},{17,1},{2,18},{18,2},{3,19},{19,3},{4,20},{20... | collective-permute-start | bytes 1990664 | tf_op jit(solution)/shard_map/ppermute | solution.py:106
  121.3 2.4 %copy-start.2 = (bf16[288,1152]{1,0:T(8,128)(2,1)}, bf16[288,1152]{1,0:T(8,128)(2,1)S(1)}, u32[]{:S(2)}) copy-start(bf16[288,1152]{1,0:T(8,128)(2,1)S(1)} %unstack.13) | copy-start | bytes 1990660
  125.2 28.3 %copy-start.1 = (bf16[8,144,576]{2,1,0:T(8,128)(2,1)S(1)}, bf16[8,144,576]{2,1,0:T(8,128)(2,1)}, u32[]{:S(2)}) copy-start(bf16[8,144,576]{2,1,0:T(8,128)(2,1)} %copy-done) | copy-start | bytes 3981316
  125.2 14.7 %all-to-all-start.4 = ((bf16[4,72,576]{2,1,0:T(8,128)(2,1)}), bf16[4,72,576]{2,1,0:T(8,128)(2,1)S(1)}, u32[]{:S(2)}, u32[]{:S(2)}) async-start(bf16[4,72,576]{2,1,0:T(8,128)(2,1)} %bitcast.20), calls=%async_computation.4 | async-start | bytes 737280 | tf_op jit(solution)/shard_map/all_to_all | solution.py:21
  176.7 8.0 %copy-start.3 = (bf16[288,1152]{1,0:T(8,128)(2,1)S(1)}, bf16[288,1152]{1,0:T(8,128)(2,1)}, u32[]{:S(2)}) copy-start(bf16[288,1152]{1,0:T(8,128)(2,1)} %copy-done.2) | copy-start | bytes 1990660
  176.8 7.6 %collective-permute-start.7 = (bf16[72,576]{1,0:T(8,128)(2,1)S(1)}, bf16[72,576]{1,0:T(8,128)(2,1)S(1)}, u32[]{:S(2)}, u32[]{:S(2)}) collective-permute-start(bf16[72,576]{1,0:T(8,128)(2,1)S(1)} %reduce_sum.47), channel_id=1, source_target_pairs={{0,64},{64,0},{1,65},{65,1},{2,66},{66,2},{3,67},{67,3},{4,68},{68... | collective-permute-start | bytes 248840 | tf_op jit(solution)/shard_map/ppermute | solution.py:120
  190.5 13.5 %collective-permute-start.8 = (bf16[8,72,576]{2,1,0:T(8,128)(2,1)S(1)}, bf16[8,72,576]{2,1,0:T(8,128)(2,1)S(1)}, u32[]{:S(2)}, u32[]{:S(2)}) collective-permute-start(bf16[8,72,576]{2,1,0:T(8,128)(2,1)S(1)} %fusion.1), channel_id=1, source_target_pairs={{0,16},{16,0},{1,17},{17,1},{2,18},{18,2},{3,19},{19,3},{4,20},{20... | collective-permute-start | bytes 1990664 | tf_op jit(solution)/shard_map/ppermute | solution.py:137
Sparse Core Ops, SparseCore 0:
  58.0 55.3 all-gather.2

commit v4 on v3

--- a/solution.py
+++ b/solution.py
@@ -68,6 +68,13 @@
     low_core, low_rep, low_z1 = c == 0, z2 == 0, z1 == 0
 
 
+    bo = basis_out.astype(bf16)
+    low = jnp.concatenate([bo[:, i * quarter : i * quarter + half] for i in range(4)], axis=1)
+    high = jnp.concatenate([bo[:, i * quarter + half : (i + 1) * quarter] for i in range(4)], axis=1)
+    low, high = pack(low), pack(high)
+    bo = jnp.stack([jnp.where(low_rep, low, high), jnp.where(low_rep, high, low)])
+    bo = lax.ppermute(bo, ("z1", "y"), pairs_z1y0())
+
     grad = grad_parts[0]
     parts = jnp.stack([pack(grad[:, i * quarter : (i + 1) * quarter]) for i in range(4)])
 
@@ -82,21 +89,20 @@
     other = (from_part(1, 0) + from_part(1, 1)).astype(bf16)
     grad = in_order(low_z1, mine, other, 1)
 
+    bo, grad = lax.optimization_barrier((bo, grad))
+    bo = lax.all_gather(bo, "y", axis=0)
+    bo = bo.reshape(4, 2, 2, half, 2, wide).transpose(2, 1, 4, 3, 0, 5)
+    near, far = bo.reshape(2, wide, 4 * wide)
+
     bi = basis_in.astype(bf16)
     bi = jnp.where(low_rep, bi[:half], bi[half:])
     bi = lax.ppermute(bi, ("z1", "z0", "c", "z2"), pairs_rows())
-    bi = gather(bi, RING, 8)
+    other = lax.ppermute(bi, "z0", SWAP)
+    pair = in_order(z0 == 0, bi[None], other[None], 0)
+    turn = [pair] + [lax.ppermute(pair, "x", [(i, (i - s) % 4) for i in range(4)]) for s in (1, 2, 3)]
+    turn = jnp.concatenate(turn + turn[:3], axis=0)
+    bi = lax.dynamic_slice_in_dim(turn, 2 * ((4 - x) % 4), 8, 0)
     bi = in_order(low_core, bi, lax.ppermute(bi, "c", SWAP), 1).reshape(8 * rows, cols)
-
-    bo = basis_out.astype(bf16)
-    low = jnp.concatenate([bo[:, i * quarter : i * quarter + half] for i in range(4)], axis=1)
-    high = jnp.concatenate([bo[:, i * quarter + half : (i + 1) * quarter] for i in range(4)], axis=1)
-    low, high = pack(low), pack(high)
-    bo = jnp.stack([jnp.where(low_rep, low, high), jnp.where(low_rep, high, low)])
-    bo = lax.ppermute(bo, ("z1", "y"), pairs_z1y0())
-    bo = lax.all_gather(bo, "y", axis=0)
-    bo = bo.reshape(4, 2, 2, half, 2, wide).transpose(2, 1, 4, 3, 0, 5)
-    near, far = bo.reshape(2, wide, 4 * wide)
 
     grad = gather(grad, "y", 8)
     grad = grad.reshape(8, half, 4, quarter).transpose(2, 1, 0, 3).reshape(wide, 8 * quarter)

time: 229 us -> 237 us (1.035)
  blocking collectives: 71.3 us -> 85.3 us
  waiting for transfers between devices: 43.1 us -> 32.1 us
  starting transfers between devices: 64 us -> 68.8 us
    ppermute x0 -> x4, starting transfers between devices: none -> 16.1 us  [the longest x3 9.33 us: body(): lax.ppermute(pair, 'x', [(i, (i - s) % 4) for i in range(4)])]
    all_to_all x2, blocking collectives: 25.2 us -> 35.6 us  [gather(): lax.all_to_all(jnp.broadcast_to(block[None], (count,) + block.shape), axe...]
    ppermute x1, starting transfers between devices: 11.7 us -> 4.74 us  [body(): part = (keep + lax.ppermute(give, 'c', SWAP).astype(f32)).astype(bf16)]
    ppermute x1, waiting for transfers between devices: 7.15 us -> 0.77 us  [body(): bi = lax.ppermute(bi, ('z1', 'z0', 'c', 'z2'), pairs_rows())]
    ppermute x3, starting transfers between devices: 11.4 us -> 17.7 us  [from_part(): return lax.ppermute(piece(d1, d2), PART, pairs_part(d1, d2)).astype(f32)]
    all_to_all x2 -> x1, starting transfers between devices: 12.8 us -> 6.79 us  [gather(): lax.all_to_all(jnp.broadcast_to(block[None], (count,) + block.shape), axe...]
    ppermute x3, waiting for transfers between devices: 4.33 us -> 0.01 us  [from_part(): return lax.ppermute(piece(d1, d2), PART, pairs_part(d1, d2)).astype(f32)]
    ppermute x1, starting transfers between devices: 9.32 us -> 5.36 us  [body(): other = lax.ppermute(turned, 'c', SWAP)]
  transfers between devices with their start and end apart: 13 -> 16, of which waited for: 6 -> 8; matrix products, arithmetic and copies ran while one was open for 7% -> 8% of each run, Pallas kernels for 0% -> 0%
where the time goes in v4:
time: 237 us; the launch traced here: 236 us
  blocking collectives  85.3 us (36%)
  starting transfers between devices  68.8 us (29%)
  waiting for transfers between devices  32.1 us (14%)
  local copies, waits for them, and re-layouts  22.3 us (9%)
  between operations  14 us (6%)
  other arithmetic  7.74 us (3%)
  matrix products  6.13 us (3%)
    all_to_all x3, blocking collectives, scatter_sum(): got = lax.all_to_all(blocks, axes, 0, 0, tiled=True)  49.7 us
    all_to_all x2, blocking collectives, gather(): lax.all_to_all(jnp.broadcast_to(block[None], (count,) + block.shape), axe...  35.6 us
    ppermute x3, starting transfers between devices, from_part(): return lax.ppermute(piece(d1, d2), PART, pairs_part(d1, d2)).astype(f32)  17.7 us
    all_to_all x1, waiting for transfers between devices, gather(): lax.all_to_all(jnp.broadcast_to(block[None], (count,) + block.shape), axe...  14 us
    ppermute x3, starting transfers between devices, body(): lax.ppermute(pair, 'x', [(i, (i - s) % 4) for i in range(4)])  9.33 us
    all_to_all x1, waiting for transfers between devices, scatter_sum(): got = lax.all_to_all(blocks, axes, 0, 0, tiled=True)  8.16 us
    ppermute x1, starting transfers between devices, body(): other = lax.ppermute(bi, 'z0', SWAP)  6.8 us
    all_to_all x1, starting transfers between devices, gather(): lax.all_to_all(jnp.broadcast_to(block[None], (count,) + block.shape), axe...  6.79 us
  transfers between devices with their start and end apart: 16, of which 8 were waited for; matrix products, arithmetic and copies ran while one was open for 8% of the time, Pallas kernels for 0%

profile of v4, /device:TPU:1, one launch (start us, length us, event | category | flops | bytes accessed | tf_op | source)
XLA Modules:
  0.0 236.4 jit_solution(14342871017026069523)
XLA Ops:
  8.0 11.5 %collective-permute-start.3 = (bf16[72,288]{1,0:T(8,128)(2,1)S(1)}, bf16[72,288]{1,0:T(8,128)(2,1)S(1)}, u32[]{:S(2)}, u32[]{:S(2)}) collective-permute-start(bf16[72,288]{1,0:T(8,128)(2,1)S(1)} %get-tuple-element.14), channel_id=1, source_target_pairs={{0,65},{1,64},{64,1},{65,0},{2,67},{3,66},{66,3},{67,2},{4,69},{5,... | collective-permute-start | bytes 124424 | tf_op jit(solution)/shard_map/ppermute | solution.py:86
  19.5 2.2 collective-permute-start.2
  21.7 5.1 %collective-permute-start.4 = (bf16[72,576]{1,0:T(8,128)(2,1)S(1)}, bf16[72,576]{1,0:T(8,128)(2,1)S(1)}, u32[]{:S(2)}, u32[]{:S(2)}) collective-permute-start(bf16[72,576]{1,0:T(8,128)(2,1)S(1)} %slice_select_fusion), channel_id=1, source_target_pairs={{0,0},{1,16},{16,64},{17,80},{32,1},{33,17},{48,65},{49,81},{64,32... | collective-permute-start | bytes 248840 | tf_op jit(solution)/shard_map/ppermute | solution.py:99
  28.1 4.1 %collective-permute-start.1 = (bf16[72,288]{1,0:T(8,128)(2,1)S(1)}, bf16[72,288]{1,0:T(8,128)(2,1)S(1)}, u32[]{:S(2)}, u32[]{:S(2)}) collective-permute-start(bf16[72,288]{1,0:T(8,128)(2,1)S(1)} %get-tuple-element.13), channel_id=1, source_target_pairs={{0,1},{1,0},{64,65},{65,64},{2,3},{3,2},{66,67},{67,66},{4,5},{5,4... | collective-permute-start | bytes 124424 | tf_op jit(solution)/shard_map/ppermute | solution.py:86
  33.0 6.8 %collective-permute-start.5 = (bf16[72,576]{1,0:T(8,128)(2,1)S(1)}, bf16[72,576]{1,0:T(8,128)(2,1)S(1)}, u32[]{:S(2)}, u32[]{:S(2)}) collective-permute-start(bf16[72,576]{1,0:T(8,128)(2,1)S(1)} %collective-permute-done.4), channel_id=1, source_target_pairs={{0,32},{32,0},{1,33},{33,1},{2,34},{34,2},{3,35},{35,3},{4,36},{36... | collective-permute-start | bytes 248840 | tf_op jit(solution)/shard_map/ppermute | solution.py:100
  39.9 2.7 %collective-permute-done.5 = bf16[72,576]{1,0:T(8,128)(2,1)S(1)} collective-permute-done((bf16[72,576]{1,0:T(8,128)(2,1)S(1)}, bf16[72,576]{1,0:T(8,128)(2,1)S(1)}, u32[]{:S(2)}, u32[]{:S(2)}) %collective-permute-start.5) | collective-permute-done | bytes 82976 | tf_op jit(solution)/shard_map/ppermute | solution.py:100
  42.7 4.4 %collective-permute-start.6 = (bf16[2,72,576]{2,1,0:T(8,128)(2,1)S(1)}, bf16[2,72,576]{2,1,0:T(8,128)(2,1)S(1)}, u32[]{:S(2)}, u32[]{:S(2)}) collective-permute-start(bf16[2,72,576]{2,1,0:T(8,128)(2,1)S(1)} %get-tuple-element.10), channel_id=1, source_target_pairs={{0,384},{128,0},{256,128},{384,256},{1,385},{129,1},{257,129},{385... | collective-permute-start | bytes 497672 | tf_op jit(solution)/shard_map/ppermute | solution.py:102
  47.1 2.4 %collective-permute-start.7 = (bf16[2,72,576]{2,1,0:T(8,128)(2,1)S(1)}, bf16[2,72,576]{2,1,0:T(8,128)(2,1)S(1)}, u32[]{:S(2)}, u32[]{:S(2)}) collective-permute-start(bf16[2,72,576]{2,1,0:T(8,128)(2,1)S(1)} %get-tuple-element.10), channel_id=1, source_target_pairs={{0,256},{128,384},{256,0},{384,128},{1,257},{129,385},{257,1},{385... | collective-permute-start | bytes 497672 | tf_op jit(solution)/shard_map/ppermute | solution.py:102
  49.6 2.5 %collective-permute-start.8 = (bf16[2,72,576]{2,1,0:T(8,128)(2,1)S(1)}, bf16[2,72,576]{2,1,0:T(8,128)(2,1)S(1)}, u32[]{:S(2)}, u32[]{:S(2)}) collective-permute-start(bf16[2,72,576]{2,1,0:T(8,128)(2,1)S(1)} %get-tuple-element.10), channel_id=1, source_target_pairs={{0,128},{128,256},{256,384},{384,0},{1,129},{129,257},{257,385},{3... | collective-permute-start | bytes 497672 | tf_op jit(solution)/shard_map/ppermute | solution.py:102
  53.1 6.8 %all-to-all-start = ((bf16[8,72,576]{2,1,0:T(8,128)(2,1)}), bf16[8,72,576]{2,1,0:T(8,128)(2,1)S(1)}, u32[]{:S(2)}, u32[]{:S(2)}) async-start(bf16[8,72,576]{2,1,0:T(8,128)(2,1)} %broadcast_in_dim.14), calls=%async_computation | async-start | bytes 1474560 | tf_op jit(solution)/shard_map/all_to_all | solution.py:15
  60.7 3.0 %collective-permute-start.9 = (bf16[8,72,576]{2,1,0:T(8,128)(2,1)S(1)}, bf16[8,72,576]{2,1,0:T(8,128)(2,1)S(1)}, u32[]{:S(2)}, u32[]{:S(2)}) collective-permute-start(bf16[8,72,576]{2,1,0:T(8,128)(2,1)S(1)} %constant_dynamic-slice_fusion), channel_id=1, source_target_pairs={{0,16},{16,0},{1,17},{17,1},{2,18},{18,2},{3,19},{19,3},{4,20},{20... | collective-permute-start | bytes 1990664 | tf_op jit(solution)/shard_map/ppermute | solution.py:105
  63.8 1.8 collective-permute-done.9
  65.6 1.8 maximum_select_fusion
  67.4 14.0 %all-to-all-done = bf16[8,72,576]{2,1,0:T(8,128)(2,1)S(1)} async-done(((bf16[8,72,576]{2,1,0:T(8,128)(2,1)}), bf16[8,72,576]{2,1,0:T(8,128)(2,1)S(1)}, u32[]{:S(2)}, u32[]{:S(2)}) %all-to-all-start) | async-done | bytes 663584 | tf_op jit(solution)/shard_map/all_to_all | solution.py:15
  82.8 2.1 reshape.215
  84.9 1.8 convolution_convert_fusion.2
  86.7 12.5 %all_to_all.35 = bf16[4,72,576]{2,1,0:T(8,128)(2,1)S(1)} all-to-all(bf16[4,72,576]{2,1,0:T(8,128)(2,1)S(1)} %bitcast.70), channel_id=1, replica_groups=mesh['x'=4,'z1'=2,'z0'=2,'c'=2,'y'=8,'z2'=2] {'z1','z2'}, dimensions={0} | all-to-all | bytes 663552 | tf_op jit(solution)/shard_map/all_to_all | solution.py:21
  99.3 17.6 %all_to_all.36 = bf16[8,72,576]{2,1,0:T(8,128)(2,1)} all-to-all(bf16[8,72,576]{2,1,0:T(8,128)(2,1)S(1)} %broadcast_in_dim.17), channel_id=1, replica_groups=mesh['x'=4,'z1'=2,'z0'=2,'c'=2,'y'=8,'z2'=2] {'x','z0'}, dimensions={0} | all-to-all | bytes 1327104 | tf_op jit(solution)/shard_map/all_to_all | solution.py:15
  117.0 5.4 %collective-permute-start.10 = (bf16[8,72,576]{2,1,0:T(8,128)(2,1)}, bf16[8,72,576]{2,1,0:T(8,128)(2,1)S(1)}, u32[]{:S(2)}, u32[]{:S(2)}) collective-permute-start(bf16[8,72,576]{2,1,0:T(8,128)(2,1)} %all_to_all.36), channel_id=1, source_target_pairs={{0,16},{16,0},{1,17},{17,1},{2,18},{18,2},{3,19},{19,3},{4,20},{20... | collective-permute-start | bytes 1990664 | tf_op jit(solution)/shard_map/ppermute | solution.py:112
  122.4 4.1 %reshape.213 = bf16[4,2,2,72,2,288]{5,4,3,2,1,0:T(2,128)(2,1)S(1)} reshape(bf16[16,72,576]{2,1,0:T(8,128)(2,1)} %all-gather.3.cloned.1.call-done) | data formatting | bytes 2654208 | tf_op jit(solution)/shard_map/reshape | solution.py:94
  129.1 2.0 maximum_select_fusion.1
  132.5 3.8 %all-to-all-start.3 = ((bf16[4,72,576]{2,1,0:T(8,128)(2,1)}), bf16[4,72,576]{2,1,0:T(8,128)(2,1)S(1)}, u32[]{:S(2)}, u32[]{:S(2)}) async-start(bf16[4,72,576]{2,1,0:T(8,128)(2,1)} %bitcast.22), calls=%async_computation.3 | async-start | bytes 737280 | tf_op jit(solution)/shard_map/all_to_all | solution.py:21
  137.9 8.2 %all-to-all-done.3 = bf16[4,72,576]{2,1,0:T(8,128)(2,1)S(1)} async-done(((bf16[4,72,576]{2,1,0:T(8,128)(2,1)}), bf16[4,72,576]{2,1,0:T(8,128)(2,1)S(1)}, u32[]{:S(2)}, u32[]{:S(2)}) %all-to-all-start.3) | async-done | bytes 331808 | tf_op jit(solution)/shard_map/all_to_all | solution.py:21
  146.3 17.9 %all_to_all.37 = bf16[4,72,576]{2,1,0:T(8,128)(2,1)S(1)} all-to-all(bf16[4,72,576]{2,1,0:T(8,128)(2,1)S(1)} %broadcast_in_dim.38), channel_id=1, replica_groups=mesh['x'=4,'z1'=2,'z0'=2,'c'=2,'y'=8,'z2'=2] {'z1','z2'}, dimensions={0} | all-to-all | bytes 663552 | tf_op jit(solution)/shard_map/all_to_all | solution.py:15
  165.8 2.7 %reshape.219 = bf16[4,72,8,144]{3,2,1,0:T(8,128)(2,1)S(1)} reshape(bf16[288,1152]{1,0:T(8,128)(2,1)} %convolution_convert_fusion) | data formatting | bytes 1327104 | tf_op jit(solution)/shard_map/reshape | solution.py:124
  170.2 21.8 %all_to_all.38 = bf16[8,72,576]{2,1,0:T(8,128)(2,1)S(1)} all-to-all(bf16[8,72,576]{2,1,0:T(8,128)(2,1)S(1)} %reshape.220), channel_id=1, replica_groups=mesh['x'=4,'z1'=2,'z0'=2,'c'=2,'y'=8,'z2'=2] {'y'}, dimensions={0} | all-to-all | bytes 1327104 | tf_op jit(solution)/shard_map/all_to_all | solution.py:21
  192.1 5.4 %collective-permute-start.11 = (bf16[72,576]{1,0:T(8,128)(2,1)S(1)}, bf16[72,576]{1,0:T(8,128)(2,1)S(1)}, u32[]{:S(2)}, u32[]{:S(2)}) collective-permute-start(bf16[72,576]{1,0:T(8,128)(2,1)S(1)} %reduce_sum.47), channel_id=1, source_target_pairs={{0,64},{64,0},{1,65},{65,1},{2,66},{66,2},{3,67},{67,3},{4,68},{68... | collective-permute-start | bytes 248840 | tf_op jit(solution)/shard_map/ppermute | solution.py:126
  198.0 2.3 collective-permute-done.11
  203.6 2.7 %copy.20 = f32[1152,576]{1,0:T(8,128)S(1)} copy(f32[1152,576]{0,1:T(8,128)} %pad_maximum_fusion) | data formatting | bytes 5308416 | tf_op jit(solution)/shard_map/concatenate | solution.py:139
  206.4 4.7 %collective-permute-start.12 = (bf16[8,72,576]{2,1,0:T(8,128)(2,1)S(1)}, bf16[8,72,576]{2,1,0:T(8,128)(2,1)S(1)}, u32[]{:S(2)}, u32[]{:S(2)}) collective-permute-start(bf16[8,72,576]{2,1,0:T(8,128)(2,1)S(1)} %fusion.1), channel_id=1, source_target_pairs={{0,16},{16,0},{1,17},{17,1},{2,18},{18,2},{3,19},{19,3},{4,20},{20... | collective-permute-start | bytes 1990664 | tf_op jit(solution)/shard_map/ppermute | solution.py:143
  211.2 1.8 collective-permute-done.12
  213.2 15.5 %all_to_all.39 = bf16[8,72,576]{2,1,0:T(8,128)(2,1)S(1)} all-to-all(bf16[8,72,576]{2,1,0:T(8,128)(2,1)S(1)} %fusion), channel_id=1, replica_groups=mesh['x'=4,'z1'=2,'z0'=2,'c'=2,'y'=8,'z2'=2] {'x','z0'}, dimensions={0} | all-to-all | bytes 1327104 | tf_op jit(solution)/shard_map/all_to_all | solution.py:21
  (82 shorter events, 21.0 us)
Async XLA Ops:
  6.5 15.1 %copy-start.4 = (f32[144,576]{1,0:T(8,128)S(1)}, f32[144,576]{1,0:T(8,128)}, u32[]{:S(2)}) copy-start(f32[144,576]{1,0:T(8,128)} %param.6) | copy-start | bytes 995332
  6.5 20.4 %copy-start.5 = (f32[144,576]{1,0:T(8,128)S(1)}, f32[144,576]{1,0:T(8,128)}, u32[]{:S(2)}) copy-start(f32[144,576]{1,0:T(8,128)} %param.7) | copy-start | bytes 995332
  8.0 31.8 %collective-permute-start.3 = (bf16[72,288]{1,0:T(8,128)(2,1)S(1)}, bf16[72,288]{1,0:T(8,128)(2,1)S(1)}, u32[]{:S(2)}, u32[]{:S(2)}) collective-permute-start(bf16[72,288]{1,0:T(8,128)(2,1)S(1)} %get-tuple-element.14), channel_id=1, source_target_pairs={{0,65},{1,64},{64,1},{65,0},{2,67},{3,66},{66,3},{67,2},{4,69},{5,... | collective-permute-start | bytes 124424 | tf_op jit(solution)/shard_map/ppermute | solution.py:86
  19.5 20.3 %collective-permute-start.2 = (bf16[72,288]{1,0:T(8,128)(2,1)S(1)}, bf16[72,288]{1,0:T(8,128)(2,1)S(1)}, u32[]{:S(2)}, u32[]{:S(2)}) collective-permute-start(bf16[72,288]{1,0:T(8,128)(2,1)S(1)} %get-tuple-element.15), channel_id=1, source_target_pairs={{0,64},{1,65},{64,0},{65,1},{2,66},{3,67},{66,2},{67,3},{4,68},{5,... | collective-permute-start | bytes 124424 | tf_op jit(solution)/shard_map/ppermute | solution.py:86
  21.7 11.3 %collective-permute-start.4 = (bf16[72,576]{1,0:T(8,128)(2,1)S(1)}, bf16[72,576]{1,0:T(8,128)(2,1)S(1)}, u32[]{:S(2)}, u32[]{:S(2)}) collective-permute-start(bf16[72,576]{1,0:T(8,128)(2,1)S(1)} %slice_select_fusion), channel_id=1, source_target_pairs={{0,0},{1,16},{16,64},{17,80},{32,1},{33,17},{48,65},{49,81},{64,32... | collective-permute-start | bytes 248840 | tf_op jit(solution)/shard_map/ppermute | solution.py:99
  27.5 24.7 %collective-permute-start = (bf16[2,72,576]{2,1,0:T(8,128)(2,1)S(1)}, bf16[2,72,576]{2,1,0:T(8,128)(2,1)S(1)}, u32[]{:S(2)}, u32[]{:S(2)}) collective-permute-start(bf16[2,72,576]{2,1,0:T(8,128)(2,1)S(1)} %pad_maximum_fusion.2), channel_id=1, source_target_pairs={{0,0},{2,64},{4,4},{6,68},{8,8},{10,72},{12,12},{14,76},{64,2},{66... | collective-permute-start | bytes 497672 | tf_op jit(solution)/shard_map/ppermute | solution.py:76
  28.1 18.9 %collective-permute-start.1 = (bf16[72,288]{1,0:T(8,128)(2,1)S(1)}, bf16[72,288]{1,0:T(8,128)(2,1)S(1)}, u32[]{:S(2)}, u32[]{:S(2)}) collective-permute-start(bf16[72,288]{1,0:T(8,128)(2,1)S(1)} %get-tuple-element.13), channel_id=1, source_target_pairs={{0,1},{1,0},{64,65},{65,64},{2,3},{3,2},{66,67},{67,66},{4,5},{5,4... | collective-permute-start | bytes 124424 | tf_op jit(solution)/shard_map/ppermute | solution.py:86
  33.0 9.6 %collective-permute-start.5 = (bf16[72,576]{1,0:T(8,128)(2,1)S(1)}, bf16[72,576]{1,0:T(8,128)(2,1)S(1)}, u32[]{:S(2)}, u32[]{:S(2)}) collective-permute-start(bf16[72,576]{1,0:T(8,128)(2,1)S(1)} %collective-permute-done.4), channel_id=1, source_target_pairs={{0,32},{32,0},{1,33},{33,1},{2,34},{34,2},{3,35},{35,3},{4,36},{36... | collective-permute-start | bytes 248840 | tf_op jit(solution)/shard_map/ppermute | solution.py:100
  42.7 17.3 %collective-permute-start.6 = (bf16[2,72,576]{2,1,0:T(8,128)(2,1)S(1)}, bf16[2,72,576]{2,1,0:T(8,128)(2,1)S(1)}, u32[]{:S(2)}, u32[]{:S(2)}) collective-permute-start(bf16[2,72,576]{2,1,0:T(8,128)(2,1)S(1)} %get-tuple-element.10), channel_id=1, source_target_pairs={{0,384},{128,0},{256,128},{384,256},{1,385},{129,1},{257,129},{385... | collective-permute-start | bytes 497672 | tf_op jit(solution)/shard_map/ppermute | solution.py:102
  47.1 12.9 %collective-permute-start.7 = (bf16[2,72,576]{2,1,0:T(8,128)(2,1)S(1)}, bf16[2,72,576]{2,1,0:T(8,128)(2,1)S(1)}, u32[]{:S(2)}, u32[]{:S(2)}) collective-permute-start(bf16[2,72,576]{2,1,0:T(8,128)(2,1)S(1)} %get-tuple-element.10), channel_id=1, source_target_pairs={{0,256},{128,384},{256,0},{384,128},{1,257},{129,385},{257,1},{385... | collective-permute-start | bytes 497672 | tf_op jit(solution)/shard_map/ppermute | solution.py:102
  49.6 10.9 %collective-permute-start.8 = (bf16[2,72,576]{2,1,0:T(8,128)(2,1)S(1)}, bf16[2,72,576]{2,1,0:T(8,128)(2,1)S(1)}, u32[]{:S(2)}, u32[]{:S(2)}) collective-permute-start(bf16[2,72,576]{2,1,0:T(8,128)(2,1)S(1)} %get-tuple-element.10), channel_id=1, source_target_pairs={{0,128},{128,256},{256,384},{384,0},{1,129},{129,257},{257,385},{3... | collective-permute-start | bytes 497672 | tf_op jit(solution)/shard_map/ppermute | solution.py:102
  52.2 7.9 %copy-start.6 = (bf16[2,72,576]{2,1,0:T(8,128)(2,1)}, bf16[2,72,576]{2,1,0:T(8,128)(2,1)S(1)}, u32[]{:S(2)}) copy-start(bf16[2,72,576]{2,1,0:T(8,128)(2,1)S(1)} %collective-permute-done) | copy-start | bytes 497668
  53.1 28.2 %all-to-all-start = ((bf16[8,72,576]{2,1,0:T(8,128)(2,1)}), bf16[8,72,576]{2,1,0:T(8,128)(2,1)S(1)}, u32[]{:S(2)}, u32[]{:S(2)}) async-start(bf16[8,72,576]{2,1,0:T(8,128)(2,1)} %broadcast_in_dim.14), calls=%async_computation | async-start | bytes 1474560 | tf_op jit(solution)/shard_map/all_to_all | solution.py:15
  59.9 62.4 %all-gather.3.cloned.1.call-start = ((), (), s32[]{:S(2)}) async-start(), calls=%async_computation.7 | async-start | bytes 1658880 | tf_op jit(solution)/shard_map/all_gather | solution.py:93
  60.7 4.9 %collective-permute-start.9 = (bf16[8,72,576]{2,1,0:T(8,128)(2,1)S(1)}, bf16[8,72,576]{2,1,0:T(8,128)(2,1)S(1)}, u32[]{:S(2)}, u32[]{:S(2)}) collective-permute-start(bf16[8,72,576]{2,1,0:T(8,128)(2,1)S(1)} %constant_dynamic-slice_fusion), channel_id=1, source_target_pairs={{0,16},{16,0},{1,17},{17,1},{2,18},{18,2},{3,19},{19,3},{4,20},{20... | collective-permute-start | bytes 1990664 | tf_op jit(solution)/shard_map/ppermute | solution.py:105
  82.8 2.1 copy-start
  117.0 12.1 %collective-permute-start.10 = (bf16[8,72,576]{2,1,0:T(8,128)(2,1)}, bf16[8,72,576]{2,1,0:T(8,128)(2,1)S(1)}, u32[]{:S(2)}, u32[]{:S(2)}) collective-permute-start(bf16[8,72,576]{2,1,0:T(8,128)(2,1)} %all_to_all.36), channel_id=1, source_target_pairs={{0,16},{16,0},{1,17},{17,1},{2,18},{18,2},{3,19},{19,3},{4,20},{20... | collective-permute-start | bytes 1990664 | tf_op jit(solution)/shard_map/ppermute | solution.py:112
  129.1 2.0 copy-start.2
  132.5 31.7 %copy-start.1 = (bf16[8,144,576]{2,1,0:T(8,128)(2,1)S(1)}, bf16[8,144,576]{2,1,0:T(8,128)(2,1)}, u32[]{:S(2)}) copy-start(bf16[8,144,576]{2,1,0:T(8,128)(2,1)} %maximum_select_fusion) | copy-start | bytes 3981316
  132.5 13.5 %all-to-all-start.3 = ((bf16[4,72,576]{2,1,0:T(8,128)(2,1)}), bf16[4,72,576]{2,1,0:T(8,128)(2,1)S(1)}, u32[]{:S(2)}, u32[]{:S(2)}) async-start(bf16[4,72,576]{2,1,0:T(8,128)(2,1)} %bitcast.22), calls=%async_computation.3 | async-start | bytes 737280 | tf_op jit(solution)/shard_map/all_to_all | solution.py:21
  192.0 8.6 %copy-start.3 = (bf16[288,1152]{1,0:T(8,128)(2,1)S(1)}, bf16[288,1152]{1,0:T(8,128)(2,1)}, u32[]{:S(2)}) copy-start(bf16[288,1152]{1,0:T(8,128)(2,1)} %copy-done.2) | copy-start | bytes 1990660
  192.1 8.3 %collective-permute-start.11 = (bf16[72,576]{1,0:T(8,128)(2,1)S(1)}, bf16[72,576]{1,0:T(8,128)(2,1)S(1)}, u32[]{:S(2)}, u32[]{:S(2)}) collective-permute-start(bf16[72,576]{1,0:T(8,128)(2,1)S(1)} %reduce_sum.47), channel_id=1, source_target_pairs={{0,64},{64,0},{1,65},{65,1},{2,66},{66,2},{3,67},{67,3},{4,68},{68... | collective-permute-start | bytes 248840 | tf_op jit(solution)/shard_map/ppermute | solution.py:126
  206.4 6.6 %collective-permute-start.12 = (bf16[8,72,576]{2,1,0:T(8,128)(2,1)S(1)}, bf16[8,72,576]{2,1,0:T(8,128)(2,1)S(1)}, u32[]{:S(2)}, u32[]{:S(2)}) collective-permute-start(bf16[8,72,576]{2,1,0:T(8,128)(2,1)S(1)} %fusion.1), channel_id=1, source_target_pairs={{0,16},{16,0},{1,17},{17,1},{2,18},{18,2},{3,19},{19,3},{4,20},{20... | collective-permute-start | bytes 1990664 | tf_op jit(solution)/shard_map/ppermute | solution.py:143
Sparse Core Ops, SparseCore 0:
  63.9 36.8 all-gather.2

commit v5 on v4

--- a/solution.py
+++ b/solution.py
@@ -89,25 +89,23 @@
     other = (from_part(1, 0) + from_part(1, 1)).astype(bf16)
     grad = in_order(low_z1, mine, other, 1)
 
-    bo, grad = lax.optimization_barrier((bo, grad))
-    bo = lax.all_gather(bo, "y", axis=0)
-    bo = bo.reshape(4, 2, 2, half, 2, wide).transpose(2, 1, 4, 3, 0, 5)
-    near, far = bo.reshape(2, wide, 4 * wide)
-
     bi = basis_in.astype(bf16)
     bi = jnp.where(low_rep, bi[:half], bi[half:])
     bi = lax.ppermute(bi, ("z1", "z0", "c", "z2"), pairs_rows())
-    other = lax.ppermute(bi, "z0", SWAP)
-    pair = in_order(z0 == 0, bi[None], other[None], 0)
-    turn = [pair] + [lax.ppermute(pair, "x", [(i, (i - s) % 4) for i in range(4)]) for s in (1, 2, 3)]
-    turn = jnp.concatenate(turn + turn[:3], axis=0)
-    bi = lax.dynamic_slice_in_dim(turn, 2 * ((4 - x) % 4), 8, 0)
+
+    bo, bi, grad = lax.optimization_barrier((bo, bi, grad))
+    bi = gather(bi, RING, 8)
     bi = in_order(low_core, bi, lax.ppermute(bi, "c", SWAP), 1).reshape(8 * rows, cols)
+    bo = lax.all_gather(bo, "y", axis=0)
 
     grad = gather(grad, "y", 8)
     grad = grad.reshape(8, half, 4, quarter).transpose(2, 1, 0, 3).reshape(wide, 8 * quarter)
     part = dot(grad, bi, 1, 0).astype(bf16).reshape(4, half, cols)
     turned = scatter_sum(part, PART).astype(bf16)
+
+    bo, turned = lax.optimization_barrier((bo, turned))
+    bo = bo.reshape(4, 2, 2, half, 2, wide).transpose(2, 1, 4, 3, 0, 5)
+    near, far = bo.reshape(2, wide, 4 * wide)
     turned = gather(turned, RING, 8)
     other = lax.ppermute(turned, "c", SWAP)
     turned = in_order(low_core, turned[:, None], other[:, None], 1).reshape(16 * half, cols)
@@ -136,11 +134,13 @@
         axis=0,
     )
 
-    part = jnp.concatenate([dot(near, back, 0, 0), dot(far, back, 0, 0)], axis=1)
+    part = jnp.concatenate(
+        [dot(near, back, 0, 0).astype(bf16), dot(far, back, 0, 0).astype(bf16)], axis=1
+    )
     part = part.reshape(8, 2, half, cols)
     keep = jnp.where(low_core, part[:, 0], part[:, 1])
-    give = jnp.where(low_core, part[:, 1], part[:, 0]).astype(bf16)
-    part = (keep + lax.ppermute(give, "c", SWAP).astype(f32)).astype(bf16)
+    give = jnp.where(low_core, part[:, 1], part[:, 0])
+    part = (keep.astype(f32) + lax.ppermute(give, "c", SWAP).astype(f32)).astype(bf16)
     out = scatter_sum(part, RING).astype(bf16)
     return in_order(low_rep, out[:, :wide], out[:, wide:], 0)
 

time: 237 us -> 243 us (1.025)
  waiting for transfers between devices: 32.1 us -> 51.2 us
  starting transfers between devices: 68.8 us -> 61.6 us
  local copies, waits for them, and re-layouts: 22.3 us -> 17.3 us
    all_to_all x1 -> x2, waiting for transfers between devices: 14 us -> 33.8 us  [gather(): lax.all_to_all(jnp.broadcast_to(block[None], (count,) + block.shape), axe...]
    ppermute x5 -> x1, starting transfers between devices: 20.9 us -> 3.62 us  [body(): lax.ppermute(give, 'c', SWAP).astype(f32)]
    ppermute x3, waiting for transfers between devices: 0.01 us -> 4.95 us  [from_part(): return lax.ppermute(piece(d1, d2), PART, pairs_part(d1, d2)).astype(f32)]
    all_to_all x1 -> x2, starting transfers between devices: 6.79 us -> 11 us  [gather(): lax.all_to_all(jnp.broadcast_to(block[None], (count,) + block.shape), axe...]
    reshape x2 -> x1, local copies, waits for them, and re-layouts: 5.49 us -> 1.7 us  [body(): bo = bo.reshape(4, 2, 2, half, 2, wide).transpose(2, 1, 4, 3, 0, 5)]
    ppermute x5 -> x1, waiting for transfers between devices: 5.04 us -> 1.82 us  [body(): lax.ppermute(give, 'c', SWAP).astype(f32)]
    ppermute x1, starting transfers between devices: 5.36 us -> 7.98 us  [body(): other = lax.ppermute(back, 'z1', SWAP)]
  transfers between devices with their start and end apart: 16 -> 13, of which waited for: 8 -> 6; matrix products, arithmetic and copies ran while one was open for 8% -> 6% of each run, Pallas kernels for 0% -> 0%
where the time goes in v5:
time: 243 us; the launch traced here: 242 us
  blocking collectives  86 us (35%)
  starting transfers between devices  61.6 us (25%)
  waiting for transfers between devices  51.2 us (21%)
  local copies, waits for them, and re-layouts  17.3 us (7%)
  between operations  14 us (6%)
  other arithmetic  7.74 us (3%)
  matrix products  4.23 us (2%)
    all_to_all x3, blocking collectives, scatter_sum(): got = lax.all_to_all(blocks, axes, 0, 0, tiled=True)  51.8 us
    all_to_all x2, blocking collectives, gather(): lax.all_to_all(jnp.broadcast_to(block[None], (count,) + block.shape), axe...  34.2 us
    all_to_all x2, waiting for transfers between devices, gather(): lax.all_to_all(jnp.broadcast_to(block[None], (count,) + block.shape), axe...  33.8 us
    ppermute x3, starting transfers between devices, from_part(): return lax.ppermute(piece(d1, d2), PART, pairs_part(d1, d2)).astype(f32)  19.7 us
    all_to_all x2, starting transfers between devices, gather(): lax.all_to_all(jnp.broadcast_to(block[None], (count,) + block.shape), axe...  11 us
    all_to_all x1, waiting for transfers between devices, scatter_sum(): got = lax.all_to_all(blocks, axes, 0, 0, tiled=True)  8.02 us
    ppermute x1, starting transfers between devices, body(): other = lax.ppermute(back, 'z1', SWAP)  7.98 us
    ppermute x1, starting transfers between devices, body(): bi = lax.ppermute(bi, ('z1', 'z0', 'c', 'z2'), pairs_rows())  5.66 us
  transfers between devices with their start and end apart: 13, of which 6 were waited for; matrix products, arithmetic and copies ran while one was open for 6% of the time, Pallas kernels for 0%

profile of v5, /device:TPU:1, one launch (start us, length us, event | category | flops | bytes accessed | tf_op | source)
XLA Modules:
  0.0 242.1 jit_solution(14970667301721474982)
XLA Ops:
  6.5 1.0 convert_element_type.70
  9.3 14.0 %collective-permute-start.4 = (bf16[72,288]{1,0:T(8,128)(2,1)S(1)}, bf16[72,288]{1,0:T(8,128)(2,1)S(1)}, u32[]{:S(2)}, u32[]{:S(2)}) collective-permute-start(bf16[72,288]{1,0:T(8,128)(2,1)S(1)} %get-tuple-element.18), channel_id=1, source_target_pairs={{0,65},{1,64},{64,1},{65,0},{2,67},{3,66},{66,3},{67,2},{4,69},{5,... | collective-permute-start | bytes 124424 | tf_op jit(solution)/shard_map/ppermute | solution.py:86
  23.3 1.9 collective-permute-start.3
  25.3 5.7 %collective-permute-start.1 = (bf16[72,576]{1,0:T(8,128)(2,1)S(1)}, bf16[72,576]{1,0:T(8,128)(2,1)S(1)}, u32[]{:S(2)}, u32[]{:S(2)}) collective-permute-start(bf16[72,576]{1,0:T(8,128)(2,1)S(1)} %slice_select_fusion), channel_id=1, source_target_pairs={{0,0},{1,16},{16,64},{17,80},{32,1},{33,17},{48,65},{49,81},{64,32... | collective-permute-start | bytes 248840 | tf_op jit(solution)/shard_map/ppermute | solution.py:94
  31.0 3.8 %collective-permute-start.2 = (bf16[72,288]{1,0:T(8,128)(2,1)S(1)}, bf16[72,288]{1,0:T(8,128)(2,1)S(1)}, u32[]{:S(2)}, u32[]{:S(2)}) collective-permute-start(bf16[72,288]{1,0:T(8,128)(2,1)S(1)} %get-tuple-element.17), channel_id=1, source_target_pairs={{0,1},{1,0},{64,65},{65,64},{2,3},{3,2},{66,67},{67,66},{4,5},{5,4... | collective-permute-start | bytes 124424 | tf_op jit(solution)/shard_map/ppermute | solution.py:86
  34.8 4.9 %collective-permute-done.2 = bf16[72,288]{1,0:T(8,128)(2,1)S(1)} collective-permute-done((bf16[72,288]{1,0:T(8,128)(2,1)S(1)}, bf16[72,288]{1,0:T(8,128)(2,1)S(1)}, u32[]{:S(2)}, u32[]{:S(2)}) %collective-permute-start.2) | collective-permute-done | bytes 41504 | tf_op jit(solution)/shard_map/ppermute | solution.py:86
  40.9 4.0 %all-to-all-start.1 = ((bf16[8,72,576]{2,1,0:T(8,128)(2,1)}), bf16[8,72,576]{2,1,0:T(8,128)(2,1)S(1)}, u32[]{:S(2)}, u32[]{:S(2)}) async-start(bf16[8,72,576]{2,1,0:T(8,128)(2,1)} %broadcast_in_dim.13), calls=%async_computation.1 | async-start | bytes 1474560 | tf_op jit(solution)/shard_map/all_to_all | solution.py:15
  45.6 10.3 %all-to-all-done.1 = bf16[8,72,576]{2,1,0:T(8,128)(2,1)S(1)} async-done(((bf16[8,72,576]{2,1,0:T(8,128)(2,1)}), bf16[8,72,576]{2,1,0:T(8,128)(2,1)S(1)}, u32[]{:S(2)}, u32[]{:S(2)}) %all-to-all-start.1) | async-done | bytes 663584 | tf_op jit(solution)/shard_map/all_to_all | solution.py:15
  56.8 7.0 %all-to-all-start = ((bf16[8,72,576]{2,1,0:T(8,128)(2,1)}), bf16[8,72,576]{2,1,0:T(8,128)(2,1)S(1)}, u32[]{:S(2)}, u32[]{:S(2)}) async-start(bf16[8,72,576]{2,1,0:T(8,128)(2,1)} %broadcast_in_dim.12), calls=%async_computation | async-start | bytes 1474560 | tf_op jit(solution)/shard_map/all_to_all | solution.py:15
  63.8 4.4 %collective-permute-start.5 = (bf16[8,72,576]{2,1,0:T(8,128)(2,1)S(1)}, bf16[8,72,576]{2,1,0:T(8,128)(2,1)}, u32[]{:S(2)}, u32[]{:S(2)}) collective-permute-start(bf16[8,72,576]{2,1,0:T(8,128)(2,1)S(1)} %all-to-all-done.1), channel_id=1, source_target_pairs={{0,16},{16,0},{1,17},{17,1},{2,18},{18,2},{3,19},{19,3},{4,20},{20... | collective-permute-start | bytes 1990664 | tf_op jit(solution)/shard_map/ppermute | solution.py:98
  68.3 23.5 %all-to-all-done = bf16[8,72,576]{2,1,0:T(8,128)(2,1)S(1)} async-done(((bf16[8,72,576]{2,1,0:T(8,128)(2,1)}), bf16[8,72,576]{2,1,0:T(8,128)(2,1)S(1)}, u32[]{:S(2)}, u32[]{:S(2)}) %all-to-all-start) | async-done | bytes 663584 | tf_op jit(solution)/shard_map/all_to_all | solution.py:15
  93.3 1.2 reshape.216
  94.5 1.9 maximum_select_fusion
  97.5 14.2 %all_to_all.40 = bf16[4,72,576]{2,1,0:T(8,128)(2,1)S(1)} all-to-all(bf16[4,72,576]{2,1,0:T(8,128)(2,1)S(1)} %bitcast.68), channel_id=1, replica_groups=mesh['x'=4,'z1'=2,'z0'=2,'c'=2,'y'=8,'z2'=2] {'z1','z2'}, dimensions={0} | all-to-all | bytes 663552 | tf_op jit(solution)/shard_map/all_to_all | solution.py:21
  111.9 17.1 %all_to_all.41 = bf16[8,72,576]{2,1,0:T(8,128)(2,1)} all-to-all(bf16[8,72,576]{2,1,0:T(8,128)(2,1)S(1)} %broadcast_in_dim.14), channel_id=1, replica_groups=mesh['x'=4,'z1'=2,'z0'=2,'c'=2,'y'=8,'z2'=2] {'x','z0'}, dimensions={0} | all-to-all | bytes 1327104 | tf_op jit(solution)/shard_map/all_to_all | solution.py:15
  128.9 4.9 %collective-permute-start.6 = (bf16[8,72,576]{2,1,0:T(8,128)(2,1)}, bf16[8,72,576]{2,1,0:T(8,128)(2,1)}, u32[]{:S(2)}, u32[]{:S(2)}) collective-permute-start(bf16[8,72,576]{2,1,0:T(8,128)(2,1)} %all_to_all.41), channel_id=1, source_target_pairs={{0,16},{16,0},{1,17},{17,1},{2,18},{18,2},{3,19},{19,3},{4,20},{20... | collective-permute-start | bytes 1990664 | tf_op jit(solution)/shard_map/ppermute | solution.py:110
  133.8 1.7 reshape.218
  135.5 1.2 fusion.2
  137.8 2.4 maximum_select_fusion.1
  140.2 1.5 convolution_convert_fusion.3
  141.7 3.6 %all-to-all-start.4 = ((bf16[4,72,576]{2,1,0:T(8,128)(2,1)}), bf16[4,72,576]{2,1,0:T(8,128)(2,1)S(1)}, u32[]{:S(2)}, u32[]{:S(2)}) async-start(bf16[4,72,576]{2,1,0:T(8,128)(2,1)} %bitcast.21), calls=%async_computation.4 | async-start | bytes 737280 | tf_op jit(solution)/shard_map/all_to_all | solution.py:21
  146.9 8.0 %all-to-all-done.4 = bf16[4,72,576]{2,1,0:T(8,128)(2,1)S(1)} async-done(((bf16[4,72,576]{2,1,0:T(8,128)(2,1)}), bf16[4,72,576]{2,1,0:T(8,128)(2,1)S(1)}, u32[]{:S(2)}, u32[]{:S(2)}) %all-to-all-start.4) | async-done | bytes 331808 | tf_op jit(solution)/shard_map/all_to_all | solution.py:21
  155.1 17.1 %all_to_all.42 = bf16[4,72,576]{2,1,0:T(8,128)(2,1)S(1)} all-to-all(bf16[4,72,576]{2,1,0:T(8,128)(2,1)S(1)} %broadcast_in_dim.17), channel_id=1, replica_groups=mesh['x'=4,'z1'=2,'z0'=2,'c'=2,'y'=8,'z2'=2] {'z1','z2'}, dimensions={0} | all-to-all | bytes 663552 | tf_op jit(solution)/shard_map/all_to_all | solution.py:15
  173.0 1.5 reshape.221
  175.4 1.6 reshape.222
  177.1 22.3 %all_to_all.43 = bf16[8,72,576]{2,1,0:T(8,128)(2,1)S(1)} all-to-all(bf16[8,72,576]{2,1,0:T(8,128)(2,1)} %reshape.222), channel_id=1, replica_groups=mesh['x'=4,'z1'=2,'z0'=2,'c'=2,'y'=8,'z2'=2] {'y'}, dimensions={0} | all-to-all | bytes 1327104 | tf_op jit(solution)/shard_map/all_to_all | solution.py:21
  199.4 8.0 %collective-permute-start.7 = (bf16[72,576]{1,0:T(8,128)(2,1)S(1)}, bf16[72,576]{1,0:T(8,128)(2,1)S(1)}, u32[]{:S(2)}, u32[]{:S(2)}) collective-permute-start(bf16[72,576]{1,0:T(8,128)(2,1)S(1)} %reduce_sum.47), channel_id=1, source_target_pairs={{0,64},{64,0},{1,65},{65,1},{2,66},{66,2},{3,67},{67,3},{4,68},{68... | collective-permute-start | bytes 248840 | tf_op jit(solution)/shard_map/ppermute | solution.py:124
  208.5 1.9 collective-permute-done.7
  212.0 1.1 copy.21
  213.2 3.6 %collective-permute-start.8 = (bf16[8,72,576]{2,1,0:T(8,128)(2,1)S(1)}, bf16[8,72,576]{2,1,0:T(8,128)(2,1)S(1)}, u32[]{:S(2)}, u32[]{:S(2)}) collective-permute-start(bf16[8,72,576]{2,1,0:T(8,128)(2,1)S(1)} %select_bitcast_fusion), channel_id=1, source_target_pairs={{0,16},{16,0},{1,17},{17,1},{2,18},{18,2},{3,19},{19,3},{4,20},{20... | collective-permute-start | bytes 1990664 | tf_op jit(solution)/shard_map/ppermute | solution.py:143
  216.8 1.8 collective-permute-done.8
  219.0 15.4 %all_to_all.44 = bf16[8,72,576]{2,1,0:T(8,128)(2,1)S(1)} all-to-all(bf16[8,72,576]{2,1,0:T(8,128)(2,1)S(1)} %fusion), channel_id=1, replica_groups=mesh['x'=4,'z1'=2,'z0'=2,'c'=2,'y'=8,'z2'=2] {'x','z0'}, dimensions={0} | all-to-all | bytes 1327104 | tf_op jit(solution)/shard_map/all_to_all | solution.py:21
  (72 shorter events, 15.4 us)
Async XLA Ops:
  6.5 2.3 copy-start.5
  8.0 17.3 %copy-start.6 = (f32[144,576]{1,0:T(8,128)S(1)}, f32[144,576]{1,0:T(8,128)}, u32[]{:S(2)}) copy-start(f32[144,576]{1,0:T(8,128)} %param.6) | copy-start | bytes 995332
  8.1 31.8 %collective-permute-start = (bf16[2,72,576]{2,1,0:T(8,128)(2,1)S(1)}, bf16[2,72,576]{2,1,0:T(8,128)(2,1)S(1)}, u32[]{:S(2)}, u32[]{:S(2)}) collective-permute-start(bf16[2,72,576]{2,1,0:T(8,128)(2,1)S(1)} %pad_maximum_fusion.2), channel_id=1, source_target_pairs={{0,0},{2,64},{4,4},{6,68},{8,8},{10,72},{12,12},{14,76},{64,2},{66... | collective-permute-start | bytes 497672 | tf_op jit(solution)/shard_map/ppermute | solution.py:76
  9.3 25.5 %collective-permute-start.4 = (bf16[72,288]{1,0:T(8,128)(2,1)S(1)}, bf16[72,288]{1,0:T(8,128)(2,1)S(1)}, u32[]{:S(2)}, u32[]{:S(2)}) collective-permute-start(bf16[72,288]{1,0:T(8,128)(2,1)S(1)} %get-tuple-element.18), channel_id=1, source_target_pairs={{0,65},{1,64},{64,1},{65,0},{2,67},{3,66},{66,3},{67,2},{4,69},{5,... | collective-permute-start | bytes 124424 | tf_op jit(solution)/shard_map/ppermute | solution.py:86
  23.3 11.5 %collective-permute-start.3 = (bf16[72,288]{1,0:T(8,128)(2,1)S(1)}, bf16[72,288]{1,0:T(8,128)(2,1)S(1)}, u32[]{:S(2)}, u32[]{:S(2)}) collective-permute-start(bf16[72,288]{1,0:T(8,128)(2,1)S(1)} %get-tuple-element.19), channel_id=1, source_target_pairs={{0,64},{1,65},{64,0},{65,1},{2,66},{3,67},{66,2},{67,3},{4,68},{5,... | collective-permute-start | bytes 124424 | tf_op jit(solution)/shard_map/ppermute | solution.py:86
  25.3 14.6 %collective-permute-start.1 = (bf16[72,576]{1,0:T(8,128)(2,1)S(1)}, bf16[72,576]{1,0:T(8,128)(2,1)S(1)}, u32[]{:S(2)}, u32[]{:S(2)}) collective-permute-start(bf16[72,576]{1,0:T(8,128)(2,1)S(1)} %slice_select_fusion), channel_id=1, source_target_pairs={{0,0},{1,16},{16,64},{17,80},{32,1},{33,17},{48,65},{49,81},{64,32... | collective-permute-start | bytes 248840 | tf_op jit(solution)/shard_map/ppermute | solution.py:94
  31.0 8.8 %collective-permute-start.2 = (bf16[72,288]{1,0:T(8,128)(2,1)S(1)}, bf16[72,288]{1,0:T(8,128)(2,1)S(1)}, u32[]{:S(2)}, u32[]{:S(2)}) collective-permute-start(bf16[72,288]{1,0:T(8,128)(2,1)S(1)} %get-tuple-element.17), channel_id=1, source_target_pairs={{0,1},{1,0},{64,65},{65,64},{2,3},{3,2},{66,67},{67,66},{4,5},{5,4... | collective-permute-start | bytes 124424 | tf_op jit(solution)/shard_map/ppermute | solution.py:86
  39.9 5.0 %copy-start.7 = (bf16[2,72,576]{2,1,0:T(8,128)(2,1)}, bf16[2,72,576]{2,1,0:T(8,128)(2,1)S(1)}, u32[]{:S(2)}) copy-start(bf16[2,72,576]{2,1,0:T(8,128)(2,1)S(1)} %collective-permute-done) | copy-start | bytes 497668
  40.9 15.0 %all-to-all-start.1 = ((bf16[8,72,576]{2,1,0:T(8,128)(2,1)}), bf16[8,72,576]{2,1,0:T(8,128)(2,1)S(1)}, u32[]{:S(2)}, u32[]{:S(2)}) async-start(bf16[8,72,576]{2,1,0:T(8,128)(2,1)} %broadcast_in_dim.13), calls=%async_computation.1 | async-start | bytes 1474560 | tf_op jit(solution)/shard_map/all_to_all | solution.py:15
  44.9 66.9 %all-gather.3.cloned.1.call-start = ((), (), s32[]{:S(2)}) async-start(), calls=%async_computation.8 | async-start | bytes 1658880 | tf_op jit(solution)/shard_map/all_gather | solution.py:99
  56.8 35.0 %all-to-all-start = ((bf16[8,72,576]{2,1,0:T(8,128)(2,1)}), bf16[8,72,576]{2,1,0:T(8,128)(2,1)S(1)}, u32[]{:S(2)}, u32[]{:S(2)}) async-start(bf16[8,72,576]{2,1,0:T(8,128)(2,1)} %broadcast_in_dim.12), calls=%async_computation | async-start | bytes 1474560 | tf_op jit(solution)/shard_map/all_to_all | solution.py:15
  63.8 30.6 %collective-permute-start.5 = (bf16[8,72,576]{2,1,0:T(8,128)(2,1)S(1)}, bf16[8,72,576]{2,1,0:T(8,128)(2,1)}, u32[]{:S(2)}, u32[]{:S(2)}) collective-permute-start(bf16[8,72,576]{2,1,0:T(8,128)(2,1)S(1)} %all-to-all-done.1), channel_id=1, source_target_pairs={{0,16},{16,0},{1,17},{17,1},{2,18},{18,2},{3,19},{19,3},{4,20},{20... | collective-permute-start | bytes 1990664 | tf_op jit(solution)/shard_map/ppermute | solution.py:98
  96.4 1.1 copy-start
  111.8 22.0 %copy-start.2 = (bf16[16,72,576]{2,1,0:T(8,128)(2,1)S(1)}, bf16[16,72,576]{2,1,0:T(8,128)(2,1)}, u32[]{:S(2)}) copy-start(bf16[16,72,576]{2,1,0:T(8,128)(2,1)} %all-gather.3.cloned.1.call-done) | copy-start | bytes 3981316
  128.9 8.9 %collective-permute-start.6 = (bf16[8,72,576]{2,1,0:T(8,128)(2,1)}, bf16[8,72,576]{2,1,0:T(8,128)(2,1)}, u32[]{:S(2)}, u32[]{:S(2)}) collective-permute-start(bf16[8,72,576]{2,1,0:T(8,128)(2,1)} %all_to_all.41), channel_id=1, source_target_pairs={{0,16},{16,0},{1,17},{17,1},{2,18},{18,2},{3,19},{19,3},{4,20},{20... | collective-permute-start | bytes 1990664 | tf_op jit(solution)/shard_map/ppermute | solution.py:110
  137.8 2.4 %copy-start.3 = (bf16[288,1152]{1,0:T(8,128)(2,1)}, bf16[288,1152]{1,0:T(8,128)(2,1)S(1)}, u32[]{:S(2)}) copy-start(bf16[288,1152]{1,0:T(8,128)(2,1)S(1)} %unstack.13) | copy-start | bytes 1990660
  141.7 30.5 %copy-start.1 = (bf16[8,144,576]{2,1,0:T(8,128)(2,1)S(1)}, bf16[8,144,576]{2,1,0:T(8,128)(2,1)}, u32[]{:S(2)}) copy-start(bf16[8,144,576]{2,1,0:T(8,128)(2,1)} %copy-done) | copy-start | bytes 3981316
  141.7 13.2 %all-to-all-start.4 = ((bf16[4,72,576]{2,1,0:T(8,128)(2,1)}), bf16[4,72,576]{2,1,0:T(8,128)(2,1)S(1)}, u32[]{:S(2)}, u32[]{:S(2)}) async-start(bf16[4,72,576]{2,1,0:T(8,128)(2,1)} %bitcast.21), calls=%async_computation.4 | async-start | bytes 737280 | tf_op jit(solution)/shard_map/all_to_all | solution.py:21
  199.4 10.9 %collective-permute-start.7 = (bf16[72,576]{1,0:T(8,128)(2,1)S(1)}, bf16[72,576]{1,0:T(8,128)(2,1)S(1)}, u32[]{:S(2)}, u32[]{:S(2)}) collective-permute-start(bf16[72,576]{1,0:T(8,128)(2,1)S(1)} %reduce_sum.47), channel_id=1, source_target_pairs={{0,64},{64,0},{1,65},{65,1},{2,66},{66,2},{3,67},{67,3},{4,68},{68... | collective-permute-start | bytes 248840 | tf_op jit(solution)/shard_map/ppermute | solution.py:124
  207.9 2.7 %copy-start.4 = (bf16[288,1152]{1,0:T(8,128)(2,1)S(1)}, bf16[288,1152]{1,0:T(8,128)(2,1)}, u32[]{:S(2)}) copy-start(bf16[288,1152]{1,0:T(8,128)(2,1)} %copy-done.3) | copy-start | bytes 1990660
  213.2 5.4 %collective-permute-start.8 = (bf16[8,72,576]{2,1,0:T(8,128)(2,1)S(1)}, bf16[8,72,576]{2,1,0:T(8,128)(2,1)S(1)}, u32[]{:S(2)}, u32[]{:S(2)}) collective-permute-start(bf16[8,72,576]{2,1,0:T(8,128)(2,1)S(1)} %select_bitcast_fusion), channel_id=1, source_target_pairs={{0,16},{16,0},{1,17},{17,1},{2,18},{18,2},{3,19},{19,3},{4,20},{20... | collective-permute-start | bytes 1990664 | tf_op jit(solution)/shard_map/ppermute | solution.py:143
Sparse Core Ops, SparseCore 0:
  47.8 49.1 all-gather.2

commit v6 on v3

v6 whole, which is shorter than its diff:
```python
import jax
import jax.numpy as jnp
from jax import lax
from jax.experimental import pallas as pl
from jax.experimental.pallas import tpu as pltpu
from jax.sharding import Mesh, PartitionSpec as P

DAMPING = 0.1
AXES = ("x", "z1", "z0", "c", "y", "z2")
ROWS = ("x", "z1", "z0", "c")
RING = ("x", "z0")
PART = ("z1", "z2")
SWAP = [(0, 1), (1, 0)]


def gather(block, axes, count):
    return lax.all_to_all(
        jnp.broadcast_to(block[None], (count,) + block.shape), axes, 0, 0, tiled=True
    )


def scatter_sum(blocks, axes):
    got = lax.all_to_all(blocks, axes, 0, 0, tiled=True)
    return jnp.sum(got.astype(jnp.float32), axis=0)


def dot(left, right, left_dim, right_dim):
    return lax.dot_general(
        left, right, (((left_dim,), (right_dim,)), ((), ())), preferred_element_type=jnp.float32
    )


def in_order(first, mine, other, axis):
    return jnp.where(
        first,
        jnp.concatenate([mine, other], axis=axis),
        jnp.concatenate([other, mine], axis=axis),
    )


def pairs_z1y0():
    return [(z1 * 8 + y, (y % 2) * 8 + (y // 2) * 2 + z1) for z1 in range(2) for y in range(8)]


def pairs_part(d1, d2):
    return [(i, i ^ (2 * d1 + d2)) for i in range(4)]


def pairs_rows():
    return [
        (z1 * 8 + z0 * 4 + c * 2 + z2, c * 8 + z1 * 4 + z2 * 2 + z0)
        for z1 in range(2)
        for z0 in range(2)
        for c in range(2)
        for z2 in range(2)
    ]


def pack(rows):
    q = rows.shape[0] // 2
    return jnp.concatenate([rows[:q], rows[q:]], axis=1)


def run(kernel, outs, args, scratch=(), flags=0):
    size = sum(a.size * a.dtype.itemsize for a in (*args, *jax.tree.leaves(outs)))
    return pl.pallas_call(
        kernel,
        out_shape=outs,
        in_specs=[
            pl.BlockSpec(memory_space=pltpu.SMEM if i < flags else pltpu.VMEM)
            for i in range(len(args))
        ],
        scratch_shapes=[pltpu.VMEM(shape, jnp.bfloat16) for shape in scratch],
        cost_estimate=pl.CostEstimate(flops=2 * 288 * 1152 * 576, bytes_accessed=size, transcendentals=0),
        compiler_params=pltpu.CompilerParams(vmem_limit_bytes=32 * 2**20),
    )(*args)


def shape(*dims):
    return jax.ShapeDtypeStruct(dims, jnp.bfloat16)


def order_out(core, rep, rows, out):
    q = out.shape[1]
    low_core, low_rep = core[0] == 0, rep[0] == 0
    for a in range(2):
        block = rows[q * a : q * a + q].astype(jnp.bfloat16).astype(jnp.float32)
        for t in range(4):
            def cut(block_c, half):
                at = (4 * (t // 2) + 2 * block_c + half) * q
                return block[:, at : at + q]

            for far in range(2):
                first = jnp.where(low_core, cut(t % 2, far), cut(1 - t % 2, far))
                second = jnp.where(low_core, cut(t % 2, 1 - far), cut(1 - t % 2, 1 - far))
                at = (4 * a + t) * q
                out[far, :, at : at + q] = jnp.where(low_rep, first, second).astype(jnp.bfloat16)


def turn_in(grad, basis, out, left):
    count, _, wide = grad.shape
    q = wide // 4
    for y in range(count):
        for g in range(4):
            left[g, :, q * y : q * y + q] = grad[y, :, q * g : q * g + q]
    right = basis[...].reshape(count * q, basis.shape[2])
    for g in range(4):
        out[g] = dot(left[g], right, 1, 0).astype(out.dtype)


def turn_out(rows, own, other, out, left, right):
    q, wide = own.shape[1], rows.shape[3] // 2
    for x in range(4):
        for b in range(2):
            for h in range(2):
                left[2 * b + h, :, wide * x : wide * x + wide] = rows[
                    2 * x + b, 0, :, wide * h : wide * h + wide
                ]
    for i in range(8):
        right[2 * q * i : 2 * q * i + q] = own[i]
        right[2 * q * i + q : 2 * q * i + 2 * q] = other[i]
    right = right[...]
    for g in range(4):
        out[g] = dot(left[g], right, 1, 0).astype(out.dtype)


def back_in(scaled, basis, out):
    q = basis.shape[1]
    for y in range(basis.shape[0]):
        for g in range(4):
            out[y, :, q * g : q * g + q] = dot(scaled[g], basis[y], 1, 1).astype(out.dtype)


def back_out(part, rows, mine, other, keep, give, right):
    q, wide = mine.shape[0], mine.shape[1] // 2
    low = part[0] == 0
    for g in range(4):
        a = mine[:, wide // 2 * g : wide // 2 * (g + 1)]
        b = other[:, wide // 2 * g : wide // 2 * (g + 1)]
        right[g, :, : wide // 2] = jnp.where(low, a, b)
        right[g, :, wide // 2 :] = jnp.where(low, b, a)
    for x in range(4):
        for n in range(2):
            total = jnp.zeros((wide, wide), jnp.float32)
            for b in range(2):
                for h in range(2):
                    left = rows[2 * x + b, n, :, wide * h : wide * h + wide]
                    total += dot(left, right[2 * b + h], 0, 0)
            total = total.astype(keep.dtype)
            for z in range(2):
                at = 2 * q * z
                keep[2 * x + z, :, wide * n : wide * n + wide] = total[at : at + q]
                give[2 * x + z, :, wide * n : wide * n + wide] = total[at + q : at + 2 * q]


def body(grad_parts, basis_in, basis_out, eig_in, eig_out):
    bf16, f32 = jnp.bfloat16, jnp.float32
    x, z1, z0, c, y, z2 = (lax.axis_index(a) for a in AXES)
    rows, cols = basis_in.shape
    half, quarter = rows // 2, cols // 4
    wide = 2 * rows
    low_core, low_rep, low_z1 = c == 0, z2 == 0, z1 == 0


    core, rep, part_z1 = (i.astype(jnp.int32).reshape(1) for i in (c, z2, z1))

    bo = run(order_out, shape(2, half, cols), (core, rep, basis_out), flags=2)
    bo = lax.ppermute(bo, ("z1", "y"), pairs_z1y0())

    grad = grad_parts[0]
    parts = jnp.stack([pack(grad[:, i * quarter : (i + 1) * quarter]) for i in range(4)])

    def piece(d1, d2):
        which = 2 * (z2 ^ d2) + (z1 ^ d1)
        return lax.dynamic_index_in_dim(parts, which, 0, keepdims=False)

    def from_part(d1, d2):
        return lax.ppermute(piece(d1, d2), PART, pairs_part(d1, d2)).astype(f32)

    mine = (piece(0, 0).astype(f32) + from_part(0, 1)).astype(bf16)
    other = (from_part(1, 0) + from_part(1, 1)).astype(bf16)
    grad = in_order(low_z1, mine, other, 1)

    bi = basis_in.astype(bf16)
    bi = jnp.where(low_rep, bi[:half], bi[half:])
    bi = lax.ppermute(bi, ("z1", "z0", "c", "z2"), pairs_rows())
    bi = gather(bi, RING, 8)
    bi = in_order(low_core, bi, lax.ppermute(bi, "c", SWAP), 1)

    bo, grad = lax.optimization_barrier((bo, grad))
    grad = gather(grad, "y", 8)
    bo, grad = lax.optimization_barrier((bo, grad))
    bo = lax.all_gather(bo, "y", axis=0)

    left = (4, half, 8 * quarter)
    part = run(turn_in, shape(4, half, cols), (grad, bi), (left,))
    turned = scatter_sum(part, PART).astype(bf16)
    turned = gather(turned, RING, 8)
    other = lax.ppermute(turned, "c", SWAP)

    right = (8 * rows, cols)
    part = run(turn_out, shape(4, half, cols), (bo, turned, other), (left, right))
    rotated = scatter_sum(part, PART)
    first = (((x * 2 + z1) * 2 + z0) * 2 + c) * rows + z2 * half
    out_scale = lax.dynamic_slice_in_dim(eig_out, first, half, 0)
    in_scale = lax.dynamic_slice_in_dim(eig_in, y * cols, cols, 0)
    scaled = (rotated / (out_scale[:, None] * in_scale[None, :] + DAMPING)).astype(bf16)
    scaled = gather(scaled, PART, 4)

    part = run(back_in, shape(8, half, cols), (scaled, bi))
    back = scatter_sum(part, "y").astype(bf16)
    other = lax.ppermute(back, "z1", SWAP)

    keep, give = run(
        back_out,
        (shape(8, half, cols), shape(8, half, cols)),
        (part_z1, bo, back, other),
        ((4, half, wide),),
        flags=1,
    )
    part = (keep.astype(f32) + lax.ppermute(give, "c", SWAP).astype(f32)).astype(bf16)
    out = scatter_sum(part, RING).astype(bf16)
    return in_order(low_rep, out[:, :wide], out[:, wide:], 0)


def solution(mesh):
    fine = Mesh(mesh.devices.reshape(4, 2, 2, 2, 8, 2), AXES)
    in_specs = (P("z2", ROWS, "y"), P(ROWS, "y"), P(ROWS, "y"), P(), P())
    out_specs = P(ROWS, ("y", "z2"))
    return jax.shard_map(body, mesh=fine, in_specs=in_specs, out_specs=out_specs, check_vma=False)
```

time: 229 us -> 228 us (level)
  local copies, waits for them, and re-layouts: 21.8 us -> 5.15 us
  starting transfers between devices: 64 us -> 79.5 us
  Pallas kernels: 0 us -> 9.71 us
  waiting for transfers between devices: 43.1 us -> 49.9 us
  blocking collectives: 71.3 us -> 64.7 us
  other arithmetic: 9.35 us -> 4.68 us
  matrix products: 4.2 us -> 0 us
    all_to_all x3 -> x2, blocking collectives: 46 us -> 33.8 us  [scatter_sum(): got = lax.all_to_all(blocks, axes, 0, 0, tiled=True)]
    reshape x7 -> x0, local copies, waits for them, and re-layouts: 11.5 us -> none  [the longest x2 5.49 us: body(): bo = bo.reshape(4, 2, 2, half, 2, wide).transpose(2, 1, 4, 3, 0, 5)]
    pallas_call x0 -> x5, Pallas kernels: none -> 9.71 us  [run(): pl.pallas_call(kernel, out_shape=outs, in_specs=[pl.BlockSpec(memory_spac...]
    all_gather x1, waiting for transfers between devices: 0.02 us -> 9.6 us  [body(): bo = lax.all_gather(bo, 'y', axis=0)]
    all_to_all x2, waiting for transfers between devices: 17.7 us -> 9.31 us  [gather(): lax.all_to_all(jnp.broadcast_to(block[None], (count,) + block.shape), axe...]
    all_to_all x1 -> x2, waiting for transfers between devices: 7.13 us -> 14.9 us  [scatter_sum(): got = lax.all_to_all(blocks, axes, 0, 0, tiled=True)]
    all_to_all x2, starting transfers between devices: 12.8 us -> 19.7 us  [gather(): lax.all_to_all(jnp.broadcast_to(block[None], (count,) + block.shape), axe...]
    all_to_all x1 -> x2, starting transfers between devices: 5.99 us -> 12.3 us  [scatter_sum(): got = lax.all_to_all(blocks, axes, 0, 0, tiled=True)]
  transfers between devices with their start and end apart: 13 -> 14, of which waited for: 6 -> 8; matrix products, arithmetic and copies ran while one was open for 7% -> 1% of each run, Pallas kernels for 0% -> 0%
where the time goes in v6:
time: 228 us; the launch traced here: 227 us
  starting transfers between devices  79.5 us (35%)
  blocking collectives  64.7 us (28%)
  waiting for transfers between devices  49.9 us (22%)
  between operations  13.7 us (6%)
  Pallas kernels  9.71 us (4%)
  local copies, waits for them, and re-layouts  5.15 us (2%)
  other arithmetic  4.68 us (2%)
    all_to_all x2, blocking collectives, scatter_sum(): got = lax.all_to_all(blocks, axes, 0, 0, tiled=True)  33.8 us
    all_to_all x2, blocking collectives, gather(): lax.all_to_all(jnp.broadcast_to(block[None], (count,) + block.shape), axe...  30.9 us
    all_to_all x2, starting transfers between devices, gather(): lax.all_to_all(jnp.broadcast_to(block[None], (count,) + block.shape), axe...  19.7 us
    all_to_all x2, waiting for transfers between devices, scatter_sum(): got = lax.all_to_all(blocks, axes, 0, 0, tiled=True)  14.9 us
    all_to_all x2, starting transfers between devices, scatter_sum(): got = lax.all_to_all(blocks, axes, 0, 0, tiled=True)  12.3 us
    ppermute x1, starting transfers between devices, body(): lax.ppermute(give, 'c', SWAP).astype(f32)  11.7 us
    ppermute x3, starting transfers between devices, from_part(): return lax.ppermute(piece(d1, d2), PART, pairs_part(d1, d2)).astype(f32)  11.4 us
    pallas_call x5, Pallas kernels, run(): pl.pallas_call(kernel, out_shape=outs, in_specs=[pl.BlockSpec(memory_spac...  9.71 us
  transfers between devices with their start and end apart: 14, of which 8 were waited for; matrix products, arithmetic and copies ran while one was open for 1% of the time, Pallas kernels for 0%

profile of v6, /device:TPU:1, one launch (start us, length us, event | category | flops | bytes accessed | tf_op | source)
XLA Modules:
  0.0 227.3 jit_solution(7500501281886484177)
XLA Ops:
  6.5 1.0 convert_element_type.56
  7.6 7.2 %collective-permute-start.4 = (bf16[72,576]{1,0:T(8,128)(2,1)S(1)}, bf16[72,576]{1,0:T(8,128)(2,1)S(1)}, u32[]{:S(2)}, u32[]{:S(2)}) collective-permute-start(bf16[72,576]{1,0:T(8,128)(2,1)S(1)} %slice_select_fusion), channel_id=1, source_target_pairs={{0,0},{1,16},{16,64},{17,80},{32,1},{33,17},{48,65},{49,81},{64,32... | collective-permute-start | bytes 248840 | tf_op jit(solution)/shard_map/ppermute | solution.py:186
  14.8 7.1 %collective-permute-done.4 = bf16[72,576]{1,0:T(8,128)(2,1)S(1)} collective-permute-done((bf16[72,576]{1,0:T(8,128)(2,1)S(1)}, bf16[72,576]{1,0:T(8,128)(2,1)S(1)}, u32[]{:S(2)}, u32[]{:S(2)}) %collective-permute-start.4) | collective-permute-done | bytes 82976 | tf_op jit(solution)/shard_map/ppermute | solution.py:186
  22.9 5.9 %all-to-all-start.1 = ((bf16[8,72,576]{2,1,0:T(8,128)(2,1)}), bf16[8,72,576]{2,1,0:T(8,128)(2,1)S(1)}, u32[]{:S(2)}, u32[]{:S(2)}) async-start(bf16[8,72,576]{2,1,0:T(8,128)(2,1)} %broadcast_in_dim.9), calls=%async_computation.1 | async-start | bytes 1474560 | tf_op jit(solution)/shard_map/all_to_all | solution.py:17
  29.3 2.4 %collective-permute-start.2 = (bf16[72,288]{1,0:T(8,128)(2,1)S(1)}, bf16[72,288]{1,0:T(8,128)(2,1)S(1)}, u32[]{:S(2)}, u32[]{:S(2)}) collective-permute-start(bf16[72,288]{1,0:T(8,128)(2,1)S(1)} %get-tuple-element.19), channel_id=1, source_target_pairs={{0,64},{1,65},{64,0},{65,1},{2,66},{3,67},{66,2},{67,3},{4,68},{5,... | collective-permute-start | bytes 124424 | tf_op jit(solution)/shard_map/ppermute | solution.py:178
  31.7 2.9 %collective-permute-start.3 = (bf16[72,288]{1,0:T(8,128)(2,1)S(1)}, bf16[72,288]{1,0:T(8,128)(2,1)S(1)}, u32[]{:S(2)}, u32[]{:S(2)}) collective-permute-start(bf16[72,288]{1,0:T(8,128)(2,1)S(1)} %get-tuple-element.18), channel_id=1, source_target_pairs={{0,65},{1,64},{64,1},{65,0},{2,67},{3,66},{66,3},{67,2},{4,69},{5,... | collective-permute-start | bytes 124424 | tf_op jit(solution)/shard_map/ppermute | solution.py:178
  34.6 6.2 %collective-permute-start.1 = (bf16[72,288]{1,0:T(8,128)(2,1)S(1)}, bf16[72,288]{1,0:T(8,128)(2,1)S(1)}, u32[]{:S(2)}, u32[]{:S(2)}) collective-permute-start(bf16[72,288]{1,0:T(8,128)(2,1)S(1)} %get-tuple-element.17), channel_id=1, source_target_pairs={{0,1},{1,0},{64,65},{65,64},{2,3},{3,2},{66,67},{67,66},{4,5},{5,4... | collective-permute-start | bytes 124424 | tf_op jit(solution)/shard_map/ppermute | solution.py:178
  40.7 1.1 shard_map.55
  43.5 0.9 broadcast_in_dim.8
  44.5 13.7 %all-to-all-start = ((bf16[8,72,576]{2,1,0:T(8,128)(2,1)}), bf16[8,72,576]{2,1,0:T(8,128)(2,1)S(1)}, u32[]{:S(2)}, u32[]{:S(2)}) async-start(bf16[8,72,576]{2,1,0:T(8,128)(2,1)} %broadcast_in_dim.8), calls=%async_computation | async-start | bytes 1474560 | tf_op jit(solution)/shard_map/all_to_all | solution.py:17
  58.2 7.5 %collective-permute-start.5 = (bf16[8,72,576]{2,1,0:T(8,128)(2,1)S(1)}, bf16[8,72,576]{2,1,0:T(8,128)(2,1)}, u32[]{:S(2)}, u32[]{:S(2)}) collective-permute-start(bf16[8,72,576]{2,1,0:T(8,128)(2,1)S(1)} %all-to-all-done.1), channel_id=1, source_target_pairs={{0,16},{16,0},{1,17},{17,1},{2,18},{18,2},{3,19},{19,3},{4,20},{20... | collective-permute-start | bytes 1990664 | tf_op jit(solution)/shard_map/ppermute | solution.py:188
  65.7 9.3 %all-to-all-done.grad = bf16[8,72,576]{2,1,0:T(8,128)(2,1)S(1)} async-done(((bf16[8,72,576]{2,1,0:T(8,128)(2,1)}), bf16[8,72,576]{2,1,0:T(8,128)(2,1)S(1)}, u32[]{:S(2)}, u32[]{:S(2)}) %all-to-all-start) | async-done | bytes 663584 | tf_op jit(solution)/shard_map/all_to_all | solution.py:17
  75.0 1.9 maximum_select_fusion.basis
  77.0 1.9 shard_map.56
  78.8 5.2 %all-to-all-start.2 = ((bf16[4,72,576]{2,1,0:T(8,128)(2,1)}), bf16[4,72,576]{2,1,0:T(8,128)(2,1)S(1)}, u32[]{:S(2)}, u32[]{:S(2)}) async-start(bf16[4,72,576]{2,1,0:T(8,128)(2,1)} %shard_map.56), calls=%async_computation.2 | async-start | bytes 737280 | tf_op jit(solution)/shard_map/all_to_all | solution.py:23
  84.7 7.8 %all-to-all-done.2 = bf16[4,72,576]{2,1,0:T(8,128)(2,1)S(1)} async-done(((bf16[4,72,576]{2,1,0:T(8,128)(2,1)}), bf16[4,72,576]{2,1,0:T(8,128)(2,1)S(1)}, u32[]{:S(2)}, u32[]{:S(2)}) %all-to-all-start.2) | async-done | bytes 331808 | tf_op jit(solution)/shard_map/all_to_all | solution.py:23
  92.6 17.4 %all_to_all.40.own = bf16[8,72,576]{2,1,0:T(8,128)(2,1)S(1)} all-to-all(bf16[8,72,576]{2,1,0:T(8,128)(2,1)S(1)} %broadcast_in_dim.10), channel_id=1, replica_groups=mesh['x'=4,'z1'=2,'z0'=2,'c'=2,'y'=8,'z2'=2] {'x','z0'}, dimensions={0} | all-to-all | bytes 1327104 | tf_op jit(solution)/shard_map/all_to_all | solution.py:17
  110.1 7.1 %collective-permute-start.6 = (bf16[8,72,576]{2,1,0:T(8,128)(2,1)S(1)}, bf16[8,72,576]{2,1,0:T(8,128)(2,1)S(1)}, u32[]{:S(2)}, u32[]{:S(2)}) collective-permute-start(bf16[8,72,576]{2,1,0:T(8,128)(2,1)S(1)} %all_to_all.40.own), channel_id=1, source_target_pairs={{0,16},{16,0},{1,17},{17,1},{2,18},{18,2},{3,19},{19,3},{4,20},{20... | collective-permute-start | bytes 1990664 | tf_op jit(solution)/shard_map/ppermute | solution.py:199
  117.2 9.6 %all-gather.3.cloned.1.call-done = bf16[16,72,576]{2,1,0:T(8,128)(2,1)} async-done(((bf16[2,72,576]{2,1,0:T(8,128)(2,1)}), bf16[16,72,576]{2,1,0:T(8,128)(2,1)}) %all-gather.3.cloned.1.call-update) | async-done | bytes 1327120 | tf_op jit(solution)/shard_map/all_gather | solution.py:193
  126.8 1.4 copy-done
  128.2 1.9 shard_map.57
  130.1 7.1 %all-to-all-start.4 = ((bf16[4,72,576]{2,1,0:T(8,128)(2,1)}), bf16[4,72,576]{2,1,0:T(8,128)(2,1)S(1)}, u32[]{:S(2)}, u32[]{:S(2)}) async-start(bf16[4,72,576]{2,1,0:T(8,128)(2,1)} %shard_map.57), calls=%async_computation.4 | async-start | bytes 737280 | tf_op jit(solution)/shard_map/all_to_all | solution.py:23
  138.7 7.1 %all-to-all-done.4 = bf16[4,72,576]{2,1,0:T(8,128)(2,1)S(1)} async-done(((bf16[4,72,576]{2,1,0:T(8,128)(2,1)}), bf16[4,72,576]{2,1,0:T(8,128)(2,1)S(1)}, u32[]{:S(2)}, u32[]{:S(2)}) %all-to-all-start.4) | async-done | bytes 331808 | tf_op jit(solution)/shard_map/all_to_all | solution.py:23
  146.0 13.4 %all_to_all.41.scaled = bf16[4,72,576]{2,1,0:T(8,128)(2,1)S(1)} all-to-all(bf16[4,72,576]{2,1,0:T(8,128)(2,1)S(1)} %broadcast_in_dim.11), channel_id=1, replica_groups=mesh['x'=4,'z1'=2,'z0'=2,'c'=2,'y'=8,'z2'=2] {'z1','z2'}, dimensions={0} | all-to-all | bytes 663552 | tf_op jit(solution)/shard_map/all_to_all | solution.py:17
  159.5 2.5 %shard_map.58 = bf16[8,72,576]{2,1,0:T(8,128)(2,1)S(1)} custom-call(bf16[4,72,576]{2,1,0:T(8,128)(2,1)S(1)} %all_to_all.41.scaled, bf16[8,144,576]{2,1,0:T(8,128)(2,1)S(1)} %maximum_select_fusion.basis), custom_call_target="tpu_custom_call" | custom-call | flops 382205952 | bytes 2322432 | tf_op jit(solution)/shard_map/pallas_call | solution.py:66
  162.0 18.2 %all_to_all.42 = bf16[8,72,576]{2,1,0:T(8,128)(2,1)S(1)} all-to-all(bf16[8,72,576]{2,1,0:T(8,128)(2,1)S(1)} %shard_map.58), channel_id=1, replica_groups=mesh['x'=4,'z1'=2,'z0'=2,'c'=2,'y'=8,'z2'=2] {'y'}, dimensions={0} | all-to-all | bytes 1327104 | tf_op jit(solution)/shard_map/all_to_all | solution.py:23
  180.4 1.9 collective-permute-start.7
  182.3 5.5 %collective-permute-done.7.other = bf16[72,576]{1,0:T(8,128)(2,1)S(1)} collective-permute-done((bf16[72,576]{1,0:T(8,128)(2,1)S(1)}, bf16[72,576]{1,0:T(8,128)(2,1)S(1)}, u32[]{:S(2)}, u32[]{:S(2)}) %collective-permute-start.7) | collective-permute-done | bytes 82976 | tf_op jit(solution)/shard_map/ppermute | solution.py:212
  187.9 2.3 %shard_map.59 = (bf16[8,72,576]{2,1,0:T(8,128)(2,1)S(1)}, bf16[8,72,576]{2,1,0:T(8,128)(2,1)S(1)}) custom-call(s32[1]{0:T(128)} %bitcast.part, bf16[8,2,72,576]{3,2,1,0:T(8,128)(2,1)S(1)} %bitcast.23, bf16[72,576]{1,0:T(8,128)(2,1)S(1)} %reduce_sum.47.mine, bf16[72,576]{1,0:T(8,128)(2,1)S(1)} %collective-permute-done.7.other), custom_call_target="tpu_custom_call" | custom-call | flops 382205952 | bytes 2820100 | tf_op jit(solution)/shard_map/pallas_call | solution.py:66
  190.2 11.7 %collective-permute-start.8 = (bf16[8,72,576]{2,1,0:T(8,128)(2,1)S(1)}, bf16[8,72,576]{2,1,0:T(8,128)(2,1)S(1)}, u32[]{:S(2)}, u32[]{:S(2)}) collective-permute-start(bf16[8,72,576]{2,1,0:T(8,128)(2,1)S(1)} %get-tuple-element.16), channel_id=1, source_target_pairs={{0,16},{16,0},{1,17},{17,1},{2,18},{18,2},{3,19},{19,3},{4,20},{20... | collective-permute-start | bytes 1990664 | tf_op jit(solution)/shard_map/ppermute | solution.py:221
  201.9 1.8 collective-permute-done.8
  203.9 15.6 %all_to_all.43 = bf16[8,72,576]{2,1,0:T(8,128)(2,1)S(1)} all-to-all(bf16[8,72,576]{2,1,0:T(8,128)(2,1)S(1)} %add_convert_fusion), channel_id=1, replica_groups=mesh['x'=4,'z1'=2,'z0'=2,'c'=2,'y'=8,'z2'=2] {'x','z0'}, dimensions={0} | all-to-all | bytes 1327104 | tf_op jit(solution)/shard_map/all_to_all | solution.py:23
  (41 shorter events, 6.8 us)
Async XLA Ops:
  6.5 22.3 %copy-start.3 = (bf16[1,144,576]{2,1,0:T(8,128)(2,1)S(1)}, bf16[1,144,576]{2,1,0:T(8,128)(2,1)}, u32[]{:S(2)}) copy-start(bf16[1,144,576]{2,1,0:T(8,128)(2,1)} %param.5) | copy-start | bytes 497668
  7.6 14.4 %collective-permute-start.4 = (bf16[72,576]{1,0:T(8,128)(2,1)S(1)}, bf16[72,576]{1,0:T(8,128)(2,1)S(1)}, u32[]{:S(2)}, u32[]{:S(2)}) collective-permute-start(bf16[72,576]{1,0:T(8,128)(2,1)S(1)} %slice_select_fusion), channel_id=1, source_target_pairs={{0,0},{1,16},{16,64},{17,80},{32,1},{33,17},{48,65},{49,81},{64,32... | collective-permute-start | bytes 248840 | tf_op jit(solution)/shard_map/ppermute | solution.py:186
  22.9 17.8 %copy-start.2 = (f32[144,576]{1,0:T(8,128)S(1)}, f32[144,576]{1,0:T(8,128)}, u32[]{:S(2)}) copy-start(f32[144,576]{1,0:T(8,128)} %rows.1) | copy-start | bytes 995332
  22.9 20.6 %all-to-all-start.1 = ((bf16[8,72,576]{2,1,0:T(8,128)(2,1)}), bf16[8,72,576]{2,1,0:T(8,128)(2,1)S(1)}, u32[]{:S(2)}, u32[]{:S(2)}) async-start(bf16[8,72,576]{2,1,0:T(8,128)(2,1)} %broadcast_in_dim.9), calls=%async_computation.1 | async-start | bytes 1474560 | tf_op jit(solution)/shard_map/all_to_all | solution.py:17
  29.3 13.2 %collective-permute-start.2 = (bf16[72,288]{1,0:T(8,128)(2,1)S(1)}, bf16[72,288]{1,0:T(8,128)(2,1)S(1)}, u32[]{:S(2)}, u32[]{:S(2)}) collective-permute-start(bf16[72,288]{1,0:T(8,128)(2,1)S(1)} %get-tuple-element.19), channel_id=1, source_target_pairs={{0,64},{1,65},{64,0},{65,1},{2,66},{3,67},{66,2},{67,3},{4,68},{5,... | collective-permute-start | bytes 124424 | tf_op jit(solution)/shard_map/ppermute | solution.py:178
  31.7 10.8 %collective-permute-start.3 = (bf16[72,288]{1,0:T(8,128)(2,1)S(1)}, bf16[72,288]{1,0:T(8,128)(2,1)S(1)}, u32[]{:S(2)}, u32[]{:S(2)}) collective-permute-start(bf16[72,288]{1,0:T(8,128)(2,1)S(1)} %get-tuple-element.18), channel_id=1, source_target_pairs={{0,65},{1,64},{64,1},{65,0},{2,67},{3,66},{66,3},{67,2},{4,69},{5,... | collective-permute-start | bytes 124424 | tf_op jit(solution)/shard_map/ppermute | solution.py:178
  34.6 8.8 %collective-permute-start.1 = (bf16[72,288]{1,0:T(8,128)(2,1)S(1)}, bf16[72,288]{1,0:T(8,128)(2,1)S(1)}, u32[]{:S(2)}, u32[]{:S(2)}) collective-permute-start(bf16[72,288]{1,0:T(8,128)(2,1)S(1)} %get-tuple-element.17), channel_id=1, source_target_pairs={{0,1},{1,0},{64,65},{65,64},{2,3},{3,2},{66,67},{67,66},{4,5},{5,4... | collective-permute-start | bytes 124424 | tf_op jit(solution)/shard_map/ppermute | solution.py:178
  41.8 1.7 collective-permute-start
  43.5 33.4 %copy-start.4 = (bf16[2,72,576]{2,1,0:T(8,128)(2,1)}, bf16[2,72,576]{2,1,0:T(8,128)(2,1)S(1)}, u32[]{:S(2)}) copy-start(bf16[2,72,576]{2,1,0:T(8,128)(2,1)S(1)} %collective-permute-done) | copy-start | bytes 497668
  44.5 30.5 %all-to-all-start = ((bf16[8,72,576]{2,1,0:T(8,128)(2,1)}), bf16[8,72,576]{2,1,0:T(8,128)(2,1)S(1)}, u32[]{:S(2)}, u32[]{:S(2)}) async-start(bf16[8,72,576]{2,1,0:T(8,128)(2,1)} %broadcast_in_dim.8), calls=%async_computation | async-start | bytes 1474560 | tf_op jit(solution)/shard_map/all_to_all | solution.py:17
  58.2 16.8 %collective-permute-start.5 = (bf16[8,72,576]{2,1,0:T(8,128)(2,1)S(1)}, bf16[8,72,576]{2,1,0:T(8,128)(2,1)}, u32[]{:S(2)}, u32[]{:S(2)}) collective-permute-start(bf16[8,72,576]{2,1,0:T(8,128)(2,1)S(1)} %all-to-all-done.1), channel_id=1, source_target_pairs={{0,16},{16,0},{1,17},{17,1},{2,18},{18,2},{3,19},{19,3},{4,20},{20... | collective-permute-start | bytes 1990664 | tf_op jit(solution)/shard_map/ppermute | solution.py:188
  78.8 13.7 %all-to-all-start.2 = ((bf16[4,72,576]{2,1,0:T(8,128)(2,1)}), bf16[4,72,576]{2,1,0:T(8,128)(2,1)S(1)}, u32[]{:S(2)}, u32[]{:S(2)}) async-start(bf16[4,72,576]{2,1,0:T(8,128)(2,1)} %shard_map.56), calls=%async_computation.2 | async-start | bytes 737280 | tf_op jit(solution)/shard_map/all_to_all | solution.py:23
  84.0 42.8 %all-gather.3.cloned.1.call-start = ((), (), s32[]{:S(2)}) async-start(), calls=%async_computation.8 | async-start | bytes 1658880 | tf_op jit(solution)/shard_map/all_gather | solution.py:193
  110.1 16.7 %collective-permute-start.6 = (bf16[8,72,576]{2,1,0:T(8,128)(2,1)S(1)}, bf16[8,72,576]{2,1,0:T(8,128)(2,1)S(1)}, u32[]{:S(2)}, u32[]{:S(2)}) collective-permute-start(bf16[8,72,576]{2,1,0:T(8,128)(2,1)S(1)} %all_to_all.40.own), channel_id=1, source_target_pairs={{0,16},{16,0},{1,17},{17,1},{2,18},{18,2},{3,19},{19,3},{4,20},{20... | collective-permute-start | bytes 1990664 | tf_op jit(solution)/shard_map/ppermute | solution.py:199
  126.8 1.4 copy-start
  130.1 15.8 %all-to-all-start.4 = ((bf16[4,72,576]{2,1,0:T(8,128)(2,1)}), bf16[4,72,576]{2,1,0:T(8,128)(2,1)S(1)}, u32[]{:S(2)}, u32[]{:S(2)}) async-start(bf16[4,72,576]{2,1,0:T(8,128)(2,1)} %shard_map.57), calls=%async_computation.4 | async-start | bytes 737280 | tf_op jit(solution)/shard_map/all_to_all | solution.py:23
  162.0 25.8 %copy-start.1 = (bf16[16,72,576]{2,1,0:T(8,128)(2,1)S(1)}, bf16[16,72,576]{2,1,0:T(8,128)(2,1)}, u32[]{:S(2)}) copy-start(bf16[16,72,576]{2,1,0:T(8,128)(2,1)} %all-gather.3.cloned.1.call-done) | copy-start | bytes 3981316
  180.4 7.5 %collective-permute-start.7 = (bf16[72,576]{1,0:T(8,128)(2,1)S(1)}, bf16[72,576]{1,0:T(8,128)(2,1)S(1)}, u32[]{:S(2)}, u32[]{:S(2)}) collective-permute-start(bf16[72,576]{1,0:T(8,128)(2,1)S(1)} %reduce_sum.47.mine), channel_id=1, source_target_pairs={{0,64},{64,0},{1,65},{65,1},{2,66},{66,2},{3,67},{67,3},{4,68},{68... | collective-permute-start | bytes 248840 | tf_op jit(solution)/shard_map/ppermute | solution.py:212
  190.2 13.5 %collective-permute-start.8 = (bf16[8,72,576]{2,1,0:T(8,128)(2,1)S(1)}, bf16[8,72,576]{2,1,0:T(8,128)(2,1)S(1)}, u32[]{:S(2)}, u32[]{:S(2)}) collective-permute-start(bf16[8,72,576]{2,1,0:T(8,128)(2,1)S(1)} %get-tuple-element.16), channel_id=1, source_target_pairs={{0,16},{16,0},{1,17},{17,1},{2,18},{18,2},{3,19},{19,3},{4,20},{20... | collective-permute-start | bytes 1990664 | tf_op jit(solution)/shard_map/ppermute | solution.py:221
Sparse Core Ops, SparseCore 0:
  86.9 39.8 all-gather.2

commit v7 on v6

--- a/solution.py
+++ b/solution.py
@@ -36,10 +36,6 @@
         jnp.concatenate([mine, other], axis=axis),
         jnp.concatenate([other, mine], axis=axis),
     )
-
-
-def pairs_z1y0():
-    return [(z1 * 8 + y, (y % 2) * 8 + (y // 2) * 2 + z1) for z1 in range(2) for y in range(8)]
 
 
 def pairs_part(d1, d2):
@@ -108,20 +104,21 @@
         out[g] = dot(left[g], right, 1, 0).astype(out.dtype)
 
 
-def turn_out(rows, own, other, out, left, right):
+def turn_out(part, rows, near, own, other, out, left, right):
     q, wide = own.shape[1], rows.shape[3] // 2
+    z1 = part[0]
     for x in range(4):
-        for b in range(2):
-            for h in range(2):
-                left[2 * b + h, :, wide * x : wide * x + wide] = rows[
-                    2 * x + b, 0, :, wide * h : wide * h + wide
-                ]
+        for h in range(2):
+            at, cut = wide * x, wide * h
+            left[h, :, at : at + wide] = rows[2 * x + z1, 0, :, cut : cut + wide]
+            left[2 + h, :, at : at + wide] = near[x, :, cut : cut + wide]
     for i in range(8):
         right[2 * q * i : 2 * q * i + q] = own[i]
         right[2 * q * i + q : 2 * q * i + 2 * q] = other[i]
     right = right[...]
-    for g in range(4):
-        out[g] = dot(left[g], right, 1, 0).astype(out.dtype)
+    for h in range(2):
+        out[2 * z1 + h] = dot(left[h], right, 1, 0).astype(out.dtype)
+        out[2 * (1 - z1) + h] = dot(left[2 + h], right, 1, 0).astype(out.dtype)
 
 
 def back_in(scaled, basis, out):
@@ -131,9 +128,10 @@
             out[y, :, q * g : q * g + q] = dot(scaled[g], basis[y], 1, 1).astype(out.dtype)
 
 
-def back_out(part, rows, mine, other, keep, give, right):
+def back_out(part, rows, near, far, mine, other, keep, give, right):
     q, wide = mine.shape[0], mine.shape[1] // 2
-    low = part[0] == 0
+    z1 = part[0]
+    low = z1 == 0
     for g in range(4):
         a = mine[:, wide // 2 * g : wide // 2 * (g + 1)]
         b = other[:, wide // 2 * g : wide // 2 * (g + 1)]
@@ -142,10 +140,12 @@
     for x in range(4):
         for n in range(2):
             total = jnp.zeros((wide, wide), jnp.float32)
-            for b in range(2):
-                for h in range(2):
-                    left = rows[2 * x + b, n, :, wide * h : wide * h + wide]
-                    total += dot(left, right[2 * b + h], 0, 0)
+            for h in range(2):
+                cut = wide * h
+                left = rows[2 * x + z1, n, :, cut : cut + wide]
+                total += dot(left, right[2 * z1 + h], 0, 0)
+                left = (near, far)[n][x, :, cut : cut + wide]
+                total += dot(left, right[2 * (1 - z1) + h], 0, 0)
             total = total.astype(keep.dtype)
             for z in range(2):
                 at = 2 * q * z
@@ -165,7 +165,8 @@
     core, rep, part_z1 = (i.astype(jnp.int32).reshape(1) for i in (c, z2, z1))
 
     bo = run(order_out, shape(2, half, cols), (core, rep, basis_out), flags=2)
-    bo = lax.ppermute(bo, ("z1", "y"), pairs_z1y0())
+    bo, grad_parts = lax.optimization_barrier((bo, grad_parts))
+    bo = lax.all_gather(bo, "y", axis=0)
 
     grad = grad_parts[0]
     parts = jnp.stack([pack(grad[:, i * quarter : (i + 1) * quarter]) for i in range(4)])
@@ -188,18 +189,24 @@
     bi = in_order(low_core, bi, lax.ppermute(bi, "c", SWAP), 1)
 
     bo, grad = lax.optimization_barrier((bo, grad))
+    by_z1 = bo.reshape(4, 2, 2, half, cols)
+
+    def from_other_z1(far):
+        block = lax.dynamic_index_in_dim(by_z1[:, :, far], 1 - z1, 1, keepdims=False)
+        return lax.ppermute(block, "z1", SWAP)
+
+    near, far = from_other_z1(0), from_other_z1(1)
+
     grad = gather(grad, "y", 8)
-    bo, grad = lax.optimization_barrier((bo, grad))
-    bo = lax.all_gather(bo, "y", axis=0)
-
     left = (4, half, 8 * quarter)
     part = run(turn_in, shape(4, half, cols), (grad, bi), (left,))
+    near, part = lax.optimization_barrier((near, part))
     turned = scatter_sum(part, PART).astype(bf16)
     turned = gather(turned, RING, 8)
     other = lax.ppermute(turned, "c", SWAP)
 
     right = (8 * rows, cols)
-    part = run(turn_out, shape(4, half, cols), (bo, turned, other), (left, right))
+    part = run(turn_out, shape(4, half, cols), (part_z1, bo, near, turned, other), (left, right), 1)
     rotated = scatter_sum(part, PART)
     first = (((x * 2 + z1) * 2 + z0) * 2 + c) * rows + z2 * half
     out_scale = lax.dynamic_slice_in_dim(eig_out, first, half, 0)
@@ -209,12 +216,13 @@
 
     part = run(back_in, shape(8, half, cols), (scaled, bi))
     back = scatter_sum(part, "y").astype(bf16)
+    far, back = lax.optimization_barrier((far, back))
     other = lax.ppermute(back, "z1", SWAP)
 
     keep, give = run(
         back_out,
         (shape(8, half, cols), shape(8, half, cols)),
-        (part_z1, bo, back, other),
+        (part_z1, bo, near, far, back, other),
         ((4, half, wide),),
         flags=1,
     )

time: 228 us -> 234 us (1.026)
  waiting for transfers between devices: 49.9 us -> 59.5 us
  starting transfers between devices: 79.5 us -> 71.3 us
  local copies, waits for them, and re-layouts: 5.15 us -> 9.15 us
    ppermute x1 -> x2, waiting for transfers between devices: 0.01 us -> 10.4 us  [from_other_z1(): return lax.ppermute(block, 'z1', SWAP)]
    all_to_all x2, starting transfers between devices: 19.7 us -> 10.1 us  [gather(): lax.all_to_all(jnp.broadcast_to(block[None], (count,) + block.shape), axe...]
    all_to_all x2, waiting for transfers between devices: 14.9 us -> 23.1 us  [scatter_sum(): got = lax.all_to_all(blocks, axes, 0, 0, tiled=True)]
    ppermute x1 -> x2, starting transfers between devices: 0.67 us -> 8.24 us  [from_other_z1(): return lax.ppermute(block, 'z1', SWAP)]
    all_to_all x2, waiting for transfers between devices: 9.31 us -> 2.33 us  [gather(): lax.all_to_all(jnp.broadcast_to(block[None], (count,) + block.shape), axe...]
    ppermute x1, starting transfers between devices: 11.7 us -> 6.38 us  [body(): lax.ppermute(give, 'c', SWAP).astype(f32)]
    ppermute x3, waiting for transfers between devices: 0.81 us -> 4.37 us  [from_part(): return lax.ppermute(piece(d1, d2), PART, pairs_part(d1, d2)).astype(f32)]
    all_gather x1, waiting for transfers between devices: 9.6 us -> 6.11 us  [body(): bo = lax.all_gather(bo, 'y', axis=0)]
  transfers between devices with their start and end apart: 14 -> 15, of which waited for: 8 -> 11; matrix products, arithmetic and copies ran while one was open for 1% -> 3% of each run, Pallas kernels for 0% -> 1%
where the time goes in v7:
time: 234 us; the launch traced here: 233 us
  starting transfers between devices  71.3 us (30%)
  blocking collectives  63.5 us (27%)
  waiting for transfers between devices  59.5 us (25%)
  between operations  13.8 us (6%)
  Pallas kernels  10.1 us (4%)
  local copies, waits for them, and re-layouts  9.15 us (4%)
  other arithmetic  5.91 us (3%)
    all_to_all x2, blocking collectives, scatter_sum(): got = lax.all_to_all(blocks, axes, 0, 0, tiled=True)  34.2 us
    all_to_all x2, blocking collectives, gather(): lax.all_to_all(jnp.broadcast_to(block[None], (count,) + block.shape), axe...  29.2 us
    all_to_all x2, waiting for transfers between devices, scatter_sum(): got = lax.all_to_all(blocks, axes, 0, 0, tiled=True)  23.1 us
    ppermute x3, starting transfers between devices, from_part(): return lax.ppermute(piece(d1, d2), PART, pairs_part(d1, d2)).astype(f32)  11.4 us
    all_to_all x2, starting transfers between devices, scatter_sum(): got = lax.all_to_all(blocks, axes, 0, 0, tiled=True)  11 us
    ppermute x2, waiting for transfers between devices, from_other_z1(): return lax.ppermute(block, 'z1', SWAP)  10.4 us
    all_to_all x2, starting transfers between devices, gather(): lax.all_to_all(jnp.broadcast_to(block[None], (count,) + block.shape), axe...  10.1 us
    pallas_call x5, Pallas kernels, run(): pl.pallas_call(kernel, out_shape=outs, in_specs=[pl.BlockSpec(memory_spac...  10.1 us
  transfers between devices with their start and end apart: 15, of which 11 were waited for; matrix products, arithmetic and copies ran while one was open for 3% of the time, Pallas kernels for 1%

profile of v7, /device:TPU:1, one launch (start us, length us, event | category | flops | bytes accessed | tf_op | source)
XLA Modules:
  0.0 233.2 jit_solution(13848405966614964878)
XLA Ops:
  9.4 7.3 %collective-permute-start.4 = (bf16[72,576]{1,0:T(8,128)(2,1)S(1)}, bf16[72,576]{1,0:T(8,128)(2,1)S(1)}, u32[]{:S(2)}, u32[]{:S(2)}) collective-permute-start(bf16[72,576]{1,0:T(8,128)(2,1)S(1)} %slice_select_fusion), channel_id=1, source_target_pairs={{0,0},{1,16},{16,64},{17,80},{32,1},{33,17},{48,65},{49,81},{64,32... | collective-permute-start | bytes 248840 | tf_op jit(solution)/shard_map/ppermute | solution.py:187
  16.7 7.1 %collective-permute-done.4 = bf16[72,576]{1,0:T(8,128)(2,1)S(1)} collective-permute-done((bf16[72,576]{1,0:T(8,128)(2,1)S(1)}, bf16[72,576]{1,0:T(8,128)(2,1)S(1)}, u32[]{:S(2)}, u32[]{:S(2)}) %collective-permute-start.4) | collective-permute-done | bytes 82976 | tf_op jit(solution)/shard_map/ppermute | solution.py:187
  24.8 5.8 %all-to-all-start.1 = ((bf16[8,72,576]{2,1,0:T(8,128)(2,1)}), bf16[8,72,576]{2,1,0:T(8,128)(2,1)S(1)}, u32[]{:S(2)}, u32[]{:S(2)}) async-start(bf16[8,72,576]{2,1,0:T(8,128)(2,1)} %broadcast_in_dim.9), calls=%async_computation.1 | async-start | bytes 1474560 | tf_op jit(solution)/shard_map/all_to_all | solution.py:17
  31.0 3.0 %collective-permute-start = (bf16[72,288]{1,0:T(8,128)(2,1)S(1)}, bf16[72,288]{1,0:T(8,128)(2,1)S(1)}, u32[]{:S(2)}, u32[]{:S(2)}) collective-permute-start(bf16[72,288]{1,0:T(8,128)(2,1)S(1)} %get-tuple-element.27), channel_id=1, source_target_pairs={{0,1},{1,0},{64,65},{65,64},{2,3},{3,2},{66,67},{67,66},{4,5},{5,4... | collective-permute-start | bytes 124424 | tf_op jit(solution)/shard_map/ppermute | solution.py:179
  34.1 4.5 %collective-permute-start.2 = (bf16[72,288]{1,0:T(8,128)(2,1)S(1)}, bf16[72,288]{1,0:T(8,128)(2,1)S(1)}, u32[]{:S(2)}, u32[]{:S(2)}) collective-permute-start(bf16[72,288]{1,0:T(8,128)(2,1)S(1)} %get-tuple-element.28), channel_id=1, source_target_pairs={{0,65},{1,64},{64,1},{65,0},{2,67},{3,66},{66,3},{67,2},{4,69},{5,... | collective-permute-start | bytes 124424 | tf_op jit(solution)/shard_map/ppermute | solution.py:179
  38.6 3.8 %collective-permute-start.1 = (bf16[72,288]{1,0:T(8,128)(2,1)S(1)}, bf16[72,288]{1,0:T(8,128)(2,1)S(1)}, u32[]{:S(2)}, u32[]{:S(2)}) collective-permute-start(bf16[72,288]{1,0:T(8,128)(2,1)S(1)} %get-tuple-element.29), channel_id=1, source_target_pairs={{0,64},{1,65},{64,0},{65,1},{2,66},{3,67},{66,2},{67,3},{4,68},{5,... | collective-permute-start | bytes 124424 | tf_op jit(solution)/shard_map/ppermute | solution.py:179
  42.5 4.4 %collective-permute-done.1 = bf16[72,288]{1,0:T(8,128)(2,1)S(1)} collective-permute-done((bf16[72,288]{1,0:T(8,128)(2,1)S(1)}, bf16[72,288]{1,0:T(8,128)(2,1)S(1)}, u32[]{:S(2)}, u32[]{:S(2)}) %collective-permute-start.1) | collective-permute-done | bytes 41504 | tf_op jit(solution)/shard_map/ppermute | solution.py:179
  47.0 6.1 %all-gather.3.cloned.1.call-done = bf16[16,72,576]{2,1,0:T(8,128)(2,1)} async-done(((bf16[2,72,576]{2,1,0:T(8,128)(2,1)}), bf16[16,72,576]{2,1,0:T(8,128)(2,1)}) %all-gather.3.cloned.1.call-update) | async-done | bytes 1327120 | tf_op jit(solution)/shard_map/all_gather | solution.py:169
  54.0 4.3 %all-to-all-start = ((bf16[8,72,576]{2,1,0:T(8,128)(2,1)}), bf16[8,72,576]{2,1,0:T(8,128)(2,1)}, u32[]{:S(2)}, u32[]{:S(2)}) async-start(bf16[8,72,576]{2,1,0:T(8,128)(2,1)} %broadcast_in_dim.8), calls=%async_computation | async-start | bytes 1474560 | tf_op jit(solution)/shard_map/all_to_all | solution.py:17
  58.4 6.8 %collective-permute-start.5 = (bf16[8,72,576]{2,1,0:T(8,128)(2,1)S(1)}, bf16[8,72,576]{2,1,0:T(8,128)(2,1)}, u32[]{:S(2)}, u32[]{:S(2)}) collective-permute-start(bf16[8,72,576]{2,1,0:T(8,128)(2,1)S(1)} %all-to-all-done.1), channel_id=1, source_target_pairs={{0,16},{16,0},{1,17},{17,1},{2,18},{18,2},{3,19},{19,3},{4,20},{20... | collective-permute-start | bytes 1990664 | tf_op jit(solution)/shard_map/ppermute | solution.py:189
  67.0 4.3 %collective-permute-start.3 = (bf16[4,72,576]{2,1,0:T(8,128)(2,1)}, bf16[4,72,576]{2,1,0:T(8,128)(2,1)S(1)}, u32[]{:S(2)}, u32[]{:S(2)}) collective-permute-start(bf16[4,72,576]{2,1,0:T(8,128)(2,1)} %dynamic-slice_bitcast_fusion.1), channel_id=1, source_target_pairs={{0,64},{64,0},{1,65},{65,1},{2,66},{66,2},{3,67},{67,3},{4,68},{68... | collective-permute-start | bytes 995336 | tf_op jit(solution)/shard_map/ppermute | solution.py:196
  71.3 2.2 maximum_select_fusion.basis
  73.5 2.3 all-to-all-done.grad
  75.9 2.3 shard_map.56
  78.2 10.1 %collective-permute-done.3.near = bf16[4,72,576]{2,1,0:T(8,128)(2,1)S(1)} collective-permute-done((bf16[4,72,576]{2,1,0:T(8,128)(2,1)}, bf16[4,72,576]{2,1,0:T(8,128)(2,1)S(1)}, u32[]{:S(2)}, u32[]{:S(2)}) %collective-permute-start.3) | collective-permute-done | bytes 331808 | tf_op jit(solution)/shard_map/ppermute | solution.py:196
  88.3 17.4 %all_to_all.40 = bf16[4,72,576]{2,1,0:T(8,128)(2,1)} all-to-all(bf16[4,72,576]{2,1,0:T(8,128)(2,1)S(1)} %shard_map.56), channel_id=1, replica_groups=mesh['x'=4,'z1'=2,'z0'=2,'c'=2,'y'=8,'z2'=2] {'z1','z2'}, dimensions={0} | all-to-all | bytes 663552 | tf_op jit(solution)/shard_map/all_to_all | solution.py:23
  106.8 12.8 %all_to_all.41.own = bf16[8,72,576]{2,1,0:T(8,128)(2,1)S(1)} all-to-all(bf16[8,72,576]{2,1,0:T(8,128)(2,1)S(1)} %broadcast_in_dim.10), channel_id=1, replica_groups=mesh['x'=4,'z1'=2,'z0'=2,'c'=2,'y'=8,'z2'=2] {'x','z0'}, dimensions={0} | all-to-all | bytes 1327104 | tf_op jit(solution)/shard_map/all_to_all | solution.py:17
  119.6 6.2 %collective-permute-start.7 = (bf16[8,72,576]{2,1,0:T(8,128)(2,1)S(1)}, bf16[8,72,576]{2,1,0:T(8,128)(2,1)S(1)}, u32[]{:S(2)}, u32[]{:S(2)}) collective-permute-start(bf16[8,72,576]{2,1,0:T(8,128)(2,1)S(1)} %all_to_all.41.own), channel_id=1, source_target_pairs={{0,16},{16,0},{1,17},{17,1},{2,18},{18,2},{3,19},{19,3},{4,20},{20... | collective-permute-start | bytes 1990664 | tf_op jit(solution)/shard_map/ppermute | solution.py:206
  125.9 1.8 collective-permute-done.7.other
  129.6 4.1 %all-to-all-start.4 = ((bf16[4,72,576]{2,1,0:T(8,128)(2,1)}), bf16[4,72,576]{2,1,0:T(8,128)(2,1)}, u32[]{:S(2)}, u32[]{:S(2)}) async-start(bf16[4,72,576]{2,1,0:T(8,128)(2,1)} %copy-done.2), calls=%async_computation.4 | async-start | bytes 737280 | tf_op jit(solution)/shard_map/all_to_all | solution.py:23
  135.2 8.7 %all-to-all-done.4 = bf16[4,72,576]{2,1,0:T(8,128)(2,1)} async-done(((bf16[4,72,576]{2,1,0:T(8,128)(2,1)}), bf16[4,72,576]{2,1,0:T(8,128)(2,1)}, u32[]{:S(2)}, u32[]{:S(2)}) %all-to-all-start.4) | async-done | bytes 331808 | tf_op jit(solution)/shard_map/all_to_all | solution.py:23
  145.1 16.4 %all_to_all.42.scaled = bf16[4,72,576]{2,1,0:T(8,128)(2,1)S(1)} all-to-all(bf16[4,72,576]{2,1,0:T(8,128)(2,1)S(1)} %broadcast_in_dim.11), channel_id=1, replica_groups=mesh['x'=4,'z1'=2,'z0'=2,'c'=2,'y'=8,'z2'=2] {'z1','z2'}, dimensions={0} | all-to-all | bytes 663552 | tf_op jit(solution)/shard_map/all_to_all | solution.py:17
  161.5 2.6 %shard_map.58 = bf16[8,72,576]{2,1,0:T(8,128)(2,1)S(1)} custom-call(bf16[4,72,576]{2,1,0:T(8,128)(2,1)S(1)} %all_to_all.42.scaled, bf16[8,144,576]{2,1,0:T(8,128)(2,1)S(1)} %maximum_select_fusion.basis), custom_call_target="tpu_custom_call" | custom-call | flops 382205952 | bytes 2322432 | tf_op jit(solution)/shard_map/pallas_call | solution.py:62
  165.0 6.9 %all-to-all-start.6 = ((bf16[8,72,576]{2,1,0:T(8,128)(2,1)}), bf16[8,72,576]{2,1,0:T(8,128)(2,1)S(1)}, u32[]{:S(2)}, u32[]{:S(2)}) async-start(bf16[8,72,576]{2,1,0:T(8,128)(2,1)} %copy-done.1), calls=%async_computation.6 | async-start | bytes 1474560 | tf_op jit(solution)/shard_map/all_to_all | solution.py:23
  172.9 3.9 %collective-permute-start.6 = (bf16[4,72,576]{2,1,0:T(8,128)(2,1)S(1)}, bf16[4,72,576]{2,1,0:T(8,128)(2,1)S(1)}, u32[]{:S(2)}, u32[]{:S(2)}) collective-permute-start(bf16[4,72,576]{2,1,0:T(8,128)(2,1)S(1)} %dynamic-slice_bitcast_fusion), channel_id=1, source_target_pairs={{0,64},{64,0},{1,65},{65,1},{2,66},{66,2},{3,67},{67,3},{4,68},{68... | collective-permute-start | bytes 995336 | tf_op jit(solution)/shard_map/ppermute | solution.py:196
  176.8 14.4 %all-to-all-done.6 = bf16[8,72,576]{2,1,0:T(8,128)(2,1)S(1)} async-done(((bf16[8,72,576]{2,1,0:T(8,128)(2,1)}), bf16[8,72,576]{2,1,0:T(8,128)(2,1)S(1)}, u32[]{:S(2)}, u32[]{:S(2)}) %all-to-all-start.6) | async-done | bytes 663584 | tf_op jit(solution)/shard_map/all_to_all | solution.py:23
  191.8 3.8 %collective-permute-start.8 = (bf16[72,576]{1,0:T(8,128)(2,1)S(1)}, bf16[72,576]{1,0:T(8,128)(2,1)S(1)}, u32[]{:S(2)}, u32[]{:S(2)}) collective-permute-start(bf16[72,576]{1,0:T(8,128)(2,1)S(1)} %reduce_sum.47.mine), channel_id=1, source_target_pairs={{0,64},{64,0},{1,65},{65,1},{2,66},{66,2},{3,67},{67,3},{4,68},{68... | collective-permute-start | bytes 248840 | tf_op jit(solution)/shard_map/ppermute | solution.py:220
  195.6 2.4 %collective-permute-done.8.other = bf16[72,576]{1,0:T(8,128)(2,1)S(1)} collective-permute-done((bf16[72,576]{1,0:T(8,128)(2,1)S(1)}, bf16[72,576]{1,0:T(8,128)(2,1)S(1)}, u32[]{:S(2)}, u32[]{:S(2)}) %collective-permute-start.8) | collective-permute-done | bytes 82976 | tf_op jit(solution)/shard_map/ppermute | solution.py:220
  198.0 2.4 %shard_map.59 = (bf16[8,72,576]{2,1,0:T(8,128)(2,1)S(1)}, bf16[8,72,576]{2,1,0:T(8,128)(2,1)S(1)}) custom-call(s32[1]{0:T(128)} %bitcast.part, bf16[8,2,72,576]{3,2,1,0:T(8,128)(2,1)S(1)} %bitcast.33, bf16[4,72,576]{2,1,0:T(8,128)(2,1)S(1)} %collective-permute-done.3.near, bf16[4,72,576]{2,1,0:T(8,128)(2,1)S(1)} %collective-permute-done.6.far, ...), custom_call_target="tpu_custom_call" | custom-call | flops 382205952 | bytes 3483652 | tf_op jit(solution)/shard_map/pallas_call | solution.py:62
  200.3 6.4 %collective-permute-start.9 = (bf16[8,72,576]{2,1,0:T(8,128)(2,1)S(1)}, bf16[8,72,576]{2,1,0:T(8,128)(2,1)S(1)}, u32[]{:S(2)}, u32[]{:S(2)}) collective-permute-start(bf16[8,72,576]{2,1,0:T(8,128)(2,1)S(1)} %get-tuple-element.24), channel_id=1, source_target_pairs={{0,16},{16,0},{1,17},{17,1},{2,18},{18,2},{3,19},{19,3},{4,20},{20... | collective-permute-start | bytes 1990664 | tf_op jit(solution)/shard_map/ppermute | solution.py:229
  206.7 1.8 collective-permute-done.9
  208.7 16.8 %all_to_all.43 = bf16[8,72,576]{2,1,0:T(8,128)(2,1)S(1)} all-to-all(bf16[8,72,576]{2,1,0:T(8,128)(2,1)S(1)} %add_convert_fusion), channel_id=1, replica_groups=mesh['x'=4,'z1'=2,'z0'=2,'c'=2,'y'=8,'z2'=2] {'x','z0'}, dimensions={0} | all-to-all | bytes 1327104 | tf_op jit(solution)/shard_map/all_to_all | solution.py:23
  (50 shorter events, 16.1 us)
Async XLA Ops:
  6.5 46.6 %all-gather.3.cloned.1.call-start = ((), (), s32[]{:S(2)}) async-start(), calls=%async_computation.8 | async-start | bytes 1658880 | tf_op jit(solution)/shard_map/all_gather | solution.py:169
  6.5 1.0 copy-start.3
  7.5 1.8 copy-start.6
  9.3 21.3 %copy-start.5 = (bf16[1,144,576]{2,1,0:T(8,128)(2,1)S(1)}, bf16[1,144,576]{2,1,0:T(8,128)(2,1)}, u32[]{:S(2)}) copy-start(bf16[1,144,576]{2,1,0:T(8,128)(2,1)} %param.5) | copy-start | bytes 497668
  9.4 14.5 %collective-permute-start.4 = (bf16[72,576]{1,0:T(8,128)(2,1)S(1)}, bf16[72,576]{1,0:T(8,128)(2,1)S(1)}, u32[]{:S(2)}, u32[]{:S(2)}) collective-permute-start(bf16[72,576]{1,0:T(8,128)(2,1)S(1)} %slice_select_fusion), channel_id=1, source_target_pairs={{0,0},{1,16},{16,64},{17,80},{32,1},{33,17},{48,65},{49,81},{64,32... | collective-permute-start | bytes 248840 | tf_op jit(solution)/shard_map/ppermute | solution.py:187
  24.8 28.3 %all-to-all-start.1 = ((bf16[8,72,576]{2,1,0:T(8,128)(2,1)}), bf16[8,72,576]{2,1,0:T(8,128)(2,1)S(1)}, u32[]{:S(2)}, u32[]{:S(2)}) async-start(bf16[8,72,576]{2,1,0:T(8,128)(2,1)} %broadcast_in_dim.9), calls=%async_computation.1 | async-start | bytes 1474560 | tf_op jit(solution)/shard_map/all_to_all | solution.py:17
  31.0 11.4 %collective-permute-start = (bf16[72,288]{1,0:T(8,128)(2,1)S(1)}, bf16[72,288]{1,0:T(8,128)(2,1)S(1)}, u32[]{:S(2)}, u32[]{:S(2)}) collective-permute-start(bf16[72,288]{1,0:T(8,128)(2,1)S(1)} %get-tuple-element.27), channel_id=1, source_target_pairs={{0,1},{1,0},{64,65},{65,64},{2,3},{3,2},{66,67},{67,66},{4,5},{5,4... | collective-permute-start | bytes 124424 | tf_op jit(solution)/shard_map/ppermute | solution.py:179
  34.1 8.4 %collective-permute-start.2 = (bf16[72,288]{1,0:T(8,128)(2,1)S(1)}, bf16[72,288]{1,0:T(8,128)(2,1)S(1)}, u32[]{:S(2)}, u32[]{:S(2)}) collective-permute-start(bf16[72,288]{1,0:T(8,128)(2,1)S(1)} %get-tuple-element.28), channel_id=1, source_target_pairs={{0,65},{1,64},{64,1},{65,0},{2,67},{3,66},{66,3},{67,2},{4,69},{5,... | collective-permute-start | bytes 124424 | tf_op jit(solution)/shard_map/ppermute | solution.py:179
  38.6 8.2 %collective-permute-start.1 = (bf16[72,288]{1,0:T(8,128)(2,1)S(1)}, bf16[72,288]{1,0:T(8,128)(2,1)S(1)}, u32[]{:S(2)}, u32[]{:S(2)}) collective-permute-start(bf16[72,288]{1,0:T(8,128)(2,1)S(1)} %get-tuple-element.29), channel_id=1, source_target_pairs={{0,64},{1,65},{64,0},{65,1},{2,66},{3,67},{66,2},{67,3},{4,68},{5,... | collective-permute-start | bytes 124424 | tf_op jit(solution)/shard_map/ppermute | solution.py:179
  53.1 12.1 %copy-start = (bf16[16,72,576]{2,1,0:T(8,128)(2,1)S(1)}, bf16[16,72,576]{2,1,0:T(8,128)(2,1)}, u32[]{:S(2)}) copy-start(bf16[16,72,576]{2,1,0:T(8,128)(2,1)} %all-gather.3.cloned.1.call-done) | copy-start | bytes 3981316
  53.1 13.1 %copy-start.4 = (bf16[8,72,576]{2,1,0:T(8,128)(2,1)}, bf16[8,72,576]{2,1,0:T(8,128)(2,1)S(1)}, u32[]{:S(2)}) copy-start(bf16[8,72,576]{2,1,0:T(8,128)(2,1)S(1)} %all-to-all-done.1) | copy-start | bytes 1990660
  54.0 21.8 %all-to-all-start = ((bf16[8,72,576]{2,1,0:T(8,128)(2,1)}), bf16[8,72,576]{2,1,0:T(8,128)(2,1)}, u32[]{:S(2)}, u32[]{:S(2)}) async-start(bf16[8,72,576]{2,1,0:T(8,128)(2,1)} %broadcast_in_dim.8), calls=%async_computation | async-start | bytes 1474560 | tf_op jit(solution)/shard_map/all_to_all | solution.py:17
  58.4 12.9 %collective-permute-start.5 = (bf16[8,72,576]{2,1,0:T(8,128)(2,1)S(1)}, bf16[8,72,576]{2,1,0:T(8,128)(2,1)}, u32[]{:S(2)}, u32[]{:S(2)}) collective-permute-start(bf16[8,72,576]{2,1,0:T(8,128)(2,1)S(1)} %all-to-all-done.1), channel_id=1, source_target_pairs={{0,16},{16,0},{1,17},{17,1},{2,18},{18,2},{3,19},{19,3},{4,20},{20... | collective-permute-start | bytes 1990664 | tf_op jit(solution)/shard_map/ppermute | solution.py:189
  67.0 21.2 %collective-permute-start.3 = (bf16[4,72,576]{2,1,0:T(8,128)(2,1)}, bf16[4,72,576]{2,1,0:T(8,128)(2,1)S(1)}, u32[]{:S(2)}, u32[]{:S(2)}) collective-permute-start(bf16[4,72,576]{2,1,0:T(8,128)(2,1)} %dynamic-slice_bitcast_fusion.1), channel_id=1, source_target_pairs={{0,64},{64,0},{1,65},{65,1},{2,66},{66,2},{3,67},{67,3},{4,68},{68... | collective-permute-start | bytes 995336 | tf_op jit(solution)/shard_map/ppermute | solution.py:196
  119.6 8.1 %collective-permute-start.7 = (bf16[8,72,576]{2,1,0:T(8,128)(2,1)S(1)}, bf16[8,72,576]{2,1,0:T(8,128)(2,1)S(1)}, u32[]{:S(2)}, u32[]{:S(2)}) collective-permute-start(bf16[8,72,576]{2,1,0:T(8,128)(2,1)S(1)} %all_to_all.41.own), channel_id=1, source_target_pairs={{0,16},{16,0},{1,17},{17,1},{2,18},{18,2},{3,19},{19,3},{4,20},{20... | collective-permute-start | bytes 1990664 | tf_op jit(solution)/shard_map/ppermute | solution.py:206
  128.8 0.7 copy-start.2
  129.6 14.3 %all-to-all-start.4 = ((bf16[4,72,576]{2,1,0:T(8,128)(2,1)}), bf16[4,72,576]{2,1,0:T(8,128)(2,1)}, u32[]{:S(2)}, u32[]{:S(2)}) async-start(bf16[4,72,576]{2,1,0:T(8,128)(2,1)} %copy-done.2), calls=%async_computation.4 | async-start | bytes 737280 | tf_op jit(solution)/shard_map/all_to_all | solution.py:23
  164.1 0.9 copy-start.1
  165.0 26.3 %all-to-all-start.6 = ((bf16[8,72,576]{2,1,0:T(8,128)(2,1)}), bf16[8,72,576]{2,1,0:T(8,128)(2,1)S(1)}, u32[]{:S(2)}, u32[]{:S(2)}) async-start(bf16[8,72,576]{2,1,0:T(8,128)(2,1)} %copy-done.1), calls=%async_computation.6 | async-start | bytes 1474560 | tf_op jit(solution)/shard_map/all_to_all | solution.py:23
  172.9 18.9 %collective-permute-start.6 = (bf16[4,72,576]{2,1,0:T(8,128)(2,1)S(1)}, bf16[4,72,576]{2,1,0:T(8,128)(2,1)S(1)}, u32[]{:S(2)}, u32[]{:S(2)}) collective-permute-start(bf16[4,72,576]{2,1,0:T(8,128)(2,1)S(1)} %dynamic-slice_bitcast_fusion), channel_id=1, source_target_pairs={{0,64},{64,0},{1,65},{65,1},{2,66},{66,2},{3,67},{67,3},{4,68},{68... | collective-permute-start | bytes 995336 | tf_op jit(solution)/shard_map/ppermute | solution.py:196
  191.8 6.2 %collective-permute-start.8 = (bf16[72,576]{1,0:T(8,128)(2,1)S(1)}, bf16[72,576]{1,0:T(8,128)(2,1)S(1)}, u32[]{:S(2)}, u32[]{:S(2)}) collective-permute-start(bf16[72,576]{1,0:T(8,128)(2,1)S(1)} %reduce_sum.47.mine), channel_id=1, source_target_pairs={{0,64},{64,0},{1,65},{65,1},{2,66},{66,2},{3,67},{67,3},{4,68},{68... | collective-permute-start | bytes 248840 | tf_op jit(solution)/shard_map/ppermute | solution.py:220
  200.3 8.2 %collective-permute-start.9 = (bf16[8,72,576]{2,1,0:T(8,128)(2,1)S(1)}, bf16[8,72,576]{2,1,0:T(8,128)(2,1)S(1)}, u32[]{:S(2)}, u32[]{:S(2)}) collective-permute-start(bf16[8,72,576]{2,1,0:T(8,128)(2,1)S(1)} %get-tuple-element.24), channel_id=1, source_target_pairs={{0,16},{16,0},{1,17},{17,1},{2,18},{18,2},{3,19},{19,3},{4,20},{20... | collective-permute-start | bytes 1990664 | tf_op jit(solution)/shard_map/ppermute | solution.py:229
Sparse Core Ops, SparseCore 0:
  9.4 43.6 all-gather.2

commit v8 on v6

--- a/solution.py
+++ b/solution.py
@@ -165,7 +165,14 @@
     core, rep, part_z1 = (i.astype(jnp.int32).reshape(1) for i in (c, z2, z1))
 
     bo = run(order_out, shape(2, half, cols), (core, rep, basis_out), flags=2)
+    bo, grad_parts, basis_in = lax.optimization_barrier((bo, grad_parts, basis_in))
     bo = lax.ppermute(bo, ("z1", "y"), pairs_z1y0())
+
+    bi = basis_in.astype(bf16)
+    bi = jnp.where(low_rep, bi[:half], bi[half:])
+    bi = lax.ppermute(bi, ("z1", "z0", "c", "z2"), pairs_rows())
+    bo, bi = lax.optimization_barrier((bo, bi))
+    bo = lax.all_gather(bo, "y", axis=0)
 
     grad = grad_parts[0]
     parts = jnp.stack([pack(grad[:, i * quarter : (i + 1) * quarter]) for i in range(4)])
@@ -181,20 +188,15 @@
     other = (from_part(1, 0) + from_part(1, 1)).astype(bf16)
     grad = in_order(low_z1, mine, other, 1)
 
-    bi = basis_in.astype(bf16)
-    bi = jnp.where(low_rep, bi[:half], bi[half:])
-    bi = lax.ppermute(bi, ("z1", "z0", "c", "z2"), pairs_rows())
     bi = gather(bi, RING, 8)
     bi = in_order(low_core, bi, lax.ppermute(bi, "c", SWAP), 1)
 
-    bo, grad = lax.optimization_barrier((bo, grad))
     grad = gather(grad, "y", 8)
-    bo, grad = lax.optimization_barrier((bo, grad))
-    bo = lax.all_gather(bo, "y", axis=0)
 
     left = (4, half, 8 * quarter)
     part = run(turn_in, shape(4, half, cols), (grad, bi), (left,))
     turned = scatter_sum(part, PART).astype(bf16)
+    bo, turned = lax.optimization_barrier((bo, turned))
     turned = gather(turned, RING, 8)
     other = lax.ppermute(turned, "c", SWAP)
 

time: 228 us -> 229 us (level)
  blocking collectives: 64.7 us -> 88.1 us
  starting transfers between devices: 79.5 us -> 61.3 us
  waiting for transfers between devices: 49.9 us -> 47.5 us
    all_to_all x2 -> x3, blocking collectives: 33.8 us -> 51.2 us  [scatter_sum(): got = lax.all_to_all(blocks, axes, 0, 0, tiled=True)]
    all_to_all x2, waiting for transfers between devices: 9.31 us -> 20 us  [gather(): lax.all_to_all(jnp.broadcast_to(block[None], (count,) + block.shape), axe...]
    all_gather x1, waiting for transfers between devices: 9.6 us -> 0.02 us  [body(): bo = lax.all_gather(bo, 'y', axis=0)]
    all_to_all x2 -> x1, starting transfers between devices: 12.3 us -> 3.46 us  [scatter_sum(): got = lax.all_to_all(blocks, axes, 0, 0, tiled=True)]
    all_to_all x2 -> x1, waiting for transfers between devices: 14.9 us -> 8.01 us  [scatter_sum(): got = lax.all_to_all(blocks, axes, 0, 0, tiled=True)]
    all_to_all x2, blocking collectives: 30.9 us -> 37 us  [gather(): lax.all_to_all(jnp.broadcast_to(block[None], (count,) + block.shape), axe...]
    ppermute x1, starting transfers between devices: 11.7 us -> 5.83 us  [body(): lax.ppermute(give, 'c', SWAP).astype(f32)]
    all_to_all x2, starting transfers between devices: 19.7 us -> 14.8 us  [gather(): lax.all_to_all(jnp.broadcast_to(block[None], (count,) + block.shape), axe...]
  transfers between devices with their start and end apart: 14 -> 13, of which waited for: 8 -> 9; matrix products, arithmetic and copies ran while one was open for 1% -> 2% of each run, Pallas kernels for 0% -> 1%
where the time goes in v8:
time: 229 us; the launch traced here: 228 us
  blocking collectives  88.1 us (38%)
  starting transfers between devices  61.3 us (27%)
  waiting for transfers between devices  47.5 us (21%)
  between operations  13.7 us (6%)
  Pallas kernels  8.98 us (4%)
  local copies, waits for them, and re-layouts  4.74 us (2%)
  other arithmetic  3.66 us (2%)
    all_to_all x3, blocking collectives, scatter_sum(): got = lax.all_to_all(blocks, axes, 0, 0, tiled=True)  51.2 us
    all_to_all x2, blocking collectives, gather(): lax.all_to_all(jnp.broadcast_to(block[None], (count,) + block.shape), axe...  37 us
    all_to_all x2, waiting for transfers between devices, gather(): lax.all_to_all(jnp.broadcast_to(block[None], (count,) + block.shape), axe...  20 us
    all_to_all x2, starting transfers between devices, gather(): lax.all_to_all(jnp.broadcast_to(block[None], (count,) + block.shape), axe...  14.8 us
    ppermute x3, starting transfers between devices, from_part(): return lax.ppermute(piece(d1, d2), PART, pairs_part(d1, d2)).astype(f32)  12.9 us
    pallas_call x5, Pallas kernels, run(): pl.pallas_call(kernel, out_shape=outs, in_specs=[pl.BlockSpec(memory_spac...  8.98 us
    ppermute x1, starting transfers between devices, body(): bi = lax.ppermute(bi, ('z1', 'z0', 'c', 'z2'), pairs_rows())  8.45 us
    all_to_all x1, waiting for transfers between devices, scatter_sum(): got = lax.all_to_all(blocks, axes, 0, 0, tiled=True)  8.01 us
  transfers between devices with their start and end apart: 13, of which 9 were waited for; matrix products, arithmetic and copies ran while one was open for 2% of the time, Pallas kernels for 1%

profile of v8, /device:TPU:1, one launch (start us, length us, event | category | flops | bytes accessed | tf_op | source)
XLA Modules:
  0.0 228.0 jit_solution(17719917446336322437)
XLA Ops:
  6.5 1.0 copy-done.1
  7.5 1.1 shard_map.55
  9.5 8.4 %collective-permute-start.1 = (bf16[72,576]{1,0:T(8,128)(2,1)S(1)}, bf16[72,576]{1,0:T(8,128)(2,1)S(1)}, u32[]{:S(2)}, u32[]{:S(2)}) collective-permute-start(bf16[72,576]{1,0:T(8,128)(2,1)S(1)} %slice_select_fusion), channel_id=1, source_target_pairs={{0,0},{1,16},{16,64},{17,80},{32,1},{33,17},{48,65},{49,81},{64,32... | collective-permute-start | bytes 248840 | tf_op jit(solution)/shard_map/ppermute | solution.py:173
  18.0 6.4 %collective-permute-done.1 = bf16[72,576]{1,0:T(8,128)(2,1)S(1)} collective-permute-done((bf16[72,576]{1,0:T(8,128)(2,1)S(1)}, bf16[72,576]{1,0:T(8,128)(2,1)S(1)}, u32[]{:S(2)}, u32[]{:S(2)}) %collective-permute-start.1) | collective-permute-done | bytes 82976 | tf_op jit(solution)/shard_map/ppermute | solution.py:173
  25.3 7.8 %all-to-all-start.1 = ((bf16[8,72,576]{2,1,0:T(8,128)(2,1)}), bf16[8,72,576]{2,1,0:T(8,128)(2,1)S(1)}, u32[]{:S(2)}, u32[]{:S(2)}) async-start(bf16[8,72,576]{2,1,0:T(8,128)(2,1)} %broadcast_in_dim.9), calls=%async_computation.1 | async-start | bytes 1474560 | tf_op jit(solution)/shard_map/all_to_all | solution.py:17
  33.9 7.2 %collective-permute-start.2 = (bf16[72,288]{1,0:T(8,128)(2,1)S(1)}, bf16[72,288]{1,0:T(8,128)(2,1)S(1)}, u32[]{:S(2)}, u32[]{:S(2)}) collective-permute-start(bf16[72,288]{1,0:T(8,128)(2,1)S(1)} %get-tuple-element.23), channel_id=1, source_target_pairs={{0,1},{1,0},{64,65},{65,64},{2,3},{3,2},{66,67},{67,66},{4,5},{5,4... | collective-permute-start | bytes 124424 | tf_op jit(solution)/shard_map/ppermute | solution.py:185
  41.1 3.8 %collective-permute-start.3 = (bf16[72,288]{1,0:T(8,128)(2,1)S(1)}, bf16[72,288]{1,0:T(8,128)(2,1)S(1)}, u32[]{:S(2)}, u32[]{:S(2)}) collective-permute-start(bf16[72,288]{1,0:T(8,128)(2,1)S(1)} %get-tuple-element.25), channel_id=1, source_target_pairs={{0,64},{1,65},{64,0},{65,1},{2,66},{3,67},{66,2},{67,3},{4,68},{5,... | collective-permute-start | bytes 124424 | tf_op jit(solution)/shard_map/ppermute | solution.py:185
  45.0 1.9 collective-permute-start.4
  46.9 3.2 %collective-permute-done.2 = bf16[72,288]{1,0:T(8,128)(2,1)S(1)} collective-permute-done((bf16[72,288]{1,0:T(8,128)(2,1)S(1)}, bf16[72,288]{1,0:T(8,128)(2,1)S(1)}, u32[]{:S(2)}, u32[]{:S(2)}) %collective-permute-start.2) | collective-permute-done | bytes 41504 | tf_op jit(solution)/shard_map/ppermute | solution.py:185
  50.1 2.1 collective-permute-done.4
  53.3 7.0 %all-to-all-start = ((bf16[8,72,576]{2,1,0:T(8,128)(2,1)}), bf16[8,72,576]{2,1,0:T(8,128)(2,1)S(1)}, u32[]{:S(2)}, u32[]{:S(2)}) async-start(bf16[8,72,576]{2,1,0:T(8,128)(2,1)} %broadcast_in_dim.8), calls=%async_computation | async-start | bytes 1474560 | tf_op jit(solution)/shard_map/all_to_all | solution.py:17
  60.2 4.5 %collective-permute-start.5 = (bf16[8,72,576]{2,1,0:T(8,128)(2,1)S(1)}, bf16[8,72,576]{2,1,0:T(8,128)(2,1)}, u32[]{:S(2)}, u32[]{:S(2)}) collective-permute-start(bf16[8,72,576]{2,1,0:T(8,128)(2,1)S(1)} %all-to-all-done.1), channel_id=1, source_target_pairs={{0,16},{16,0},{1,17},{17,1},{2,18},{18,2},{3,19},{19,3},{4,20},{20... | collective-permute-start | bytes 1990664 | tf_op jit(solution)/shard_map/ppermute | solution.py:192
  64.7 1.9 collective-permute-done.5
  66.7 1.9 maximum_select_fusion.basis
  68.6 20.0 %all-to-all-done.grad = bf16[8,72,576]{2,1,0:T(8,128)(2,1)S(1)} async-done(((bf16[8,72,576]{2,1,0:T(8,128)(2,1)}), bf16[8,72,576]{2,1,0:T(8,128)(2,1)S(1)}, u32[]{:S(2)}, u32[]{:S(2)}) %all-to-all-start) | async-done | bytes 663584 | tf_op jit(solution)/shard_map/all_to_all | solution.py:17
  88.6 1.1 shard_map.56
  89.7 14.3 %all_to_all.40 = bf16[4,72,576]{2,1,0:T(8,128)(2,1)S(1)} all-to-all(bf16[4,72,576]{2,1,0:T(8,128)(2,1)S(1)} %shard_map.56), channel_id=1, replica_groups=mesh['x'=4,'z1'=2,'z0'=2,'c'=2,'y'=8,'z2'=2] {'z1','z2'}, dimensions={0} | all-to-all | bytes 663552 | tf_op jit(solution)/shard_map/all_to_all | solution.py:23
  104.2 18.9 %all_to_all.41.own = bf16[8,72,576]{2,1,0:T(8,128)(2,1)S(1)} all-to-all(bf16[8,72,576]{2,1,0:T(8,128)(2,1)S(1)} %broadcast_in_dim.10), channel_id=1, replica_groups=mesh['x'=4,'z1'=2,'z0'=2,'c'=2,'y'=8,'z2'=2] {'x','z0'}, dimensions={0} | all-to-all | bytes 1327104 | tf_op jit(solution)/shard_map/all_to_all | solution.py:17
  123.1 5.0 %collective-permute-start.6 = (bf16[8,72,576]{2,1,0:T(8,128)(2,1)S(1)}, bf16[8,72,576]{2,1,0:T(8,128)(2,1)S(1)}, u32[]{:S(2)}, u32[]{:S(2)}) collective-permute-start(bf16[8,72,576]{2,1,0:T(8,128)(2,1)S(1)} %all_to_all.41.own), channel_id=1, source_target_pairs={{0,16},{16,0},{1,17},{17,1},{2,18},{18,2},{3,19},{19,3},{4,20},{20... | collective-permute-start | bytes 1990664 | tf_op jit(solution)/shard_map/ppermute | solution.py:201
  128.1 1.8 collective-permute-done.6.other
  129.9 1.9 shard_map.57
  131.8 3.5 %all-to-all-start.4 = ((bf16[4,72,576]{2,1,0:T(8,128)(2,1)}), bf16[4,72,576]{2,1,0:T(8,128)(2,1)S(1)}, u32[]{:S(2)}, u32[]{:S(2)}) async-start(bf16[4,72,576]{2,1,0:T(8,128)(2,1)} %shard_map.57), calls=%async_computation.4 | async-start | bytes 737280 | tf_op jit(solution)/shard_map/all_to_all | solution.py:23
  136.8 8.0 %all-to-all-done.4 = bf16[4,72,576]{2,1,0:T(8,128)(2,1)S(1)} async-done(((bf16[4,72,576]{2,1,0:T(8,128)(2,1)}), bf16[4,72,576]{2,1,0:T(8,128)(2,1)S(1)}, u32[]{:S(2)}, u32[]{:S(2)}) %all-to-all-start.4) | async-done | bytes 331808 | tf_op jit(solution)/shard_map/all_to_all | solution.py:23
  145.0 18.1 %all_to_all.42.scaled = bf16[4,72,576]{2,1,0:T(8,128)(2,1)S(1)} all-to-all(bf16[4,72,576]{2,1,0:T(8,128)(2,1)S(1)} %broadcast_in_dim.11), channel_id=1, replica_groups=mesh['x'=4,'z1'=2,'z0'=2,'c'=2,'y'=8,'z2'=2] {'z1','z2'}, dimensions={0} | all-to-all | bytes 663552 | tf_op jit(solution)/shard_map/all_to_all | solution.py:17
  163.1 2.5 %shard_map.58 = bf16[8,72,576]{2,1,0:T(8,128)(2,1)S(1)} custom-call(bf16[4,72,576]{2,1,0:T(8,128)(2,1)S(1)} %all_to_all.42.scaled, bf16[8,144,576]{2,1,0:T(8,128)(2,1)S(1)} %maximum_select_fusion.basis), custom_call_target="tpu_custom_call" | custom-call | flops 382205952 | bytes 2322432 | tf_op jit(solution)/shard_map/pallas_call | solution.py:66
  165.6 21.5 %all_to_all.43 = bf16[8,72,576]{2,1,0:T(8,128)(2,1)S(1)} all-to-all(bf16[8,72,576]{2,1,0:T(8,128)(2,1)S(1)} %shard_map.58), channel_id=1, replica_groups=mesh['x'=4,'z1'=2,'z0'=2,'c'=2,'y'=8,'z2'=2] {'y'}, dimensions={0} | all-to-all | bytes 1327104 | tf_op jit(solution)/shard_map/all_to_all | solution.py:23
  187.2 5.5 %collective-permute-start.7 = (bf16[72,576]{1,0:T(8,128)(2,1)S(1)}, bf16[72,576]{1,0:T(8,128)(2,1)S(1)}, u32[]{:S(2)}, u32[]{:S(2)}) collective-permute-start(bf16[72,576]{1,0:T(8,128)(2,1)S(1)} %reduce_sum.47.mine), channel_id=1, source_target_pairs={{0,64},{64,0},{1,65},{65,1},{2,66},{66,2},{3,67},{67,3},{4,68},{68... | collective-permute-start | bytes 248840 | tf_op jit(solution)/shard_map/ppermute | solution.py:214
  192.7 1.9 collective-permute-done.7.other
  194.7 2.3 %shard_map.59 = (bf16[8,72,576]{2,1,0:T(8,128)(2,1)S(1)}, bf16[8,72,576]{2,1,0:T(8,128)(2,1)S(1)}) custom-call(s32[1]{0:T(128)} %bitcast.part, bf16[8,2,72,576]{3,2,1,0:T(8,128)(2,1)S(1)} %bitcast.23, bf16[72,576]{1,0:T(8,128)(2,1)S(1)} %reduce_sum.47.mine, bf16[72,576]{1,0:T(8,128)(2,1)S(1)} %collective-permute-done.7.other), custom_call_target="tpu_custom_call" | custom-call | flops 382205952 | bytes 2820100 | tf_op jit(solution)/shard_map/pallas_call | solution.py:66
  197.0 5.8 %collective-permute-start.8 = (bf16[8,72,576]{2,1,0:T(8,128)(2,1)S(1)}, bf16[8,72,576]{2,1,0:T(8,128)(2,1)S(1)}, u32[]{:S(2)}, u32[]{:S(2)}) collective-permute-start(bf16[8,72,576]{2,1,0:T(8,128)(2,1)S(1)} %get-tuple-element.22), channel_id=1, source_target_pairs={{0,16},{16,0},{1,17},{17,1},{2,18},{18,2},{3,19},{19,3},{4,20},{20... | collective-permute-start | bytes 1990664 | tf_op jit(solution)/shard_map/ppermute | solution.py:223
  202.9 1.8 collective-permute-done.8
  204.9 15.3 %all_to_all.44 = bf16[8,72,576]{2,1,0:T(8,128)(2,1)S(1)} all-to-all(bf16[8,72,576]{2,1,0:T(8,128)(2,1)S(1)} %add_convert_fusion), channel_id=1, replica_groups=mesh['x'=4,'z1'=2,'z0'=2,'c'=2,'y'=8,'z2'=2] {'x','z0'}, dimensions={0} | all-to-all | bytes 1327104 | tf_op jit(solution)/shard_map/all_to_all | solution.py:23
  (40 shorter events, 6.6 us)
Async XLA Ops:
  6.5 1.0 copy-start.1
  7.5 1.9 copy-start.3
  8.6 24.6 %copy-start.2 = (bf16[1,144,576]{2,1,0:T(8,128)(2,1)S(1)}, bf16[1,144,576]{2,1,0:T(8,128)(2,1)}, u32[]{:S(2)}) copy-start(bf16[1,144,576]{2,1,0:T(8,128)(2,1)} %param.5) | copy-start | bytes 497668
  8.6 15.8 %collective-permute-start = (bf16[2,72,576]{2,1,0:T(8,128)(2,1)S(1)}, bf16[2,72,576]{2,1,0:T(8,128)(2,1)S(1)}, u32[]{:S(2)}, u32[]{:S(2)}) collective-permute-start(bf16[2,72,576]{2,1,0:T(8,128)(2,1)S(1)} %shard_map.55), channel_id=1, source_target_pairs={{0,0},{2,64},{4,4},{6,68},{8,8},{10,72},{12,12},{14,76},{64,2},{66... | collective-permute-start | bytes 497672 | tf_op jit(solution)/shard_map/ppermute | solution.py:169
  9.5 14.9 %collective-permute-start.1 = (bf16[72,576]{1,0:T(8,128)(2,1)S(1)}, bf16[72,576]{1,0:T(8,128)(2,1)S(1)}, u32[]{:S(2)}, u32[]{:S(2)}) collective-permute-start(bf16[72,576]{1,0:T(8,128)(2,1)S(1)} %slice_select_fusion), channel_id=1, source_target_pairs={{0,0},{1,16},{16,64},{17,80},{32,1},{33,17},{48,65},{49,81},{64,32... | collective-permute-start | bytes 248840 | tf_op jit(solution)/shard_map/ppermute | solution.py:173
  24.4 9.1 %copy-start.4 = (bf16[2,72,576]{2,1,0:T(8,128)(2,1)}, bf16[2,72,576]{2,1,0:T(8,128)(2,1)S(1)}, u32[]{:S(2)}) copy-start(bf16[2,72,576]{2,1,0:T(8,128)(2,1)S(1)} %collective-permute-done) | copy-start | bytes 497668
  25.3 27.0 %all-to-all-start.1 = ((bf16[8,72,576]{2,1,0:T(8,128)(2,1)}), bf16[8,72,576]{2,1,0:T(8,128)(2,1)S(1)}, u32[]{:S(2)}, u32[]{:S(2)}) async-start(bf16[8,72,576]{2,1,0:T(8,128)(2,1)} %broadcast_in_dim.9), calls=%async_computation.1 | async-start | bytes 1474560 | tf_op jit(solution)/shard_map/all_to_all | solution.py:17
  33.2 71.0 %all-gather.3.cloned.1.call-start = ((), (), s32[]{:S(2)}) async-start(), calls=%async_computation.8 | async-start | bytes 1658880 | tf_op jit(solution)/shard_map/all_gather | solution.py:175
  33.9 16.2 %collective-permute-start.2 = (bf16[72,288]{1,0:T(8,128)(2,1)S(1)}, bf16[72,288]{1,0:T(8,128)(2,1)S(1)}, u32[]{:S(2)}, u32[]{:S(2)}) collective-permute-start(bf16[72,288]{1,0:T(8,128)(2,1)S(1)} %get-tuple-element.23), channel_id=1, source_target_pairs={{0,1},{1,0},{64,65},{65,64},{2,3},{3,2},{66,67},{67,66},{4,5},{5,4... | collective-permute-start | bytes 124424 | tf_op jit(solution)/shard_map/ppermute | solution.py:185
  41.1 9.0 %collective-permute-start.3 = (bf16[72,288]{1,0:T(8,128)(2,1)S(1)}, bf16[72,288]{1,0:T(8,128)(2,1)S(1)}, u32[]{:S(2)}, u32[]{:S(2)}) collective-permute-start(bf16[72,288]{1,0:T(8,128)(2,1)S(1)} %get-tuple-element.25), channel_id=1, source_target_pairs={{0,64},{1,65},{64,0},{65,1},{2,66},{3,67},{66,2},{67,3},{4,68},{5,... | collective-permute-start | bytes 124424 | tf_op jit(solution)/shard_map/ppermute | solution.py:185
  45.0 7.2 %collective-permute-start.4 = (bf16[72,288]{1,0:T(8,128)(2,1)S(1)}, bf16[72,288]{1,0:T(8,128)(2,1)S(1)}, u32[]{:S(2)}, u32[]{:S(2)}) collective-permute-start(bf16[72,288]{1,0:T(8,128)(2,1)S(1)} %get-tuple-element.24), channel_id=1, source_target_pairs={{0,65},{1,64},{64,1},{65,0},{2,67},{3,66},{66,3},{67,2},{4,69},{5,... | collective-permute-start | bytes 124424 | tf_op jit(solution)/shard_map/ppermute | solution.py:185
  53.3 35.3 %all-to-all-start = ((bf16[8,72,576]{2,1,0:T(8,128)(2,1)}), bf16[8,72,576]{2,1,0:T(8,128)(2,1)S(1)}, u32[]{:S(2)}, u32[]{:S(2)}) async-start(bf16[8,72,576]{2,1,0:T(8,128)(2,1)} %broadcast_in_dim.8), calls=%async_computation | async-start | bytes 1474560 | tf_op jit(solution)/shard_map/all_to_all | solution.py:17
  60.2 6.4 %collective-permute-start.5 = (bf16[8,72,576]{2,1,0:T(8,128)(2,1)S(1)}, bf16[8,72,576]{2,1,0:T(8,128)(2,1)}, u32[]{:S(2)}, u32[]{:S(2)}) collective-permute-start(bf16[8,72,576]{2,1,0:T(8,128)(2,1)S(1)} %all-to-all-done.1), channel_id=1, source_target_pairs={{0,16},{16,0},{1,17},{17,1},{2,18},{18,2},{3,19},{19,3},{4,20},{20... | collective-permute-start | bytes 1990664 | tf_op jit(solution)/shard_map/ppermute | solution.py:192
  104.1 25.8 %copy-start = (bf16[16,72,576]{2,1,0:T(8,128)(2,1)S(1)}, bf16[16,72,576]{2,1,0:T(8,128)(2,1)}, u32[]{:S(2)}) copy-start(bf16[16,72,576]{2,1,0:T(8,128)(2,1)} %all-gather.3.cloned.1.call-done) | copy-start | bytes 3981316
  123.1 6.8 %collective-permute-start.6 = (bf16[8,72,576]{2,1,0:T(8,128)(2,1)S(1)}, bf16[8,72,576]{2,1,0:T(8,128)(2,1)S(1)}, u32[]{:S(2)}, u32[]{:S(2)}) collective-permute-start(bf16[8,72,576]{2,1,0:T(8,128)(2,1)S(1)} %all_to_all.41.own), channel_id=1, source_target_pairs={{0,16},{16,0},{1,17},{17,1},{2,18},{18,2},{3,19},{19,3},{4,20},{20... | collective-permute-start | bytes 1990664 | tf_op jit(solution)/shard_map/ppermute | solution.py:201
  131.8 13.0 %all-to-all-start.4 = ((bf16[4,72,576]{2,1,0:T(8,128)(2,1)}), bf16[4,72,576]{2,1,0:T(8,128)(2,1)S(1)}, u32[]{:S(2)}, u32[]{:S(2)}) async-start(bf16[4,72,576]{2,1,0:T(8,128)(2,1)} %shard_map.57), calls=%async_computation.4 | async-start | bytes 737280 | tf_op jit(solution)/shard_map/all_to_all | solution.py:23
  187.2 7.4 %collective-permute-start.7 = (bf16[72,576]{1,0:T(8,128)(2,1)S(1)}, bf16[72,576]{1,0:T(8,128)(2,1)S(1)}, u32[]{:S(2)}, u32[]{:S(2)}) collective-permute-start(bf16[72,576]{1,0:T(8,128)(2,1)S(1)} %reduce_sum.47.mine), channel_id=1, source_target_pairs={{0,64},{64,0},{1,65},{65,1},{2,66},{66,2},{3,67},{67,3},{4,68},{68... | collective-permute-start | bytes 248840 | tf_op jit(solution)/shard_map/ppermute | solution.py:214
  197.0 7.7 %collective-permute-start.8 = (bf16[8,72,576]{2,1,0:T(8,128)(2,1)S(1)}, bf16[8,72,576]{2,1,0:T(8,128)(2,1)S(1)}, u32[]{:S(2)}, u32[]{:S(2)}) collective-permute-start(bf16[8,72,576]{2,1,0:T(8,128)(2,1)S(1)} %get-tuple-element.22), channel_id=1, source_target_pairs={{0,16},{16,0},{1,17},{17,1},{2,18},{18,2},{3,19},{19,3},{4,20},{20... | collective-permute-start | bytes 1990664 | tf_op jit(solution)/shard_map/ppermute | solution.py:223
Sparse Core Ops, SparseCore 0:
  36.1 49.9 all-gather.2

commit v9 on v6

--- a/solution.py
+++ b/solution.py
@@ -40,10 +40,6 @@
 
 def pairs_z1y0():
     return [(z1 * 8 + y, (y % 2) * 8 + (y // 2) * 2 + z1) for z1 in range(2) for y in range(8)]
-
-
-def pairs_part(d1, d2):
-    return [(i, i ^ (2 * d1 + d2)) for i in range(4)]
 
 
 def pairs_rows():
@@ -54,11 +50,6 @@
         for c in range(2)
         for z2 in range(2)
     ]
-
-
-def pack(rows):
-    q = rows.shape[0] // 2
-    return jnp.concatenate([rows[:q], rows[q:]], axis=1)
 
 
 def run(kernel, outs, args, scratch=(), flags=0):
@@ -95,6 +86,41 @@
                 second = jnp.where(low_core, cut(t % 2, 1 - far), cut(1 - t % 2, 1 - far))
                 at = (4 * a + t) * q
                 out[far, :, at : at + q] = jnp.where(low_rep, first, second).astype(jnp.bfloat16)
+
+
+def cut_grad(grad, out):
+    q, wide = grad.shape[0] // 2, grad.shape[1] // 4
+    for part, block in enumerate((0, 2, 1, 3)):
+        for h in range(2):
+            piece = grad[q * h : q * h + q, wide * block : wide * block + wide]
+            out[part, :, wide * h : wide * h + wide] = piece
+
+
+def join_grad(got, out):
+    wide = got.shape[2]
+    for z1 in range(2):
+        total = got[2 * z1].astype(jnp.float32) + got[2 * z1 + 1].astype(jnp.float32)
+        total = total.astype(out.dtype)
+        for i in range(out.shape[0]):
+            out[i, :, wide * z1 : wide * z1 + wide] = total
+
+
+def sum_copies(got, out):
+    total = got[0].astype(jnp.float32)
+    for i in range(1, got.shape[0]):
+        total += got[i].astype(jnp.float32)
+    total = total.astype(out.dtype)
+    for i in range(out.shape[0]):
+        out[i] = total
+
+
+def scale_copies(got, out_scale, in_scale, out):
+    total = got[0].astype(jnp.float32)
+    for i in range(1, got.shape[0]):
+        total += got[i].astype(jnp.float32)
+    total = (total / (out_scale[...] * in_scale[...] + DAMPING)).astype(out.dtype)
+    for i in range(out.shape[0]):
+        out[i] = total
 
 
 def turn_in(grad, basis, out, left):
@@ -159,53 +185,46 @@
     rows, cols = basis_in.shape
     half, quarter = rows // 2, cols // 4
     wide = 2 * rows
-    low_core, low_rep, low_z1 = c == 0, z2 == 0, z1 == 0
+    low_core, low_rep = c == 0, z2 == 0
 
 
     core, rep, part_z1 = (i.astype(jnp.int32).reshape(1) for i in (c, z2, z1))
+
+    first = (((x * 2 + z1) * 2 + z0) * 2 + c) * rows + z2 * half
+    out_scale = lax.dynamic_slice_in_dim(eig_out, first, half, 0)[:, None]
+    in_scale = lax.dynamic_slice_in_dim(eig_in, y * cols, cols, 0)[None, :]
 
     bo = run(order_out, shape(2, half, cols), (core, rep, basis_out), flags=2)
     bo = lax.ppermute(bo, ("z1", "y"), pairs_z1y0())
-
-    grad = grad_parts[0]
-    parts = jnp.stack([pack(grad[:, i * quarter : (i + 1) * quarter]) for i in range(4)])
-
-    def piece(d1, d2):
-        which = 2 * (z2 ^ d2) + (z1 ^ d1)
-        return lax.dynamic_index_in_dim(parts, which, 0, keepdims=False)
-
-    def from_part(d1, d2):
-        return lax.ppermute(piece(d1, d2), PART, pairs_part(d1, d2)).astype(f32)
-
-    mine = (piece(0, 0).astype(f32) + from_part(0, 1)).astype(bf16)
-    other = (from_part(1, 0) + from_part(1, 1)).astype(bf16)
-    grad = in_order(low_z1, mine, other, 1)
 
     bi = basis_in.astype(bf16)
     bi = jnp.where(low_rep, bi[:half], bi[half:])
     bi = lax.ppermute(bi, ("z1", "z0", "c", "z2"), pairs_rows())
+
+    grad = run(cut_grad, shape(4, half, wide), (grad_parts[0],))
+    grad = lax.all_to_all(grad, PART, 0, 0, tiled=True)
+    grad = run(join_grad, shape(8, half, cols), (grad,))
+
+    bo, bi, grad = lax.optimization_barrier((bo, bi, grad))
     bi = gather(bi, RING, 8)
     bi = in_order(low_core, bi, lax.ppermute(bi, "c", SWAP), 1)
-
-    bo, grad = lax.optimization_barrier((bo, grad))
-    grad = gather(grad, "y", 8)
+    grad = lax.all_to_all(grad, "y", 0, 0, tiled=True)
+
     bo, grad = lax.optimization_barrier((bo, grad))
     bo = lax.all_gather(bo, "y", axis=0)
 
     left = (4, half, 8 * quarter)
     part = run(turn_in, shape(4, half, cols), (grad, bi), (left,))
-    turned = scatter_sum(part, PART).astype(bf16)
-    turned = gather(turned, RING, 8)
+    part = lax.all_to_all(part, PART, 0, 0, tiled=True)
+    turned = run(sum_copies, shape(8, half, cols), (part,))
+    turned = lax.all_to_all(turned, RING, 0, 0, tiled=True)
     other = lax.ppermute(turned, "c", SWAP)
 
     right = (8 * rows, cols)
     part = run(turn_out, shape(4, half, cols), (bo, turned, other), (left, right))
-    rotated = scatter_sum(part, PART)
-    first = (((x * 2 + z1) * 2 + z0) * 2 + c) * rows + z2 * half
-    out_scale = lax.dynamic_slice_in_dim(eig_out, first, half, 0)
-    in_scale = lax.dynamic_slice_in_dim(eig_in, y * cols, cols, 0)
-    scaled = (rotated / (out_scale[:, None] * in_scale[None, :] + DAMPING)).astype(bf16)
-    scaled = gather(scaled, PART, 4)
+    part = lax.all_to_all(part, PART, 0, 0, tiled=True)
+    scaled = run(scale_copies, shape(4, half, cols), (part, out_scale, in_scale))
+    scaled = lax.all_to_all(scaled, PART, 0, 0, tiled=True)
 
     part = run(back_in, shape(8, half, cols), (scaled, bi))
     back = scatter_sum(part, "y").astype(bf16)

time: 228 us -> 226 us (level)
  starting transfers between devices: 79.5 us -> 66.6 us
  blocking collectives: 64.7 us -> 74.4 us
    all_to_all x0 -> x2, blocking collectives: none -> 26.5 us  [the longest x1 13.4 us: body(): scaled = lax.all_to_all(scaled, PART, 0, 0, tiled=True)]
    all_to_all x2 -> x1, blocking collectives: 30.9 us -> 14.1 us  [gather(): lax.all_to_all(jnp.broadcast_to(block[None], (count,) + block.shape), axe...]
    ppermute x3 -> x0, starting transfers between devices: 11.4 us -> none  [from_part(): return lax.ppermute(piece(d1, d2), PART, pairs_part(d1, d2)).astype(f32)]
    all_to_all x4, waiting for transfers between devices: 24.2 us -> 33.3 us  [the longest x2 16 us: body(): part = lax.all_to_all(part, PART, 0, 0, tiled=True)]
    ppermute x1, waiting for transfers between devices: 7.15 us -> 2.37 us  [body(): bi = lax.ppermute(bi, ('z1', 'z0', 'c', 'z2'), pairs_rows())]
    pallas_call x5 -> x9, Pallas kernels: 9.71 us -> 11.8 us  [run(): pl.pallas_call(kernel, out_shape=outs, in_specs=[pl.BlockSpec(memory_spac...]
  transfers between devices with their start and end apart: 14 -> 11, of which waited for: 8 -> 8; matrix products, arithmetic and copies ran while one was open for 1% -> 0% of each run, Pallas kernels for 0% -> 1%
where the time goes in v9:
time: 226 us; the launch traced here: 225 us
  blocking collectives  74.4 us (33%)
  starting transfers between devices  66.6 us (29%)
  waiting for transfers between devices  51.7 us (23%)
  between operations  13.5 us (6%)
  Pallas kernels  11.8 us (5%)
  local copies, waits for them, and re-layouts  4.4 us (2%)
  other arithmetic  3.09 us (1%)
    all_to_all x2, blocking collectives, scatter_sum(): got = lax.all_to_all(blocks, axes, 0, 0, tiled=True)  33.8 us
    all_to_all x2, waiting for transfers between devices, body(): part = lax.all_to_all(part, PART, 0, 0, tiled=True)  16 us
    all_to_all x1, waiting for transfers between devices, body(): grad = lax.all_to_all(grad, 'y', 0, 0, tiled=True)  14.1 us
    all_to_all x1, blocking collectives, gather(): lax.all_to_all(jnp.broadcast_to(block[None], (count,) + block.shape), axe...  14.1 us
    all_to_all x1, blocking collectives, body(): scaled = lax.all_to_all(scaled, PART, 0, 0, tiled=True)  13.4 us
    all_to_all x1, starting transfers between devices, body(): grad = lax.all_to_all(grad, PART, 0, 0, tiled=True)  13.4 us
    all_to_all x1, blocking collectives, body(): turned = lax.all_to_all(turned, RING, 0, 0, tiled=True)  13 us
    all_to_all x2, starting transfers between devices, body(): part = lax.all_to_all(part, PART, 0, 0, tiled=True)  12.5 us
  transfers between devices with their start and end apart: 11, of which 8 were waited for; matrix products, arithmetic and copies ran while one was open for 0% of the time, Pallas kernels for 1%

profile of v9, /device:TPU:1, one launch (start us, length us, event | category | flops | bytes accessed | tf_op | source)
XLA Modules:
  0.0 225.5 jit_solution(7152043849545925243)
XLA Ops:
  6.5 1.0 copy-done.3
  7.5 1.1 shard_map.55
  9.3 0.9 copy-done.4
  11.0 13.4 %all-to-all-start = ((bf16[4,72,288]{2,1,0:T(8,128)(2,1)}), bf16[4,72,288]{2,1,0:T(8,128)(2,1)S(1)}, u32[]{:S(2)}, u32[]{:S(2)}) async-start(bf16[4,72,288]{2,1,0:T(8,128)(2,1)} %shard_map.56), calls=%async_computation | async-start | bytes 442368 | tf_op jit(solution)/shard_map/all_to_all | solution.py:205
  24.4 5.7 %collective-permute-start.1 = (bf16[72,576]{1,0:T(8,128)(2,1)S(1)}, bf16[72,576]{1,0:T(8,128)(2,1)S(1)}, u32[]{:S(2)}, u32[]{:S(2)}) collective-permute-start(bf16[72,576]{1,0:T(8,128)(2,1)S(1)} %slice_select_fusion), channel_id=1, source_target_pairs={{0,0},{1,16},{16,64},{17,80},{32,1},{33,17},{48,65},{49,81},{64,32... | collective-permute-start | bytes 248840 | tf_op jit(solution)/shard_map/ppermute | solution.py:202
  30.1 3.2 %all-to-all-done.got = bf16[4,72,288]{2,1,0:T(8,128)(2,1)S(1)} async-done(((bf16[4,72,288]{2,1,0:T(8,128)(2,1)}), bf16[4,72,288]{2,1,0:T(8,128)(2,1)S(1)}, u32[]{:S(2)}, u32[]{:S(2)}) %all-to-all-start) | async-done | bytes 165920 | tf_op jit(solution)/shard_map/all_to_all | solution.py:205
  33.3 1.0 shard_map.57
  34.3 2.4 %collective-permute-done.1 = bf16[72,576]{1,0:T(8,128)(2,1)S(1)} collective-permute-done((bf16[72,576]{1,0:T(8,128)(2,1)S(1)}, bf16[72,576]{1,0:T(8,128)(2,1)S(1)}, u32[]{:S(2)}, u32[]{:S(2)}) %collective-permute-start.1) | collective-permute-done | bytes 82976 | tf_op jit(solution)/shard_map/ppermute | solution.py:202
  36.7 14.1 %all_to_all.45 = bf16[8,72,576]{2,1,0:T(8,128)(2,1)S(1)} all-to-all(bf16[8,72,576]{2,1,0:T(8,128)(2,1)S(1)} %broadcast_in_dim.12), channel_id=1, replica_groups=mesh['x'=4,'z1'=2,'z0'=2,'c'=2,'y'=8,'z2'=2] {'x','z0'}, dimensions={0} | all-to-all | bytes 1327104 | tf_op jit(solution)/shard_map/all_to_all | solution.py:17
  50.9 7.7 %all-to-all-start.1 = ((bf16[8,72,576]{2,1,0:T(8,128)(2,1)}), bf16[8,72,576]{2,1,0:T(8,128)(2,1)S(1)}, u32[]{:S(2)}, u32[]{:S(2)}) async-start(bf16[8,72,576]{2,1,0:T(8,128)(2,1)} %shard_map.57), calls=%async_computation.1 | async-start | bytes 1474560 | tf_op jit(solution)/shard_map/all_to_all | solution.py:211
  58.5 5.2 %collective-permute-start.2 = (bf16[8,72,576]{2,1,0:T(8,128)(2,1)S(1)}, bf16[8,72,576]{2,1,0:T(8,128)(2,1)}, u32[]{:S(2)}, u32[]{:S(2)}) collective-permute-start(bf16[8,72,576]{2,1,0:T(8,128)(2,1)S(1)} %all_to_all.45), channel_id=1, source_target_pairs={{0,16},{16,0},{1,17},{17,1},{2,18},{18,2},{3,19},{19,3},{4,20},{20... | collective-permute-start | bytes 1990664 | tf_op jit(solution)/shard_map/ppermute | solution.py:210
  63.8 14.1 %all-to-all-done.1.grad = bf16[8,72,576]{2,1,0:T(8,128)(2,1)S(1)} async-done(((bf16[8,72,576]{2,1,0:T(8,128)(2,1)}), bf16[8,72,576]{2,1,0:T(8,128)(2,1)S(1)}, u32[]{:S(2)}, u32[]{:S(2)}) %all-to-all-start.1) | async-done | bytes 663584 | tf_op jit(solution)/shard_map/all_to_all | solution.py:211
  77.9 1.9 maximum_select_fusion.basis
  79.9 1.9 shard_map.58
  81.8 5.4 %all-to-all-start.3 = ((bf16[4,72,576]{2,1,0:T(8,128)(2,1)}), bf16[4,72,576]{2,1,0:T(8,128)(2,1)S(1)}, u32[]{:S(2)}, u32[]{:S(2)}) async-start(bf16[4,72,576]{2,1,0:T(8,128)(2,1)} %shard_map.58), calls=%async_computation.3 | async-start | bytes 737280 | tf_op jit(solution)/shard_map/all_to_all | solution.py:218
  88.0 8.3 %all-to-all-done.3.got = bf16[4,72,576]{2,1,0:T(8,128)(2,1)S(1)} async-done(((bf16[4,72,576]{2,1,0:T(8,128)(2,1)}), bf16[4,72,576]{2,1,0:T(8,128)(2,1)S(1)}, u32[]{:S(2)}, u32[]{:S(2)}) %all-to-all-start.3) | async-done | bytes 331808 | tf_op jit(solution)/shard_map/all_to_all | solution.py:218
  96.3 13.0 %all_to_all.46.own = bf16[8,72,576]{2,1,0:T(8,128)(2,1)S(1)} all-to-all(bf16[8,72,576]{2,1,0:T(8,128)(2,1)S(1)} %shard_map.59), channel_id=1, replica_groups=mesh['x'=4,'z1'=2,'z0'=2,'c'=2,'y'=8,'z2'=2] {'x','z0'}, dimensions={0} | all-to-all | bytes 1327104 | tf_op jit(solution)/shard_map/all_to_all | solution.py:220
  109.3 7.4 %collective-permute-start.3 = (bf16[8,72,576]{2,1,0:T(8,128)(2,1)S(1)}, bf16[8,72,576]{2,1,0:T(8,128)(2,1)S(1)}, u32[]{:S(2)}, u32[]{:S(2)}) collective-permute-start(bf16[8,72,576]{2,1,0:T(8,128)(2,1)S(1)} %all_to_all.46.own), channel_id=1, source_target_pairs={{0,16},{16,0},{1,17},{17,1},{2,18},{18,2},{3,19},{19,3},{4,20},{20... | collective-permute-start | bytes 1990664 | tf_op jit(solution)/shard_map/ppermute | solution.py:221
  116.7 8.4 %all-gather.3.cloned.1.call-done = bf16[16,72,576]{2,1,0:T(8,128)(2,1)} async-done(((bf16[2,72,576]{2,1,0:T(8,128)(2,1)}), bf16[16,72,576]{2,1,0:T(8,128)(2,1)}) %all-gather.3.cloned.1.call-update) | async-done | bytes 1327120 | tf_op jit(solution)/shard_map/all_gather | solution.py:214
  125.1 1.4 copy-done.1
  126.5 1.9 shard_map.60
  128.4 7.1 %all-to-all-start.5 = ((bf16[4,72,576]{2,1,0:T(8,128)(2,1)}), bf16[4,72,576]{2,1,0:T(8,128)(2,1)S(1)}, u32[]{:S(2)}, u32[]{:S(2)}) async-start(bf16[4,72,576]{2,1,0:T(8,128)(2,1)} %shard_map.60), calls=%async_computation.5 | async-start | bytes 737280 | tf_op jit(solution)/shard_map/all_to_all | solution.py:225
  136.4 7.7 %all-to-all-done.5.got = bf16[4,72,576]{2,1,0:T(8,128)(2,1)S(1)} async-done(((bf16[4,72,576]{2,1,0:T(8,128)(2,1)}), bf16[4,72,576]{2,1,0:T(8,128)(2,1)S(1)}, u32[]{:S(2)}, u32[]{:S(2)}) %all-to-all-start.5) | async-done | bytes 331808 | tf_op jit(solution)/shard_map/all_to_all | solution.py:225
  144.2 13.4 %all_to_all.47.scaled = bf16[4,72,576]{2,1,0:T(8,128)(2,1)S(1)} all-to-all(bf16[4,72,576]{2,1,0:T(8,128)(2,1)S(1)} %shard_map.61), channel_id=1, replica_groups=mesh['x'=4,'z1'=2,'z0'=2,'c'=2,'y'=8,'z2'=2] {'z1','z2'}, dimensions={0} | all-to-all | bytes 663552 | tf_op jit(solution)/shard_map/all_to_all | solution.py:227
  157.7 2.6 %shard_map.62 = bf16[8,72,576]{2,1,0:T(8,128)(2,1)S(1)} custom-call(bf16[4,72,576]{2,1,0:T(8,128)(2,1)S(1)} %all_to_all.47.scaled, bf16[8,144,576]{2,1,0:T(8,128)(2,1)S(1)} %maximum_select_fusion.basis), custom_call_target="tpu_custom_call" | custom-call | flops 382205952 | bytes 2322432 | tf_op jit(solution)/shard_map/pallas_call | solution.py:57
  160.2 18.2 %all_to_all.48 = bf16[8,72,576]{2,1,0:T(8,128)(2,1)S(1)} all-to-all(bf16[8,72,576]{2,1,0:T(8,128)(2,1)S(1)} %shard_map.62), channel_id=1, replica_groups=mesh['x'=4,'z1'=2,'z0'=2,'c'=2,'y'=8,'z2'=2] {'y'}, dimensions={0} | all-to-all | bytes 1327104 | tf_op jit(solution)/shard_map/all_to_all | solution.py:23
  178.6 2.4 %collective-permute-start.4 = (bf16[72,576]{1,0:T(8,128)(2,1)S(1)}, bf16[72,576]{1,0:T(8,128)(2,1)S(1)}, u32[]{:S(2)}, u32[]{:S(2)}) collective-permute-start(bf16[72,576]{1,0:T(8,128)(2,1)S(1)} %reduce_sum.24.mine), channel_id=1, source_target_pairs={{0,64},{64,0},{1,65},{65,1},{2,66},{66,2},{3,67},{67,3},{4,68},{68... | collective-permute-start | bytes 248840 | tf_op jit(solution)/shard_map/ppermute | solution.py:231
  180.9 5.1 %collective-permute-done.4.other = bf16[72,576]{1,0:T(8,128)(2,1)S(1)} collective-permute-done((bf16[72,576]{1,0:T(8,128)(2,1)S(1)}, bf16[72,576]{1,0:T(8,128)(2,1)S(1)}, u32[]{:S(2)}, u32[]{:S(2)}) %collective-permute-start.4) | collective-permute-done | bytes 82976 | tf_op jit(solution)/shard_map/ppermute | solution.py:231
  186.1 2.3 %shard_map.63 = (bf16[8,72,576]{2,1,0:T(8,128)(2,1)S(1)}, bf16[8,72,576]{2,1,0:T(8,128)(2,1)S(1)}) custom-call(s32[1]{0:T(128)} %bitcast.part, bf16[8,2,72,576]{3,2,1,0:T(8,128)(2,1)S(1)} %bitcast.8, bf16[72,576]{1,0:T(8,128)(2,1)S(1)} %reduce_sum.24.mine, bf16[72,576]{1,0:T(8,128)(2,1)S(1)} %collective-permute-done.4.other), custom_call_target="tpu_custom_call" | custom-call | flops 382205952 | bytes 2820100 | tf_op jit(solution)/shard_map/pallas_call | solution.py:57
  188.4 11.7 %collective-permute-start.5 = (bf16[8,72,576]{2,1,0:T(8,128)(2,1)S(1)}, bf16[8,72,576]{2,1,0:T(8,128)(2,1)S(1)}, u32[]{:S(2)}, u32[]{:S(2)}) collective-permute-start(bf16[8,72,576]{2,1,0:T(8,128)(2,1)S(1)} %get-tuple-element.18), channel_id=1, source_target_pairs={{0,16},{16,0},{1,17},{17,1},{2,18},{18,2},{3,19},{19,3},{4,20},{20... | collective-permute-start | bytes 1990664 | tf_op jit(solution)/shard_map/ppermute | solution.py:240
  200.1 1.8 collective-permute-done.5
  202.1 15.6 %all_to_all.49 = bf16[8,72,576]{2,1,0:T(8,128)(2,1)S(1)} all-to-all(bf16[8,72,576]{2,1,0:T(8,128)(2,1)S(1)} %add_convert_fusion), channel_id=1, replica_groups=mesh['x'=4,'z1'=2,'z0'=2,'c'=2,'y'=8,'z2'=2] {'x','z0'}, dimensions={0} | all-to-all | bytes 1327104 | tf_op jit(solution)/shard_map/all_to_all | solution.py:23
  (32 shorter events, 4.6 us)
Async XLA Ops:
  6.5 128.9 %copy-start = (f32[4608]{0:T(1024)S(1)}, f32[4608]{0:T(1024)}, u32[]{:S(2)}) copy-start(f32[4608]{0:T(1024)} %param.9) | copy-start | bytes 55300
  6.5 1.0 copy-start.3
  7.5 16.9 %copy-start.5 = (f32[144,576]{1,0:T(8,128)S(1)}, f32[144,576]{1,0:T(8,128)}, u32[]{:S(2)}) copy-start(f32[144,576]{1,0:T(8,128)} %param.6) | copy-start | bytes 995332
  8.6 28.1 %collective-permute-start = (bf16[2,72,576]{2,1,0:T(8,128)(2,1)S(1)}, bf16[2,72,576]{2,1,0:T(8,128)(2,1)S(1)}, u32[]{:S(2)}, u32[]{:S(2)}) collective-permute-start(bf16[2,72,576]{2,1,0:T(8,128)(2,1)S(1)} %shard_map.55), channel_id=1, source_target_pairs={{0,0},{2,64},{4,4},{6,68},{8,8},{10,72},{12,12},{14,76},{64,2},{66... | collective-permute-start | bytes 497672 | tf_op jit(solution)/shard_map/ppermute | solution.py:198
  9.3 0.9 copy-start.4
  11.0 22.3 %all-to-all-start = ((bf16[4,72,288]{2,1,0:T(8,128)(2,1)}), bf16[4,72,288]{2,1,0:T(8,128)(2,1)S(1)}, u32[]{:S(2)}, u32[]{:S(2)}) async-start(bf16[4,72,288]{2,1,0:T(8,128)(2,1)} %shard_map.56), calls=%async_computation | async-start | bytes 442368 | tf_op jit(solution)/shard_map/all_to_all | solution.py:205
  24.4 12.2 %collective-permute-start.1 = (bf16[72,576]{1,0:T(8,128)(2,1)S(1)}, bf16[72,576]{1,0:T(8,128)(2,1)S(1)}, u32[]{:S(2)}, u32[]{:S(2)}) collective-permute-start(bf16[72,576]{1,0:T(8,128)(2,1)S(1)} %slice_select_fusion), channel_id=1, source_target_pairs={{0,0},{1,16},{16,64},{17,80},{32,1},{33,17},{48,65},{49,81},{64,32... | collective-permute-start | bytes 248840 | tf_op jit(solution)/shard_map/ppermute | solution.py:202
  36.7 14.2 %copy-start.6 = (bf16[2,72,576]{2,1,0:T(8,128)(2,1)}, bf16[2,72,576]{2,1,0:T(8,128)(2,1)S(1)}, u32[]{:S(2)}) copy-start(bf16[2,72,576]{2,1,0:T(8,128)(2,1)S(1)} %collective-permute-done) | copy-start | bytes 497668
  50.9 27.1 %all-to-all-start.1 = ((bf16[8,72,576]{2,1,0:T(8,128)(2,1)}), bf16[8,72,576]{2,1,0:T(8,128)(2,1)S(1)}, u32[]{:S(2)}, u32[]{:S(2)}) async-start(bf16[8,72,576]{2,1,0:T(8,128)(2,1)} %shard_map.57), calls=%async_computation.1 | async-start | bytes 1474560 | tf_op jit(solution)/shard_map/all_to_all | solution.py:211
  58.5 19.4 %collective-permute-start.2 = (bf16[8,72,576]{2,1,0:T(8,128)(2,1)S(1)}, bf16[8,72,576]{2,1,0:T(8,128)(2,1)}, u32[]{:S(2)}, u32[]{:S(2)}) collective-permute-start(bf16[8,72,576]{2,1,0:T(8,128)(2,1)S(1)} %all_to_all.45), channel_id=1, source_target_pairs={{0,16},{16,0},{1,17},{17,1},{2,18},{18,2},{3,19},{19,3},{4,20},{20... | collective-permute-start | bytes 1990664 | tf_op jit(solution)/shard_map/ppermute | solution.py:210
  81.8 14.5 %all-to-all-start.3 = ((bf16[4,72,576]{2,1,0:T(8,128)(2,1)}), bf16[4,72,576]{2,1,0:T(8,128)(2,1)S(1)}, u32[]{:S(2)}, u32[]{:S(2)}) async-start(bf16[4,72,576]{2,1,0:T(8,128)(2,1)} %shard_map.58), calls=%async_computation.3 | async-start | bytes 737280 | tf_op jit(solution)/shard_map/all_to_all | solution.py:218
  87.2 37.8 %all-gather.3.cloned.1.call-start = ((), (), s32[]{:S(2)}) async-start(), calls=%async_computation.9 | async-start | bytes 1658880 | tf_op jit(solution)/shard_map/all_gather | solution.py:214
  109.3 15.7 %collective-permute-start.3 = (bf16[8,72,576]{2,1,0:T(8,128)(2,1)S(1)}, bf16[8,72,576]{2,1,0:T(8,128)(2,1)S(1)}, u32[]{:S(2)}, u32[]{:S(2)}) collective-permute-start(bf16[8,72,576]{2,1,0:T(8,128)(2,1)S(1)} %all_to_all.46.own), channel_id=1, source_target_pairs={{0,16},{16,0},{1,17},{17,1},{2,18},{18,2},{3,19},{19,3},{4,20},{20... | collective-permute-start | bytes 1990664 | tf_op jit(solution)/shard_map/ppermute | solution.py:221
  125.1 1.4 copy-start.1
  128.4 15.8 %all-to-all-start.5 = ((bf16[4,72,576]{2,1,0:T(8,128)(2,1)}), bf16[4,72,576]{2,1,0:T(8,128)(2,1)S(1)}, u32[]{:S(2)}, u32[]{:S(2)}) async-start(bf16[4,72,576]{2,1,0:T(8,128)(2,1)} %shard_map.60), calls=%async_computation.5 | async-start | bytes 737280 | tf_op jit(solution)/shard_map/all_to_all | solution.py:225
  160.2 25.8 %copy-start.2 = (bf16[16,72,576]{2,1,0:T(8,128)(2,1)S(1)}, bf16[16,72,576]{2,1,0:T(8,128)(2,1)}, u32[]{:S(2)}) copy-start(bf16[16,72,576]{2,1,0:T(8,128)(2,1)} %all-gather.3.cloned.1.call-done) | copy-start | bytes 3981316
  178.6 7.5 %collective-permute-start.4 = (bf16[72,576]{1,0:T(8,128)(2,1)S(1)}, bf16[72,576]{1,0:T(8,128)(2,1)S(1)}, u32[]{:S(2)}, u32[]{:S(2)}) collective-permute-start(bf16[72,576]{1,0:T(8,128)(2,1)S(1)} %reduce_sum.24.mine), channel_id=1, source_target_pairs={{0,64},{64,0},{1,65},{65,1},{2,66},{66,2},{3,67},{67,3},{4,68},{68... | collective-permute-start | bytes 248840 | tf_op jit(solution)/shard_map/ppermute | solution.py:231
  188.4 13.5 %collective-permute-start.5 = (bf16[8,72,576]{2,1,0:T(8,128)(2,1)S(1)}, bf16[8,72,576]{2,1,0:T(8,128)(2,1)S(1)}, u32[]{:S(2)}, u32[]{:S(2)}) collective-permute-start(bf16[8,72,576]{2,1,0:T(8,128)(2,1)S(1)} %get-tuple-element.18), channel_id=1, source_target_pairs={{0,16},{16,0},{1,17},{17,1},{2,18},{18,2},{3,19},{19,3},{4,20},{20... | collective-permute-start | bytes 1990664 | tf_op jit(solution)/shard_map/ppermute | solution.py:240
Sparse Core Ops, SparseCore 0:
  90.1 34.8 all-gather.2

commit v10 on v9

--- a/solution.py
+++ b/solution.py
@@ -105,16 +105,16 @@
             out[i, :, wide * z1 : wide * z1 + wide] = total
 
 
-def sum_copies(got, out):
-    total = got[0].astype(jnp.float32)
-    for i in range(1, got.shape[0]):
-        total += got[i].astype(jnp.float32)
+def sum_copies(p0, p1, p2, p3, out):
+    total = p0[...].astype(jnp.float32)
+    for p in (p1, p2, p3):
+        total += p[...].astype(jnp.float32)
     total = total.astype(out.dtype)
     for i in range(out.shape[0]):
         out[i] = total
 
 
-def scale_copies(got, out_scale, in_scale, out):
+def scale(got, out_scale, in_scale, out):
     total = got[0].astype(jnp.float32)
     for i in range(1, got.shape[0]):
         total += got[i].astype(jnp.float32)
@@ -123,15 +123,32 @@
         out[i] = total
 
 
-def turn_in(grad, basis, out, left):
+def join_out(rep, got, out):
+    total = got[0].astype(jnp.float32)
+    for i in range(1, got.shape[0]):
+        total += got[i].astype(jnp.float32)
+    total = total.astype(out.dtype)
+    q, wide = out.shape[0] // 2, out.shape[1]
+    low = rep[0] == 0
+    near, far = total[:, :wide], total[:, wide:]
+    out[:q] = jnp.where(low, near, far)
+    out[q:] = jnp.where(low, far, near)
+
+
+def to_part(block, d):
+    return lax.ppermute(block, PART, [(i, i ^ d) for i in range(4)])
+
+
+def turn_in(part, grad, basis, *outs_and_left):
+    *outs, left = outs_and_left
     count, _, wide = grad.shape
     q = wide // 4
     for y in range(count):
         for g in range(4):
             left[g, :, q * y : q * y + q] = grad[y, :, q * g : q * g + q]
     right = basis[...].reshape(count * q, basis.shape[2])
-    for g in range(4):
-        out[g] = dot(left[g], right, 1, 0).astype(out.dtype)
+    for d, out in enumerate(outs):
+        out[...] = dot(left[part[0] ^ d], right, 1, 0).astype(out.dtype)
 
 
 def turn_out(rows, own, other, out, left, right):
@@ -188,7 +205,9 @@
     low_core, low_rep = c == 0, z2 == 0
 
 
-    core, rep, part_z1 = (i.astype(jnp.int32).reshape(1) for i in (c, z2, z1))
+    core, rep, part_z1, this_part = (
+        i.astype(jnp.int32).reshape(1) for i in (c, z2, z1, 2 * z1 + z2)
+    )
 
     first = (((x * 2 + z1) * 2 + z0) * 2 + c) * rows + z2 * half
     out_scale = lax.dynamic_slice_in_dim(eig_out, first, half, 0)[:, None]
@@ -214,16 +233,16 @@
     bo = lax.all_gather(bo, "y", axis=0)
 
     left = (4, half, 8 * quarter)
-    part = run(turn_in, shape(4, half, cols), (grad, bi), (left,))
-    part = lax.all_to_all(part, PART, 0, 0, tiled=True)
-    turned = run(sum_copies, shape(8, half, cols), (part,))
+    blocks = run(turn_in, (shape(half, cols),) * 4, (this_part, grad, bi), (left,), 1)
+    blocks = [blocks[0]] + [to_part(blocks[d], d) for d in (1, 2, 3)]
+    turned = run(sum_copies, shape(8, half, cols), blocks)
     turned = lax.all_to_all(turned, RING, 0, 0, tiled=True)
     other = lax.ppermute(turned, "c", SWAP)
 
     right = (8 * rows, cols)
     part = run(turn_out, shape(4, half, cols), (bo, turned, other), (left, right))
     part = lax.all_to_all(part, PART, 0, 0, tiled=True)
-    scaled = run(scale_copies, shape(4, half, cols), (part, out_scale, in_scale))
+    scaled = run(scale, shape(4, half, cols), (part, out_scale, in_scale))
     scaled = lax.all_to_all(scaled, PART, 0, 0, tiled=True)
 
     part = run(back_in, shape(8, half, cols), (scaled, bi))
@@ -238,8 +257,8 @@
         flags=1,
     )
     part = (keep.astype(f32) + lax.ppermute(give, "c", SWAP).astype(f32)).astype(bf16)
-    out = scatter_sum(part, RING).astype(bf16)
-    return in_order(low_rep, out[:, :wide], out[:, wide:], 0)
+    part = lax.all_to_all(part, RING, 0, 0, tiled=True)
+    return run(join_out, shape(rows, wide), (rep, part), flags=1)
 
 
 def solution(mesh):

time: 226 us -> 221 us (0.978)
  waiting for transfers between devices: 51.7 us -> 39.2 us
  blocking collectives: 74.4 us -> 81.6 us
    all_to_all x0 -> x1, blocking collectives: none -> 15.7 us  [body(): part = lax.all_to_all(part, RING, 0, 0, tiled=True)]
    ppermute x0 -> x3, starting transfers between devices: none -> 12.3 us  [to_part(): return lax.ppermute(block, PART, [(i, i ^ d) for i in range(4)])]
    all_to_all x2 -> x1, blocking collectives: 33.8 us -> 21.9 us  [scatter_sum(): got = lax.all_to_all(blocks, axes, 0, 0, tiled=True)]
    all_to_all x2 -> x1, starting transfers between devices: 12.5 us -> 3.59 us  [body(): part = lax.all_to_all(part, PART, 0, 0, tiled=True)]
    all_gather x1, waiting for transfers between devices: 8.36 us -> 0.02 us  [body(): bo = lax.all_gather(bo, 'y', axis=0)]
    all_to_all x2 -> x1, waiting for transfers between devices: 16 us -> 8.73 us  [body(): part = lax.all_to_all(part, PART, 0, 0, tiled=True)]
    ppermute x1, starting transfers between devices: 11.7 us -> 6.04 us  [body(): lax.ppermute(give, 'c', SWAP).astype(f32)]
    ppermute x0 -> x3, waiting for transfers between devices: none -> 5.28 us  [to_part(): return lax.ppermute(block, PART, [(i, i ^ d) for i in range(4)])]
  transfers between devices with their start and end apart: 11 -> 13, of which waited for: 8 -> 9; matrix products, arithmetic and copies ran while one was open for 0% -> 1% of each run, Pallas kernels for 1% -> 1%
where the time goes in v10:
time: 221 us
  blocking collectives  81.6 us (37%)
  starting transfers between devices  67.4 us (30%)
  waiting for transfers between devices  39.2 us (18%)
  between operations  13.6 us (6%)
  Pallas kernels  12.1 us (5%)
  local copies, waits for them, and re-layouts  4.31 us (2%)
  other arithmetic  2.28 us (1%)
    all_to_all x1, blocking collectives, scatter_sum(): got = lax.all_to_all(blocks, axes, 0, 0, tiled=True)  21.9 us
    all_to_all x1, blocking collectives, body(): scaled = lax.all_to_all(scaled, PART, 0, 0, tiled=True)  17.7 us
    all_to_all x1, blocking collectives, body(): part = lax.all_to_all(part, RING, 0, 0, tiled=True)  15.7 us
    all_to_all x1, blocking collectives, gather(): lax.all_to_all(jnp.broadcast_to(block[None], (count,) + block.shape), axe...  14.1 us
    all_to_all x1, waiting for transfers between devices, body(): grad = lax.all_to_all(grad, 'y', 0, 0, tiled=True)  14.1 us
    all_to_all x1, starting transfers between devices, body(): grad = lax.all_to_all(grad, PART, 0, 0, tiled=True)  13.4 us
    ppermute x3, starting transfers between devices, to_part(): return lax.ppermute(block, PART, [(i, i ^ d) for i in range(4)])  12.3 us
    all_to_all x1, blocking collectives, body(): turned = lax.all_to_all(turned, RING, 0, 0, tiled=True)  12.2 us
  transfers between devices with their start and end apart: 13, of which 9 were waited for; matrix products, arithmetic and copies ran while one was open for 1% of the time, Pallas kernels for 1%

profile of v10, /device:TPU:1, one launch (start us, length us, event | category | flops | bytes accessed | tf_op | source)
XLA Modules:
  0.0 220.6 jit_solution(11504214157900268451)
XLA Ops:
  7.5 1.1 shard_map.55
  11.0 13.4 %all-to-all-start = ((bf16[4,72,288]{2,1,0:T(8,128)(2,1)}), bf16[4,72,288]{2,1,0:T(8,128)(2,1)S(1)}, u32[]{:S(2)}, u32[]{:S(2)}) async-start(bf16[4,72,288]{2,1,0:T(8,128)(2,1)} %shard_map.56), calls=%async_computation | async-start | bytes 442368 | tf_op jit(solution)/shard_map/all_to_all | solution.py:224
  24.4 5.7 %collective-permute-start.1 = (bf16[72,576]{1,0:T(8,128)(2,1)S(1)}, bf16[72,576]{1,0:T(8,128)(2,1)S(1)}, u32[]{:S(2)}, u32[]{:S(2)}) collective-permute-start(bf16[72,576]{1,0:T(8,128)(2,1)S(1)} %slice_select_fusion), channel_id=1, source_target_pairs={{0,0},{1,16},{16,64},{17,80},{32,1},{33,17},{48,65},{49,81},{64,32... | collective-permute-start | bytes 248840 | tf_op jit(solution)/shard_map/ppermute | solution.py:221
  30.1 3.2 %all-to-all-done.got = bf16[4,72,288]{2,1,0:T(8,128)(2,1)S(1)} async-done(((bf16[4,72,288]{2,1,0:T(8,128)(2,1)}), bf16[4,72,288]{2,1,0:T(8,128)(2,1)S(1)}, u32[]{:S(2)}, u32[]{:S(2)}) %all-to-all-start) | async-done | bytes 165920 | tf_op jit(solution)/shard_map/all_to_all | solution.py:224
  34.3 2.4 %collective-permute-done.1 = bf16[72,576]{1,0:T(8,128)(2,1)S(1)} collective-permute-done((bf16[72,576]{1,0:T(8,128)(2,1)S(1)}, bf16[72,576]{1,0:T(8,128)(2,1)S(1)}, u32[]{:S(2)}, u32[]{:S(2)}) %collective-permute-start.1) | collective-permute-done | bytes 82976 | tf_op jit(solution)/shard_map/ppermute | solution.py:221
  36.7 14.1 %all_to_all.40 = bf16[8,72,576]{2,1,0:T(8,128)(2,1)S(1)} all-to-all(bf16[8,72,576]{2,1,0:T(8,128)(2,1)S(1)} %broadcast_in_dim.12), channel_id=1, replica_groups=mesh['x'=4,'z1'=2,'z0'=2,'c'=2,'y'=8,'z2'=2] {'x','z0'}, dimensions={0} | all-to-all | bytes 1327104 | tf_op jit(solution)/shard_map/all_to_all | solution.py:17
  50.8 7.7 %all-to-all-start.1 = ((bf16[8,72,576]{2,1,0:T(8,128)(2,1)}), bf16[8,72,576]{2,1,0:T(8,128)(2,1)S(1)}, u32[]{:S(2)}, u32[]{:S(2)}) async-start(bf16[8,72,576]{2,1,0:T(8,128)(2,1)} %shard_map.57), calls=%async_computation.1 | async-start | bytes 1474560 | tf_op jit(solution)/shard_map/all_to_all | solution.py:230
  58.6 5.3 %collective-permute-start.2 = (bf16[8,72,576]{2,1,0:T(8,128)(2,1)S(1)}, bf16[8,72,576]{2,1,0:T(8,128)(2,1)}, u32[]{:S(2)}, u32[]{:S(2)}) collective-permute-start(bf16[8,72,576]{2,1,0:T(8,128)(2,1)S(1)} %all_to_all.40), channel_id=1, source_target_pairs={{0,16},{16,0},{1,17},{17,1},{2,18},{18,2},{3,19},{19,3},{4,20},{20... | collective-permute-start | bytes 1990664 | tf_op jit(solution)/shard_map/ppermute | solution.py:229
  63.8 14.1 %all-to-all-done.1.grad = bf16[8,72,576]{2,1,0:T(8,128)(2,1)S(1)} async-done(((bf16[8,72,576]{2,1,0:T(8,128)(2,1)}), bf16[8,72,576]{2,1,0:T(8,128)(2,1)S(1)}, u32[]{:S(2)}, u32[]{:S(2)}) %all-to-all-start.1) | async-done | bytes 663584 | tf_op jit(solution)/shard_map/all_to_all | solution.py:230
  78.0 1.9 maximum_select_fusion.basis
  79.9 1.4 shard_map.58
  81.3 5.3 %collective-permute-start.3 = (bf16[72,576]{1,0:T(8,128)(2,1)S(1)}, bf16[72,576]{1,0:T(8,128)(2,1)S(1)}, u32[]{:S(2)}, u32[]{:S(2)}) collective-permute-start(bf16[72,576]{1,0:T(8,128)(2,1)S(1)} %get-tuple-element.22), channel_id=1, source_target_pairs={{0,1},{1,0},{64,65},{65,64},{2,3},{3,2},{66,67},{67,66},{4,5},{5,4... | collective-permute-start | bytes 248840 | tf_op jit(solution)/shard_map/ppermute | solution.py:139
  86.6 4.9 %collective-permute-start.4 = (bf16[72,576]{1,0:T(8,128)(2,1)S(1)}, bf16[72,576]{1,0:T(8,128)(2,1)S(1)}, u32[]{:S(2)}, u32[]{:S(2)}) collective-permute-start(bf16[72,576]{1,0:T(8,128)(2,1)S(1)} %get-tuple-element.23), channel_id=1, source_target_pairs={{0,64},{1,65},{64,0},{65,1},{2,66},{3,67},{66,2},{67,3},{4,68},{5,... | collective-permute-start | bytes 248840 | tf_op jit(solution)/shard_map/ppermute | solution.py:139
  91.5 2.2 %collective-permute-start.5 = (bf16[72,576]{1,0:T(8,128)(2,1)S(1)}, bf16[72,576]{1,0:T(8,128)(2,1)S(1)}, u32[]{:S(2)}, u32[]{:S(2)}) collective-permute-start(bf16[72,576]{1,0:T(8,128)(2,1)S(1)} %get-tuple-element.24), channel_id=1, source_target_pairs={{0,65},{1,64},{64,1},{65,0},{2,67},{3,66},{66,3},{67,2},{4,69},{5,... | collective-permute-start | bytes 248840 | tf_op jit(solution)/shard_map/ppermute | solution.py:139
  93.7 4.2 %collective-permute-done.4.p2 = bf16[72,576]{1,0:T(8,128)(2,1)S(1)} collective-permute-done((bf16[72,576]{1,0:T(8,128)(2,1)S(1)}, bf16[72,576]{1,0:T(8,128)(2,1)S(1)}, u32[]{:S(2)}, u32[]{:S(2)}) %collective-permute-start.4) | collective-permute-done | bytes 82976 | tf_op jit(solution)/shard_map/ppermute | solution.py:139
  97.8 1.1 collective-permute-done.5.p3
  99.0 12.2 %all_to_all.41.own = bf16[8,72,576]{2,1,0:T(8,128)(2,1)S(1)} all-to-all(bf16[8,72,576]{2,1,0:T(8,128)(2,1)S(1)} %shard_map.59), channel_id=1, replica_groups=mesh['x'=4,'z1'=2,'z0'=2,'c'=2,'y'=8,'z2'=2] {'x','z0'}, dimensions={0} | all-to-all | bytes 1327104 | tf_op jit(solution)/shard_map/all_to_all | solution.py:239
  111.2 7.8 %collective-permute-start.6 = (bf16[8,72,576]{2,1,0:T(8,128)(2,1)S(1)}, bf16[8,72,576]{2,1,0:T(8,128)(2,1)S(1)}, u32[]{:S(2)}, u32[]{:S(2)}) collective-permute-start(bf16[8,72,576]{2,1,0:T(8,128)(2,1)S(1)} %all_to_all.41.own), channel_id=1, source_target_pairs={{0,16},{16,0},{1,17},{17,1},{2,18},{18,2},{3,19},{19,3},{4,20},{20... | collective-permute-start | bytes 1990664 | tf_op jit(solution)/shard_map/ppermute | solution.py:240
  119.1 1.8 collective-permute-done.6.other
  120.9 1.4 copy-done.1
  122.3 1.9 shard_map.60
  124.2 3.6 %all-to-all-start.4 = ((bf16[4,72,576]{2,1,0:T(8,128)(2,1)}), bf16[4,72,576]{2,1,0:T(8,128)(2,1)S(1)}, u32[]{:S(2)}, u32[]{:S(2)}) async-start(bf16[4,72,576]{2,1,0:T(8,128)(2,1)} %shard_map.60), calls=%async_computation.4 | async-start | bytes 737280 | tf_op jit(solution)/shard_map/all_to_all | solution.py:244
  128.7 8.7 %all-to-all-done.4.got = bf16[4,72,576]{2,1,0:T(8,128)(2,1)S(1)} async-done(((bf16[4,72,576]{2,1,0:T(8,128)(2,1)}), bf16[4,72,576]{2,1,0:T(8,128)(2,1)S(1)}, u32[]{:S(2)}, u32[]{:S(2)}) %all-to-all-start.4) | async-done | bytes 331808 | tf_op jit(solution)/shard_map/all_to_all | solution.py:244
  137.6 17.7 %all_to_all.42.scaled = bf16[4,72,576]{2,1,0:T(8,128)(2,1)S(1)} all-to-all(bf16[4,72,576]{2,1,0:T(8,128)(2,1)S(1)} %shard_map.61), channel_id=1, replica_groups=mesh['x'=4,'z1'=2,'z0'=2,'c'=2,'y'=8,'z2'=2] {'z1','z2'}, dimensions={0} | all-to-all | bytes 663552 | tf_op jit(solution)/shard_map/all_to_all | solution.py:246
  155.3 2.6 %shard_map.62 = bf16[8,72,576]{2,1,0:T(8,128)(2,1)S(1)} custom-call(bf16[4,72,576]{2,1,0:T(8,128)(2,1)S(1)} %all_to_all.42.scaled, bf16[8,144,576]{2,1,0:T(8,128)(2,1)S(1)} %maximum_select_fusion.basis), custom_call_target="tpu_custom_call" | custom-call | flops 382205952 | bytes 2322432 | tf_op jit(solution)/shard_map/pallas_call | solution.py:57
  157.9 21.9 %all_to_all.43 = bf16[8,72,576]{2,1,0:T(8,128)(2,1)S(1)} all-to-all(bf16[8,72,576]{2,1,0:T(8,128)(2,1)S(1)} %shard_map.62), channel_id=1, replica_groups=mesh['x'=4,'z1'=2,'z0'=2,'c'=2,'y'=8,'z2'=2] {'y'}, dimensions={0} | all-to-all | bytes 1327104 | tf_op jit(solution)/shard_map/all_to_all | solution.py:23
  179.9 4.9 %collective-permute-start.7 = (bf16[72,576]{1,0:T(8,128)(2,1)S(1)}, bf16[72,576]{1,0:T(8,128)(2,1)S(1)}, u32[]{:S(2)}, u32[]{:S(2)}) collective-permute-start(bf16[72,576]{1,0:T(8,128)(2,1)S(1)} %reduce_sum.12.mine), channel_id=1, source_target_pairs={{0,64},{64,0},{1,65},{65,1},{2,66},{66,2},{3,67},{67,3},{4,68},{68... | collective-permute-start | bytes 248840 | tf_op jit(solution)/shard_map/ppermute | solution.py:250
  184.8 1.9 collective-permute-done.7.other
  186.7 2.3 %shard_map.63 = (bf16[8,72,576]{2,1,0:T(8,128)(2,1)S(1)}, bf16[8,72,576]{2,1,0:T(8,128)(2,1)S(1)}) custom-call(s32[1]{0:T(128)} %bitcast.1.part, bf16[8,2,72,576]{3,2,1,0:T(8,128)(2,1)S(1)} %bitcast.9, bf16[72,576]{1,0:T(8,128)(2,1)S(1)} %reduce_sum.12.mine, bf16[72,576]{1,0:T(8,128)(2,1)S(1)} %collective-permute-done.7.other), custom_call_target="tpu_custom_call" | custom-call | flops 382205952 | bytes 2820100 | tf_op jit(solution)/shard_map/pallas_call | solution.py:57
  189.1 6.0 %collective-permute-start.8 = (bf16[8,72,576]{2,1,0:T(8,128)(2,1)S(1)}, bf16[8,72,576]{2,1,0:T(8,128)(2,1)S(1)}, u32[]{:S(2)}, u32[]{:S(2)}) collective-permute-start(bf16[8,72,576]{2,1,0:T(8,128)(2,1)S(1)} %get-tuple-element.26), channel_id=1, source_target_pairs={{0,16},{16,0},{1,17},{17,1},{2,18},{18,2},{3,19},{19,3},{4,20},{20... | collective-permute-start | bytes 1990664 | tf_op jit(solution)/shard_map/ppermute | solution.py:259
  195.1 1.8 collective-permute-done.8
  197.2 15.7 %all_to_all.44.got = bf16[8,72,576]{2,1,0:T(8,128)(2,1)S(1)} all-to-all(bf16[8,72,576]{2,1,0:T(8,128)(2,1)S(1)} %add_convert_fusion), channel_id=1, replica_groups=mesh['x'=4,'z1'=2,'z0'=2,'c'=2,'y'=8,'z2'=2] {'x','z0'}, dimensions={0} | all-to-all | bytes 1327104 | tf_op jit(solution)/shard_map/all_to_all | solution.py:260
  (34 shorter events, 6.8 us)
Async XLA Ops:
  6.5 121.2 %copy-start = (f32[4608]{0:T(1024)S(1)}, f32[4608]{0:T(1024)}, u32[]{:S(2)}) copy-start(f32[4608]{0:T(1024)} %param.9) | copy-start | bytes 55300
  6.5 1.0 copy-start.3
  7.5 16.9 %copy-start.5 = (f32[144,576]{1,0:T(8,128)S(1)}, f32[144,576]{1,0:T(8,128)}, u32[]{:S(2)}) copy-start(f32[144,576]{1,0:T(8,128)} %param.6) | copy-start | bytes 995332
  8.6 28.1 %collective-permute-start = (bf16[2,72,576]{2,1,0:T(8,128)(2,1)S(1)}, bf16[2,72,576]{2,1,0:T(8,128)(2,1)S(1)}, u32[]{:S(2)}, u32[]{:S(2)}) collective-permute-start(bf16[2,72,576]{2,1,0:T(8,128)(2,1)S(1)} %shard_map.55), channel_id=1, source_target_pairs={{0,0},{2,64},{4,4},{6,68},{8,8},{10,72},{12,12},{14,76},{64,2},{66... | collective-permute-start | bytes 497672 | tf_op jit(solution)/shard_map/ppermute | solution.py:217
  9.3 0.9 copy-start.4
  11.0 22.3 %all-to-all-start = ((bf16[4,72,288]{2,1,0:T(8,128)(2,1)}), bf16[4,72,288]{2,1,0:T(8,128)(2,1)S(1)}, u32[]{:S(2)}, u32[]{:S(2)}) async-start(bf16[4,72,288]{2,1,0:T(8,128)(2,1)} %shard_map.56), calls=%async_computation | async-start | bytes 442368 | tf_op jit(solution)/shard_map/all_to_all | solution.py:224
  24.4 12.2 %collective-permute-start.1 = (bf16[72,576]{1,0:T(8,128)(2,1)S(1)}, bf16[72,576]{1,0:T(8,128)(2,1)S(1)}, u32[]{:S(2)}, u32[]{:S(2)}) collective-permute-start(bf16[72,576]{1,0:T(8,128)(2,1)S(1)} %slice_select_fusion), channel_id=1, source_target_pairs={{0,0},{1,16},{16,64},{17,80},{32,1},{33,17},{48,65},{49,81},{64,32... | collective-permute-start | bytes 248840 | tf_op jit(solution)/shard_map/ppermute | solution.py:221
  36.7 14.2 %copy-start.6 = (bf16[2,72,576]{2,1,0:T(8,128)(2,1)}, bf16[2,72,576]{2,1,0:T(8,128)(2,1)S(1)}, u32[]{:S(2)}) copy-start(bf16[2,72,576]{2,1,0:T(8,128)(2,1)S(1)} %collective-permute-done) | copy-start | bytes 497668
  50.8 27.1 %all-to-all-start.1 = ((bf16[8,72,576]{2,1,0:T(8,128)(2,1)}), bf16[8,72,576]{2,1,0:T(8,128)(2,1)S(1)}, u32[]{:S(2)}, u32[]{:S(2)}) async-start(bf16[8,72,576]{2,1,0:T(8,128)(2,1)} %shard_map.57), calls=%async_computation.1 | async-start | bytes 1474560 | tf_op jit(solution)/shard_map/all_to_all | solution.py:230
  58.5 60.6 %all-gather.3.cloned.1.call-start = ((), (), s32[]{:S(2)}) async-start(), calls=%async_computation.8 | async-start | bytes 1658880 | tf_op jit(solution)/shard_map/all_gather | solution.py:233
  58.6 19.4 %collective-permute-start.2 = (bf16[8,72,576]{2,1,0:T(8,128)(2,1)S(1)}, bf16[8,72,576]{2,1,0:T(8,128)(2,1)}, u32[]{:S(2)}, u32[]{:S(2)}) collective-permute-start(bf16[8,72,576]{2,1,0:T(8,128)(2,1)S(1)} %all_to_all.40), channel_id=1, source_target_pairs={{0,16},{16,0},{1,17},{17,1},{2,18},{18,2},{3,19},{19,3},{4,20},{20... | collective-permute-start | bytes 1990664 | tf_op jit(solution)/shard_map/ppermute | solution.py:229
  81.3 12.4 %collective-permute-start.3 = (bf16[72,576]{1,0:T(8,128)(2,1)S(1)}, bf16[72,576]{1,0:T(8,128)(2,1)S(1)}, u32[]{:S(2)}, u32[]{:S(2)}) collective-permute-start(bf16[72,576]{1,0:T(8,128)(2,1)S(1)} %get-tuple-element.22), channel_id=1, source_target_pairs={{0,1},{1,0},{64,65},{65,64},{2,3},{3,2},{66,67},{67,66},{4,5},{5,4... | collective-permute-start | bytes 248840 | tf_op jit(solution)/shard_map/ppermute | solution.py:139
  86.6 11.3 %collective-permute-start.4 = (bf16[72,576]{1,0:T(8,128)(2,1)S(1)}, bf16[72,576]{1,0:T(8,128)(2,1)S(1)}, u32[]{:S(2)}, u32[]{:S(2)}) collective-permute-start(bf16[72,576]{1,0:T(8,128)(2,1)S(1)} %get-tuple-element.23), channel_id=1, source_target_pairs={{0,64},{1,65},{64,0},{65,1},{2,66},{3,67},{66,2},{67,3},{4,68},{5,... | collective-permute-start | bytes 248840 | tf_op jit(solution)/shard_map/ppermute | solution.py:139
  91.5 7.5 %collective-permute-start.5 = (bf16[72,576]{1,0:T(8,128)(2,1)S(1)}, bf16[72,576]{1,0:T(8,128)(2,1)S(1)}, u32[]{:S(2)}, u32[]{:S(2)}) collective-permute-start(bf16[72,576]{1,0:T(8,128)(2,1)S(1)} %get-tuple-element.24), channel_id=1, source_target_pairs={{0,65},{1,64},{64,1},{65,0},{2,67},{3,66},{66,3},{67,2},{4,69},{5,... | collective-permute-start | bytes 248840 | tf_op jit(solution)/shard_map/ppermute | solution.py:139
  111.2 9.6 %collective-permute-start.6 = (bf16[8,72,576]{2,1,0:T(8,128)(2,1)S(1)}, bf16[8,72,576]{2,1,0:T(8,128)(2,1)S(1)}, u32[]{:S(2)}, u32[]{:S(2)}) collective-permute-start(bf16[8,72,576]{2,1,0:T(8,128)(2,1)S(1)} %all_to_all.41.own), channel_id=1, source_target_pairs={{0,16},{16,0},{1,17},{17,1},{2,18},{18,2},{3,19},{19,3},{4,20},{20... | collective-permute-start | bytes 1990664 | tf_op jit(solution)/shard_map/ppermute | solution.py:240
  120.9 1.4 copy-start.1
  124.2 13.3 %all-to-all-start.4 = ((bf16[4,72,576]{2,1,0:T(8,128)(2,1)}), bf16[4,72,576]{2,1,0:T(8,128)(2,1)S(1)}, u32[]{:S(2)}, u32[]{:S(2)}) async-start(bf16[4,72,576]{2,1,0:T(8,128)(2,1)} %shard_map.60), calls=%async_computation.4 | async-start | bytes 737280 | tf_op jit(solution)/shard_map/all_to_all | solution.py:244
  157.8 28.9 %copy-start.2 = (bf16[16,72,576]{2,1,0:T(8,128)(2,1)S(1)}, bf16[16,72,576]{2,1,0:T(8,128)(2,1)}, u32[]{:S(2)}) copy-start(bf16[16,72,576]{2,1,0:T(8,128)(2,1)} %all-gather.3.cloned.1.call-done) | copy-start | bytes 3981316
  179.9 6.9 %collective-permute-start.7 = (bf16[72,576]{1,0:T(8,128)(2,1)S(1)}, bf16[72,576]{1,0:T(8,128)(2,1)S(1)}, u32[]{:S(2)}, u32[]{:S(2)}) collective-permute-start(bf16[72,576]{1,0:T(8,128)(2,1)S(1)} %reduce_sum.12.mine), channel_id=1, source_target_pairs={{0,64},{64,0},{1,65},{65,1},{2,66},{66,2},{3,67},{67,3},{4,68},{68... | collective-permute-start | bytes 248840 | tf_op jit(solution)/shard_map/ppermute | solution.py:250
  189.1 7.9 %collective-permute-start.8 = (bf16[8,72,576]{2,1,0:T(8,128)(2,1)S(1)}, bf16[8,72,576]{2,1,0:T(8,128)(2,1)S(1)}, u32[]{:S(2)}, u32[]{:S(2)}) collective-permute-start(bf16[8,72,576]{2,1,0:T(8,128)(2,1)S(1)} %get-tuple-element.26), channel_id=1, source_target_pairs={{0,16},{16,0},{1,17},{17,1},{2,18},{18,2},{3,19},{19,3},{4,20},{20... | collective-permute-start | bytes 1990664 | tf_op jit(solution)/shard_map/ppermute | solution.py:259
Sparse Core Ops, SparseCore 0:
  78.0 33.1 all-gather.2

commit v11 on v10

--- a/solution.py
+++ b/solution.py
@@ -13,12 +13,6 @@
 SWAP = [(0, 1), (1, 0)]
 
 
-def gather(block, axes, count):
-    return lax.all_to_all(
-        jnp.broadcast_to(block[None], (count,) + block.shape), axes, 0, 0, tiled=True
-    )
-
-
 def scatter_sum(blocks, axes):
     got = lax.all_to_all(blocks, axes, 0, 0, tiled=True)
     return jnp.sum(got.astype(jnp.float32), axis=0)
@@ -27,14 +21,6 @@
 def dot(left, right, left_dim, right_dim):
     return lax.dot_general(
         left, right, (((left_dim,), (right_dim,)), ((), ())), preferred_element_type=jnp.float32
-    )
-
-
-def in_order(first, mine, other, axis):
-    return jnp.where(
-        first,
-        jnp.concatenate([mine, other], axis=axis),
-        jnp.concatenate([other, mine], axis=axis),
     )
 
 
@@ -202,7 +188,6 @@
     rows, cols = basis_in.shape
     half, quarter = rows // 2, cols // 4
     wide = 2 * rows
-    low_core, low_rep = c == 0, z2 == 0
 
 
     core, rep, part_z1, this_part = (
@@ -213,20 +198,19 @@
     out_scale = lax.dynamic_slice_in_dim(eig_out, first, half, 0)[:, None]
     in_scale = lax.dynamic_slice_in_dim(eig_in, y * cols, cols, 0)[None, :]
 
+    bi = basis_in.astype(bf16)
+    bi = lax.ppermute(bi, ("z1", "z0", "c", "z2"), pairs_rows())
+    bi, grad_parts = lax.optimization_barrier((bi, grad_parts))
+    bi = lax.all_gather(bi, RING, axis=0)
+
     bo = run(order_out, shape(2, half, cols), (core, rep, basis_out), flags=2)
     bo = lax.ppermute(bo, ("z1", "y"), pairs_z1y0())
-
-    bi = basis_in.astype(bf16)
-    bi = jnp.where(low_rep, bi[:half], bi[half:])
-    bi = lax.ppermute(bi, ("z1", "z0", "c", "z2"), pairs_rows())
 
     grad = run(cut_grad, shape(4, half, wide), (grad_parts[0],))
     grad = lax.all_to_all(grad, PART, 0, 0, tiled=True)
     grad = run(join_grad, shape(8, half, cols), (grad,))
 
-    bo, bi, grad = lax.optimization_barrier((bo, bi, grad))
-    bi = gather(bi, RING, 8)
-    bi = in_order(low_core, bi, lax.ppermute(bi, "c", SWAP), 1)
+    bo, grad = lax.optimization_barrier((bo, grad))
     grad = lax.all_to_all(grad, "y", 0, 0, tiled=True)
 
     bo, grad = lax.optimization_barrier((bo, grad))

time: 221 us -> 217 us (0.982)
  starting transfers between devices: 67.4 us -> 47.4 us
  waiting for transfers between devices: 39.2 us -> 49.7 us
  blocking collectives: 81.6 us -> 87.2 us
    all_to_all x1 -> x0, waiting for transfers between devices: 14.1 us -> none  [body(): grad = lax.all_to_all(grad, 'y', 0, 0, tiled=True)]
    all_gather x0 -> x1, waiting for transfers between devices: none -> 12.3 us  [body(): bi = lax.all_gather(bi, RING, axis=0)]
    all_to_all x1, starting transfers between devices: 13.4 us -> 4.47 us  [body(): grad = lax.all_to_all(grad, PART, 0, 0, tiled=True)]
    all_to_all x1, blocking collectives: 14.1 us -> 21.9 us  [body(): grad = lax.all_to_all(grad, 'y', 0, 0, tiled=True)]
    all_to_all x1 -> x0, starting transfers between devices: 7.67 us -> none  [body(): grad = lax.all_to_all(grad, 'y', 0, 0, tiled=True)]
    ppermute x1, waiting for transfers between devices: 2.39 us -> 8.14 us  [body(): bi = lax.ppermute(bi, ('z1', 'z0', 'c', 'z2'), pairs_rows())]
    ppermute x1 -> x0, starting transfers between devices: 5.26 us -> none  [body(): bi = in_order(low_core, bi, lax.ppermute(bi, 'c', SWAP), 1)]
    all_to_all x1, blocking collectives: 12.2 us -> 17 us  [body(): turned = lax.all_to_all(turned, RING, 0, 0, tiled=True)]
  transfers between devices with their start and end apart: 13 -> 12, of which waited for: 9 -> 9; matrix products, arithmetic and copies ran while one was open for 1% -> 0% of each run, Pallas kernels for 1% -> 2%
where the time goes in v11:
time: 217 us; the launch traced here: 216 us
  blocking collectives  87.2 us (40%)
  waiting for transfers between devices  49.7 us (23%)
  starting transfers between devices  47.4 us (22%)
  between operations  13.6 us (6%)
  Pallas kernels  11.2 us (5%)
  local copies, waits for them, and re-layouts  5.31 us (2%)
    all_to_all x1, blocking collectives, body(): grad = lax.all_to_all(grad, 'y', 0, 0, tiled=True)  21.9 us
    all_to_all x1, blocking collectives, scatter_sum(): got = lax.all_to_all(blocks, axes, 0, 0, tiled=True)  20.6 us
    all_to_all x1, blocking collectives, body(): turned = lax.all_to_all(turned, RING, 0, 0, tiled=True)  17 us
    all_to_all x1, blocking collectives, body(): part = lax.all_to_all(part, RING, 0, 0, tiled=True)  14.3 us
    all_to_all x1, blocking collectives, body(): scaled = lax.all_to_all(scaled, PART, 0, 0, tiled=True)  13.4 us
    ppermute x3, starting transfers between devices, to_part(): return lax.ppermute(block, PART, [(i, i ^ d) for i in range(4)])  12.7 us
    all_gather x1, waiting for transfers between devices, body(): bi = lax.all_gather(bi, RING, axis=0)  12.3 us
    pallas_call x10, Pallas kernels, run(): pl.pallas_call(kernel, out_shape=outs, in_specs=[pl.BlockSpec(memory_spac...  11.2 us
  transfers between devices with their start and end apart: 12, of which 9 were waited for; matrix products, arithmetic and copies ran while one was open for 0% of the time, Pallas kernels for 2%

profile of v11, /device:TPU:1, one launch (start us, length us, event | category | flops | bytes accessed | tf_op | source)
XLA Modules:
  0.0 215.8 jit_solution(224420496485147259)
XLA Ops:
  6.5 1.1 convert_element_type.14
  7.6 7.2 %collective-permute-start.1 = (bf16[144,576]{1,0:T(8,128)(2,1)S(1)}, bf16[144,576]{1,0:T(8,128)(2,1)S(1)}, u32[]{:S(2)}, u32[]{:S(2)}) collective-permute-start(bf16[144,576]{1,0:T(8,128)(2,1)S(1)} %convert_element_type.14), channel_id=1, source_target_pairs={{0,0},{1,16},{16,64},{17,80},{32,1},{33,17},{48,65},{49,81},{64,32... | collective-permute-start | bytes 497672 | tf_op jit(solution)/shard_map/ppermute | solution.py:202
  14.8 8.1 %collective-permute-done.1 = bf16[144,576]{1,0:T(8,128)(2,1)S(1)} collective-permute-done((bf16[144,576]{1,0:T(8,128)(2,1)S(1)}, bf16[144,576]{1,0:T(8,128)(2,1)S(1)}, u32[]{:S(2)}, u32[]{:S(2)}) %collective-permute-start.1) | collective-permute-done | bytes 165920 | tf_op jit(solution)/shard_map/ppermute | solution.py:202
  23.7 0.9 copy-done.6
  25.4 4.5 %all-to-all-start = ((bf16[4,72,288]{2,1,0:T(8,128)(2,1)}), bf16[4,72,288]{2,1,0:T(8,128)(2,1)S(1)}, u32[]{:S(2)}, u32[]{:S(2)}) async-start(bf16[4,72,288]{2,1,0:T(8,128)(2,1)} %shard_map.56), calls=%async_computation | async-start | bytes 442368 | tf_op jit(solution)/shard_map/all_to_all | solution.py:210
  29.9 1.1 shard_map.55
  31.6 6.5 %all-to-all-done.got = bf16[4,72,288]{2,1,0:T(8,128)(2,1)S(1)} async-done(((bf16[4,72,288]{2,1,0:T(8,128)(2,1)}), bf16[4,72,288]{2,1,0:T(8,128)(2,1)S(1)}, u32[]{:S(2)}, u32[]{:S(2)}) %all-to-all-start) | async-done | bytes 165920 | tf_op jit(solution)/shard_map/all_to_all | solution.py:210
  38.3 21.9 %all_to_all.35.grad = bf16[8,72,576]{2,1,0:T(8,128)(2,1)S(1)} all-to-all(bf16[8,72,576]{2,1,0:T(8,128)(2,1)S(1)} %shard_map.57), channel_id=1, replica_groups=mesh['x'=4,'z1'=2,'z0'=2,'c'=2,'y'=8,'z2'=2] {'y'}, dimensions={0} | all-to-all | bytes 1327104 | tf_op jit(solution)/shard_map/all_to_all | solution.py:214
  60.3 12.3 %all-gather.7.cloned.1.call-done = bf16[1152,576]{1,0:T(8,128)(2,1)} async-done(((bf16[144,576]{1,0:T(8,128)(2,1)}), bf16[1152,576]{1,0:T(8,128)(2,1)}) %all-gather.7.cloned.1.call-update) | async-done | bytes 1327120 | tf_op jit(solution)/shard_map/all_gather | solution.py:204
  72.6 1.4 copy-done.1
  74.0 1.4 shard_map.58
  75.4 8.4 %collective-permute-start.2 = (bf16[72,576]{1,0:T(8,128)(2,1)S(1)}, bf16[72,576]{1,0:T(8,128)(2,1)S(1)}, u32[]{:S(2)}, u32[]{:S(2)}) collective-permute-start(bf16[72,576]{1,0:T(8,128)(2,1)S(1)} %get-tuple-element.24), channel_id=1, source_target_pairs={{0,1},{1,0},{64,65},{65,64},{2,3},{3,2},{66,67},{67,66},{4,5},{5,4... | collective-permute-start | bytes 248840 | tf_op jit(solution)/shard_map/ppermute | solution.py:125
  83.7 2.4 %collective-permute-start.3 = (bf16[72,576]{1,0:T(8,128)(2,1)S(1)}, bf16[72,576]{1,0:T(8,128)(2,1)S(1)}, u32[]{:S(2)}, u32[]{:S(2)}) collective-permute-start(bf16[72,576]{1,0:T(8,128)(2,1)S(1)} %get-tuple-element.25), channel_id=1, source_target_pairs={{0,64},{1,65},{64,0},{65,1},{2,66},{3,67},{66,2},{67,3},{4,68},{5,... | collective-permute-start | bytes 248840 | tf_op jit(solution)/shard_map/ppermute | solution.py:125
  86.2 1.9 collective-permute-start.4
  88.1 5.1 %collective-permute-done.3.p2 = bf16[72,576]{1,0:T(8,128)(2,1)S(1)} collective-permute-done((bf16[72,576]{1,0:T(8,128)(2,1)S(1)}, bf16[72,576]{1,0:T(8,128)(2,1)S(1)}, u32[]{:S(2)}, u32[]{:S(2)}) %collective-permute-start.3) | collective-permute-done | bytes 82976 | tf_op jit(solution)/shard_map/ppermute | solution.py:125
  93.2 1.3 collective-permute-done.4.p3
  94.6 17.0 %all_to_all.36.own = bf16[8,72,576]{2,1,0:T(8,128)(2,1)S(1)} all-to-all(bf16[8,72,576]{2,1,0:T(8,128)(2,1)S(1)} %shard_map.59), channel_id=1, replica_groups=mesh['x'=4,'z1'=2,'z0'=2,'c'=2,'y'=8,'z2'=2] {'x','z0'}, dimensions={0} | all-to-all | bytes 1327104 | tf_op jit(solution)/shard_map/all_to_all | solution.py:223
  111.6 4.2 %collective-permute-start.5 = (bf16[8,72,576]{2,1,0:T(8,128)(2,1)S(1)}, bf16[8,72,576]{2,1,0:T(8,128)(2,1)S(1)}, u32[]{:S(2)}, u32[]{:S(2)}) collective-permute-start(bf16[8,72,576]{2,1,0:T(8,128)(2,1)S(1)} %all_to_all.36.own), channel_id=1, source_target_pairs={{0,16},{16,0},{1,17},{17,1},{2,18},{18,2},{3,19},{19,3},{4,20},{20... | collective-permute-start | bytes 1990664 | tf_op jit(solution)/shard_map/ppermute | solution.py:224
  115.9 1.8 collective-permute-done.5.other
  117.7 1.4 copy-done.3
  119.0 1.9 shard_map.60
  120.9 4.9 %all-to-all-start.3 = ((bf16[4,72,576]{2,1,0:T(8,128)(2,1)}), bf16[4,72,576]{2,1,0:T(8,128)(2,1)S(1)}, u32[]{:S(2)}, u32[]{:S(2)}) async-start(bf16[4,72,576]{2,1,0:T(8,128)(2,1)} %shard_map.60), calls=%async_computation.3 | async-start | bytes 737280 | tf_op jit(solution)/shard_map/all_to_all | solution.py:228
  126.8 7.7 %all-to-all-done.3.got = bf16[4,72,576]{2,1,0:T(8,128)(2,1)S(1)} async-done(((bf16[4,72,576]{2,1,0:T(8,128)(2,1)}), bf16[4,72,576]{2,1,0:T(8,128)(2,1)S(1)}, u32[]{:S(2)}, u32[]{:S(2)}) %all-to-all-start.3) | async-done | bytes 331808 | tf_op jit(solution)/shard_map/all_to_all | solution.py:228
  134.6 13.4 %all_to_all.37.scaled = bf16[4,72,576]{2,1,0:T(8,128)(2,1)S(1)} all-to-all(bf16[4,72,576]{2,1,0:T(8,128)(2,1)S(1)} %shard_map.61), channel_id=1, replica_groups=mesh['x'=4,'z1'=2,'z0'=2,'c'=2,'y'=8,'z2'=2] {'z1','z2'}, dimensions={0} | all-to-all | bytes 663552 | tf_op jit(solution)/shard_map/all_to_all | solution.py:230
  148.1 2.6 %shard_map.62 = bf16[8,72,576]{2,1,0:T(8,128)(2,1)S(1)} custom-call(bf16[4,72,576]{2,1,0:T(8,128)(2,1)S(1)} %all_to_all.37.scaled, bf16[8,144,576]{2,1,0:T(8,128)(2,1)S(1)} %bitcast.10), custom_call_target="tpu_custom_call" | custom-call | flops 382205952 | bytes 2322432 | tf_op jit(solution)/shard_map/pallas_call | solution.py:43
  150.6 20.6 %all_to_all.38 = bf16[8,72,576]{2,1,0:T(8,128)(2,1)S(1)} all-to-all(bf16[8,72,576]{2,1,0:T(8,128)(2,1)S(1)} %shard_map.62), channel_id=1, replica_groups=mesh['x'=4,'z1'=2,'z0'=2,'c'=2,'y'=8,'z2'=2] {'y'}, dimensions={0} | all-to-all | bytes 1327104 | tf_op jit(solution)/shard_map/all_to_all | solution.py:17
  171.3 2.4 %collective-permute-start.6 = (bf16[72,576]{1,0:T(8,128)(2,1)S(1)}, bf16[72,576]{1,0:T(8,128)(2,1)S(1)}, u32[]{:S(2)}, u32[]{:S(2)}) collective-permute-start(bf16[72,576]{1,0:T(8,128)(2,1)S(1)} %reduce_sum.12.mine), channel_id=1, source_target_pairs={{0,64},{64,0},{1,65},{65,1},{2,66},{66,2},{3,67},{67,3},{4,68},{68... | collective-permute-start | bytes 248840 | tf_op jit(solution)/shard_map/ppermute | solution.py:234
  173.7 4.9 %collective-permute-done.6.other = bf16[72,576]{1,0:T(8,128)(2,1)S(1)} collective-permute-done((bf16[72,576]{1,0:T(8,128)(2,1)S(1)}, bf16[72,576]{1,0:T(8,128)(2,1)S(1)}, u32[]{:S(2)}, u32[]{:S(2)}) %collective-permute-start.6) | collective-permute-done | bytes 82976 | tf_op jit(solution)/shard_map/ppermute | solution.py:234
  178.7 2.3 %shard_map.63 = (bf16[8,72,576]{2,1,0:T(8,128)(2,1)S(1)}, bf16[8,72,576]{2,1,0:T(8,128)(2,1)S(1)}) custom-call(s32[1]{0:T(128)} %bitcast.1.part, bf16[8,2,72,576]{3,2,1,0:T(8,128)(2,1)S(1)} %bitcast.12, bf16[72,576]{1,0:T(8,128)(2,1)S(1)} %reduce_sum.12.mine, bf16[72,576]{1,0:T(8,128)(2,1)S(1)} %collective-permute-done.6.other), custom_call_target="tpu_custom_call" | custom-call | flops 382205952 | bytes 2820100 | tf_op jit(solution)/shard_map/pallas_call | solution.py:43
  181.0 10.8 %collective-permute-start.7 = (bf16[8,72,576]{2,1,0:T(8,128)(2,1)S(1)}, bf16[8,72,576]{2,1,0:T(8,128)(2,1)S(1)}, u32[]{:S(2)}, u32[]{:S(2)}) collective-permute-start(bf16[8,72,576]{2,1,0:T(8,128)(2,1)S(1)} %get-tuple-element.28), channel_id=1, source_target_pairs={{0,16},{16,0},{1,17},{17,1},{2,18},{18,2},{3,19},{19,3},{4,20},{20... | collective-permute-start | bytes 1990664 | tf_op jit(solution)/shard_map/ppermute | solution.py:243
  191.8 1.8 collective-permute-done.7
  193.8 14.3 %all_to_all.39.got = bf16[8,72,576]{2,1,0:T(8,128)(2,1)S(1)} all-to-all(bf16[8,72,576]{2,1,0:T(8,128)(2,1)S(1)} %add_convert_fusion), channel_id=1, replica_groups=mesh['x'=4,'z1'=2,'z0'=2,'c'=2,'y'=8,'z2'=2] {'x','z0'}, dimensions={0} | all-to-all | bytes 1327104 | tf_op jit(solution)/shard_map/all_to_all | solution.py:244
  (34 shorter events, 4.7 us)
Async XLA Ops:
  6.5 119.3 %copy-start = (f32[4608]{0:T(1024)S(1)}, f32[4608]{0:T(1024)}, u32[]{:S(2)}) copy-start(f32[4608]{0:T(1024)} %param.9) | copy-start | bytes 55300
  6.5 23.3 %copy-start.5 = (f32[144,576]{1,0:T(8,128)S(1)}, f32[144,576]{1,0:T(8,128)}, u32[]{:S(2)}) copy-start(f32[144,576]{1,0:T(8,128)} %rows.1) | copy-start | bytes 995332
  6.5 66.0 %all-gather.7.cloned.1.call-start = ((), (), s32[]{:S(2)}) async-start(), calls=%async_computation.8 | async-start | bytes 1658880 | tf_op jit(solution)/shard_map/all_gather | solution.py:204
  7.6 15.3 %collective-permute-start.1 = (bf16[144,576]{1,0:T(8,128)(2,1)S(1)}, bf16[144,576]{1,0:T(8,128)(2,1)S(1)}, u32[]{:S(2)}, u32[]{:S(2)}) collective-permute-start(bf16[144,576]{1,0:T(8,128)(2,1)S(1)} %convert_element_type.14), channel_id=1, source_target_pairs={{0,0},{1,16},{16,64},{17,80},{32,1},{33,17},{48,65},{49,81},{64,32... | collective-permute-start | bytes 497672 | tf_op jit(solution)/shard_map/ppermute | solution.py:202
  23.0 0.7 copy-start.8
  23.7 0.9 copy-start.6
  25.4 12.8 %all-to-all-start = ((bf16[4,72,288]{2,1,0:T(8,128)(2,1)}), bf16[4,72,288]{2,1,0:T(8,128)(2,1)S(1)}, u32[]{:S(2)}, u32[]{:S(2)}) async-start(bf16[4,72,288]{2,1,0:T(8,128)(2,1)} %shard_map.56), calls=%async_computation | async-start | bytes 442368 | tf_op jit(solution)/shard_map/all_to_all | solution.py:210
  29.9 86.0 %all-gather.5.cloned.1.call-start = ((), (), s32[]{:S(2)}) async-start(), calls=%async_computation.7 | async-start | bytes 1658880 | tf_op jit(solution)/shard_map/all_gather | solution.py:217
  31.0 7.3 %collective-permute-start = (bf16[2,72,576]{2,1,0:T(8,128)(2,1)S(1)}, bf16[2,72,576]{2,1,0:T(8,128)(2,1)S(1)}, u32[]{:S(2)}, u32[]{:S(2)}) collective-permute-start(bf16[2,72,576]{2,1,0:T(8,128)(2,1)S(1)} %shard_map.55), channel_id=1, source_target_pairs={{0,0},{2,64},{4,4},{6,68},{8,8},{10,72},{12,12},{14,76},{64,2},{66... | collective-permute-start | bytes 497672 | tf_op jit(solution)/shard_map/ppermute | solution.py:207
  38.3 21.9 %copy-start.7 = (bf16[2,72,576]{2,1,0:T(8,128)(2,1)}, bf16[2,72,576]{2,1,0:T(8,128)(2,1)S(1)}, u32[]{:S(2)}) copy-start(bf16[2,72,576]{2,1,0:T(8,128)(2,1)S(1)} %collective-permute-done) | copy-start | bytes 497668
  72.6 1.4 copy-start.1
  75.4 12.7 %collective-permute-start.2 = (bf16[72,576]{1,0:T(8,128)(2,1)S(1)}, bf16[72,576]{1,0:T(8,128)(2,1)S(1)}, u32[]{:S(2)}, u32[]{:S(2)}) collective-permute-start(bf16[72,576]{1,0:T(8,128)(2,1)S(1)} %get-tuple-element.24), channel_id=1, source_target_pairs={{0,1},{1,0},{64,65},{65,64},{2,3},{3,2},{66,67},{67,66},{4,5},{5,4... | collective-permute-start | bytes 248840 | tf_op jit(solution)/shard_map/ppermute | solution.py:125
  83.7 9.5 %collective-permute-start.3 = (bf16[72,576]{1,0:T(8,128)(2,1)S(1)}, bf16[72,576]{1,0:T(8,128)(2,1)S(1)}, u32[]{:S(2)}, u32[]{:S(2)}) collective-permute-start(bf16[72,576]{1,0:T(8,128)(2,1)S(1)} %get-tuple-element.25), channel_id=1, source_target_pairs={{0,64},{1,65},{64,0},{65,1},{2,66},{3,67},{66,2},{67,3},{4,68},{5,... | collective-permute-start | bytes 248840 | tf_op jit(solution)/shard_map/ppermute | solution.py:125
  86.2 8.3 %collective-permute-start.4 = (bf16[72,576]{1,0:T(8,128)(2,1)S(1)}, bf16[72,576]{1,0:T(8,128)(2,1)S(1)}, u32[]{:S(2)}, u32[]{:S(2)}) collective-permute-start(bf16[72,576]{1,0:T(8,128)(2,1)S(1)} %get-tuple-element.26), channel_id=1, source_target_pairs={{0,65},{1,64},{64,1},{65,0},{2,67},{3,66},{66,3},{67,2},{4,69},{5,... | collective-permute-start | bytes 248840 | tf_op jit(solution)/shard_map/ppermute | solution.py:125
  111.6 6.1 %collective-permute-start.5 = (bf16[8,72,576]{2,1,0:T(8,128)(2,1)S(1)}, bf16[8,72,576]{2,1,0:T(8,128)(2,1)S(1)}, u32[]{:S(2)}, u32[]{:S(2)}) collective-permute-start(bf16[8,72,576]{2,1,0:T(8,128)(2,1)S(1)} %all_to_all.36.own), channel_id=1, source_target_pairs={{0,16},{16,0},{1,17},{17,1},{2,18},{18,2},{3,19},{19,3},{4,20},{20... | collective-permute-start | bytes 1990664 | tf_op jit(solution)/shard_map/ppermute | solution.py:224
  117.7 1.4 copy-start.3
  120.9 27.2 %copy-start.2 = (bf16[1152,576]{1,0:T(8,128)(2,1)S(1)}, bf16[1152,576]{1,0:T(8,128)(2,1)}, u32[]{:S(2)}) copy-start(bf16[1152,576]{1,0:T(8,128)(2,1)} %all-gather.7.cloned.1.call-done) | copy-start | bytes 3981316
  120.9 13.6 %all-to-all-start.3 = ((bf16[4,72,576]{2,1,0:T(8,128)(2,1)}), bf16[4,72,576]{2,1,0:T(8,128)(2,1)S(1)}, u32[]{:S(2)}, u32[]{:S(2)}) async-start(bf16[4,72,576]{2,1,0:T(8,128)(2,1)} %shard_map.60), calls=%async_computation.3 | async-start | bytes 737280 | tf_op jit(solution)/shard_map/all_to_all | solution.py:228
  150.6 28.0 %copy-start.4 = (bf16[16,72,576]{2,1,0:T(8,128)(2,1)S(1)}, bf16[16,72,576]{2,1,0:T(8,128)(2,1)}, u32[]{:S(2)}) copy-start(bf16[16,72,576]{2,1,0:T(8,128)(2,1)} %all-gather.5.cloned.1.call-done) | copy-start | bytes 3981316
  171.3 7.3 %collective-permute-start.6 = (bf16[72,576]{1,0:T(8,128)(2,1)S(1)}, bf16[72,576]{1,0:T(8,128)(2,1)S(1)}, u32[]{:S(2)}, u32[]{:S(2)}) collective-permute-start(bf16[72,576]{1,0:T(8,128)(2,1)S(1)} %reduce_sum.12.mine), channel_id=1, source_target_pairs={{0,64},{64,0},{1,65},{65,1},{2,66},{66,2},{3,67},{67,3},{4,68},{68... | collective-permute-start | bytes 248840 | tf_op jit(solution)/shard_map/ppermute | solution.py:234
  181.0 12.6 %collective-permute-start.7 = (bf16[8,72,576]{2,1,0:T(8,128)(2,1)S(1)}, bf16[8,72,576]{2,1,0:T(8,128)(2,1)S(1)}, u32[]{:S(2)}, u32[]{:S(2)}) collective-permute-start(bf16[8,72,576]{2,1,0:T(8,128)(2,1)S(1)} %get-tuple-element.28), channel_id=1, source_target_pairs={{0,16},{16,0},{1,17},{17,1},{2,18},{18,2},{3,19},{19,3},{4,20},{20... | collective-permute-start | bytes 1990664 | tf_op jit(solution)/shard_map/ppermute | solution.py:243
Sparse Core Ops, SparseCore 0:
  23.8 48.7 all-gather.6
  74.7 40.6 all-gather.4

commit v12 on v11

--- a/solution.py
+++ b/solution.py
@@ -1,3 +1,5 @@
+import functools
+
 import jax
 import jax.numpy as jnp
 from jax import lax
@@ -160,7 +162,7 @@
             out[y, :, q * g : q * g + q] = dot(scaled[g], basis[y], 1, 1).astype(out.dtype)
 
 
-def back_out(part, rows, mine, other, keep, give, right):
+def back_out(side, part, rows, mine, other, out, right):
     q, wide = mine.shape[0], mine.shape[1] // 2
     low = part[0] == 0
     for g in range(4):
@@ -170,16 +172,21 @@
         right[g, :, wide // 2 :] = jnp.where(low, b, a)
     for x in range(4):
         for n in range(2):
-            total = jnp.zeros((wide, wide), jnp.float32)
+            total = jnp.zeros((2 * q, wide), jnp.float32)
             for b in range(2):
                 for h in range(2):
-                    left = rows[2 * x + b, n, :, wide * h : wide * h + wide]
+                    at = wide * h + q * side
+                    left = jnp.concatenate(
+                        [
+                            rows[2 * x + b, n, :, at : at + q],
+                            rows[2 * x + b, n, :, at + 2 * q : at + 3 * q],
+                        ],
+                        axis=1,
+                    )
                     total += dot(left, right[2 * b + h], 0, 0)
-            total = total.astype(keep.dtype)
+            total = total.astype(out.dtype)
             for z in range(2):
-                at = 2 * q * z
-                keep[2 * x + z, :, wide * n : wide * n + wide] = total[at : at + q]
-                give[2 * x + z, :, wide * n : wide * n + wide] = total[at + q : at + 2 * q]
+                out[2 * x + z, :, wide * n : wide * n + wide] = total[q * z : q * z + q]
 
 
 def body(grad_parts, basis_in, basis_out, eig_in, eig_out):
@@ -233,14 +240,17 @@
     back = scatter_sum(part, "y").astype(bf16)
     other = lax.ppermute(back, "z1", SWAP)
 
-    keep, give = run(
-        back_out,
-        (shape(8, half, cols), shape(8, half, cols)),
-        (part_z1, bo, back, other),
-        ((4, half, wide),),
-        flags=1,
-    )
-    part = (keep.astype(f32) + lax.ppermute(give, "c", SWAP).astype(f32)).astype(bf16)
+    def half_of_m(side):
+        return run(
+            functools.partial(back_out, side),
+            shape(8, half, cols),
+            (part_z1, bo, back, other),
+            ((4, half, wide),),
+            flags=1,
+        )
+
+    got = lax.ppermute(half_of_m(1), "c", SWAP)
+    part = (half_of_m(0).astype(f32) + got.astype(f32)).astype(bf16)
     part = lax.all_to_all(part, RING, 0, 0, tiled=True)
     return run(join_out, shape(rows, wide), (rep, part), flags=1)
 

time: 217 us -> 219 us (level)
  Pallas kernels: 11.2 us -> 14.7 us
    pallas_call x10 -> x11, Pallas kernels: 11.2 us -> 14.7 us  [run(): pl.pallas_call(kernel, out_shape=outs, in_specs=[pl.BlockSpec(memory_spac...]
  transfers between devices with their start and end apart: 12 -> 12, of which waited for: 9 -> 8; matrix products, arithmetic and copies ran while one was open for 0% -> 0% of each run, Pallas kernels for 2% -> 3%
where the time goes in v12:
time: 219 us; the launch traced here: 218 us
  blocking collectives  87.9 us (40%)
  waiting for transfers between devices  47.7 us (22%)
  starting transfers between devices  47.4 us (22%)
  Pallas kernels  14.7 us (7%)
  between operations  13.6 us (6%)
  local copies, waits for them, and re-layouts  5.32 us (2%)
    all_to_all x1, blocking collectives, body(): grad = lax.all_to_all(grad, 'y', 0, 0, tiled=True)  21.9 us
    all_to_all x1, blocking collectives, scatter_sum(): got = lax.all_to_all(blocks, axes, 0, 0, tiled=True)  20.6 us
    all_to_all x1, blocking collectives, body(): turned = lax.all_to_all(turned, RING, 0, 0, tiled=True)  17.2 us
    pallas_call x11, Pallas kernels, run(): pl.pallas_call(kernel, out_shape=outs, in_specs=[pl.BlockSpec(memory_spac...  14.7 us
    all_to_all x1, blocking collectives, body(): part = lax.all_to_all(part, RING, 0, 0, tiled=True)  14.7 us
    all_to_all x1, blocking collectives, body(): scaled = lax.all_to_all(scaled, PART, 0, 0, tiled=True)  13.4 us
    ppermute x3, starting transfers between devices, to_part(): return lax.ppermute(block, PART, [(i, i ^ d) for i in range(4)])  12.7 us
    all_gather x1, waiting for transfers between devices, body(): bi = lax.all_gather(bi, RING, axis=0)  12.3 us
  transfers between devices with their start and end apart: 12, of which 8 were waited for; matrix products, arithmetic and copies ran while one was open for 0% of the time, Pallas kernels for 3%

profile of v12, /device:TPU:1, one launch (start us, length us, event | category | flops | bytes accessed | tf_op | source)
XLA Modules:
  0.0 217.9 jit_solution(184796840884829402)
XLA Ops:
  6.5 1.1 convert_element_type.14
  7.6 7.2 %collective-permute-start.1 = (bf16[144,576]{1,0:T(8,128)(2,1)S(1)}, bf16[144,576]{1,0:T(8,128)(2,1)S(1)}, u32[]{:S(2)}, u32[]{:S(2)}) collective-permute-start(bf16[144,576]{1,0:T(8,128)(2,1)S(1)} %convert_element_type.14), channel_id=1, source_target_pairs={{0,0},{1,16},{16,64},{17,80},{32,1},{33,17},{48,65},{49,81},{64,32... | collective-permute-start | bytes 497672 | tf_op jit(solution)/shard_map/ppermute | solution.py:209
  14.8 8.1 %collective-permute-done.1 = bf16[144,576]{1,0:T(8,128)(2,1)S(1)} collective-permute-done((bf16[144,576]{1,0:T(8,128)(2,1)S(1)}, bf16[144,576]{1,0:T(8,128)(2,1)S(1)}, u32[]{:S(2)}, u32[]{:S(2)}) %collective-permute-start.1) | collective-permute-done | bytes 165920 | tf_op jit(solution)/shard_map/ppermute | solution.py:209
  23.7 0.9 copy-done.6
  25.4 4.5 %all-to-all-start = ((bf16[4,72,288]{2,1,0:T(8,128)(2,1)}), bf16[4,72,288]{2,1,0:T(8,128)(2,1)S(1)}, u32[]{:S(2)}, u32[]{:S(2)}) async-start(bf16[4,72,288]{2,1,0:T(8,128)(2,1)} %shard_map.56), calls=%async_computation | async-start | bytes 442368 | tf_op jit(solution)/shard_map/all_to_all | solution.py:217
  29.9 1.1 shard_map.55
  31.6 6.5 %all-to-all-done.got = bf16[4,72,288]{2,1,0:T(8,128)(2,1)S(1)} async-done(((bf16[4,72,288]{2,1,0:T(8,128)(2,1)}), bf16[4,72,288]{2,1,0:T(8,128)(2,1)S(1)}, u32[]{:S(2)}, u32[]{:S(2)}) %all-to-all-start) | async-done | bytes 165920 | tf_op jit(solution)/shard_map/all_to_all | solution.py:217
  38.3 21.9 %all_to_all.35.grad = bf16[8,72,576]{2,1,0:T(8,128)(2,1)S(1)} all-to-all(bf16[8,72,576]{2,1,0:T(8,128)(2,1)S(1)} %shard_map.57), channel_id=1, replica_groups=mesh['x'=4,'z1'=2,'z0'=2,'c'=2,'y'=8,'z2'=2] {'y'}, dimensions={0} | all-to-all | bytes 1327104 | tf_op jit(solution)/shard_map/all_to_all | solution.py:221
  60.3 12.3 %all-gather.7.cloned.1.call-done = bf16[1152,576]{1,0:T(8,128)(2,1)} async-done(((bf16[144,576]{1,0:T(8,128)(2,1)}), bf16[1152,576]{1,0:T(8,128)(2,1)}) %all-gather.7.cloned.1.call-update) | async-done | bytes 1327120 | tf_op jit(solution)/shard_map/all_gather | solution.py:211
  72.6 1.4 copy-done.3
  74.0 1.4 shard_map.58
  75.4 8.4 %collective-permute-start.2 = (bf16[72,576]{1,0:T(8,128)(2,1)S(1)}, bf16[72,576]{1,0:T(8,128)(2,1)S(1)}, u32[]{:S(2)}, u32[]{:S(2)}) collective-permute-start(bf16[72,576]{1,0:T(8,128)(2,1)S(1)} %get-tuple-element.22), channel_id=1, source_target_pairs={{0,1},{1,0},{64,65},{65,64},{2,3},{3,2},{66,67},{67,66},{4,5},{5,4... | collective-permute-start | bytes 248840 | tf_op jit(solution)/shard_map/ppermute | solution.py:127
  83.8 2.4 %collective-permute-start.3 = (bf16[72,576]{1,0:T(8,128)(2,1)S(1)}, bf16[72,576]{1,0:T(8,128)(2,1)S(1)}, u32[]{:S(2)}, u32[]{:S(2)}) collective-permute-start(bf16[72,576]{1,0:T(8,128)(2,1)S(1)} %get-tuple-element.23), channel_id=1, source_target_pairs={{0,64},{1,65},{64,0},{65,1},{2,66},{3,67},{66,2},{67,3},{4,68},{5,... | collective-permute-start | bytes 248840 | tf_op jit(solution)/shard_map/ppermute | solution.py:127
  86.2 1.9 collective-permute-start.4
  88.1 5.1 %collective-permute-done.3.p2 = bf16[72,576]{1,0:T(8,128)(2,1)S(1)} collective-permute-done((bf16[72,576]{1,0:T(8,128)(2,1)S(1)}, bf16[72,576]{1,0:T(8,128)(2,1)S(1)}, u32[]{:S(2)}, u32[]{:S(2)}) %collective-permute-start.3) | collective-permute-done | bytes 82976 | tf_op jit(solution)/shard_map/ppermute | solution.py:127
  93.2 1.1 collective-permute-done.4.p3
  94.4 17.2 %all_to_all.36.own = bf16[8,72,576]{2,1,0:T(8,128)(2,1)S(1)} all-to-all(bf16[8,72,576]{2,1,0:T(8,128)(2,1)S(1)} %shard_map.59), channel_id=1, replica_groups=mesh['x'=4,'z1'=2,'z0'=2,'c'=2,'y'=8,'z2'=2] {'x','z0'}, dimensions={0} | all-to-all | bytes 1327104 | tf_op jit(solution)/shard_map/all_to_all | solution.py:230
  111.6 4.2 %collective-permute-start.5 = (bf16[8,72,576]{2,1,0:T(8,128)(2,1)S(1)}, bf16[8,72,576]{2,1,0:T(8,128)(2,1)S(1)}, u32[]{:S(2)}, u32[]{:S(2)}) collective-permute-start(bf16[8,72,576]{2,1,0:T(8,128)(2,1)S(1)} %all_to_all.36.own), channel_id=1, source_target_pairs={{0,16},{16,0},{1,17},{17,1},{2,18},{18,2},{3,19},{19,3},{4,20},{20... | collective-permute-start | bytes 1990664 | tf_op jit(solution)/shard_map/ppermute | solution.py:231
  115.9 1.8 collective-permute-done.5.other
  117.7 1.4 copy-done.1
  119.0 1.9 shard_map.60
  121.0 4.9 %all-to-all-start.3 = ((bf16[4,72,576]{2,1,0:T(8,128)(2,1)}), bf16[4,72,576]{2,1,0:T(8,128)(2,1)S(1)}, u32[]{:S(2)}, u32[]{:S(2)}) async-start(bf16[4,72,576]{2,1,0:T(8,128)(2,1)} %shard_map.60), calls=%async_computation.3 | async-start | bytes 737280 | tf_op jit(solution)/shard_map/all_to_all | solution.py:235
  126.8 7.7 %all-to-all-done.3.got = bf16[4,72,576]{2,1,0:T(8,128)(2,1)S(1)} async-done(((bf16[4,72,576]{2,1,0:T(8,128)(2,1)}), bf16[4,72,576]{2,1,0:T(8,128)(2,1)S(1)}, u32[]{:S(2)}, u32[]{:S(2)}) %all-to-all-start.3) | async-done | bytes 331808 | tf_op jit(solution)/shard_map/all_to_all | solution.py:235
  134.6 13.4 %all_to_all.37.scaled = bf16[4,72,576]{2,1,0:T(8,128)(2,1)S(1)} all-to-all(bf16[4,72,576]{2,1,0:T(8,128)(2,1)S(1)} %shard_map.61), channel_id=1, replica_groups=mesh['x'=4,'z1'=2,'z0'=2,'c'=2,'y'=8,'z2'=2] {'z1','z2'}, dimensions={0} | all-to-all | bytes 663552 | tf_op jit(solution)/shard_map/all_to_all | solution.py:237
  148.1 2.6 %shard_map.62 = bf16[8,72,576]{2,1,0:T(8,128)(2,1)S(1)} custom-call(bf16[4,72,576]{2,1,0:T(8,128)(2,1)S(1)} %all_to_all.37.scaled, bf16[8,144,576]{2,1,0:T(8,128)(2,1)S(1)} %bitcast.13), custom_call_target="tpu_custom_call" | custom-call | flops 382205952 | bytes 2322432 | tf_op jit(solution)/shard_map/pallas_call | solution.py:45
  150.7 20.6 %all_to_all.38 = bf16[8,72,576]{2,1,0:T(8,128)(2,1)S(1)} all-to-all(bf16[8,72,576]{2,1,0:T(8,128)(2,1)S(1)} %shard_map.62), channel_id=1, replica_groups=mesh['x'=4,'z1'=2,'z0'=2,'c'=2,'y'=8,'z2'=2] {'y'}, dimensions={0} | all-to-all | bytes 1327104 | tf_op jit(solution)/shard_map/all_to_all | solution.py:19
  171.3 2.5 %collective-permute-start.6 = (bf16[72,576]{1,0:T(8,128)(2,1)S(1)}, bf16[72,576]{1,0:T(8,128)(2,1)S(1)}, u32[]{:S(2)}, u32[]{:S(2)}) collective-permute-start(bf16[72,576]{1,0:T(8,128)(2,1)S(1)} %reduce_sum.12.mine), channel_id=1, source_target_pairs={{0,64},{64,0},{1,65},{65,1},{2,66},{66,2},{3,67},{67,3},{4,68},{68... | collective-permute-start | bytes 248840 | tf_op jit(solution)/shard_map/ppermute | solution.py:241
  173.8 4.9 %collective-permute-done.6.other = bf16[72,576]{1,0:T(8,128)(2,1)S(1)} collective-permute-done((bf16[72,576]{1,0:T(8,128)(2,1)S(1)}, bf16[72,576]{1,0:T(8,128)(2,1)S(1)}, u32[]{:S(2)}, u32[]{:S(2)}) %collective-permute-start.6) | collective-permute-done | bytes 82976 | tf_op jit(solution)/shard_map/ppermute | solution.py:241
  178.7 3.3 %shard_map.64 = bf16[8,72,576]{2,1,0:T(8,128)(2,1)S(1)} custom-call(s32[1]{0:T(128)} %bitcast.1.part, bf16[8,2,72,576]{3,2,1,0:T(8,128)(2,1)S(1)} %bitcast.10, bf16[72,576]{1,0:T(8,128)(2,1)S(1)} %reduce_sum.12.mine, bf16[72,576]{1,0:T(8,128)(2,1)S(1)} %collective-permute-done.6.other), custom_call_target="tpu_custom_call" | custom-call | flops 382205952 | bytes 2156548 | tf_op jit(solution)/shard_map/pallas_call | solution.py:45
  182.0 10.8 %collective-permute-start.7 = (bf16[8,72,576]{2,1,0:T(8,128)(2,1)S(1)}, bf16[8,72,576]{2,1,0:T(8,128)(2,1)S(1)}, u32[]{:S(2)}, u32[]{:S(2)}) collective-permute-start(bf16[8,72,576]{2,1,0:T(8,128)(2,1)S(1)} %shard_map.64), channel_id=1, source_target_pairs={{0,16},{16,0},{1,17},{17,1},{2,18},{18,2},{3,19},{19,3},{4,20},{20... | collective-permute-start | bytes 1990664 | tf_op jit(solution)/shard_map/ppermute | solution.py:252
  192.7 2.6 %shard_map.63 = bf16[8,72,576]{2,1,0:T(8,128)(2,1)S(1)} custom-call(s32[1]{0:T(128)} %bitcast.1.part, bf16[8,2,72,576]{3,2,1,0:T(8,128)(2,1)S(1)} %bitcast.11, bf16[72,576]{1,0:T(8,128)(2,1)S(1)} %reduce_sum.12.mine, bf16[72,576]{1,0:T(8,128)(2,1)S(1)} %collective-permute-done.6.other), custom_call_target="tpu_custom_call" | custom-call | flops 382205952 | bytes 2156548 | tf_op jit(solution)/shard_map/pallas_call | solution.py:45
  195.5 14.7 %all_to_all.39.got = bf16[8,72,576]{2,1,0:T(8,128)(2,1)S(1)} all-to-all(bf16[8,72,576]{2,1,0:T(8,128)(2,1)S(1)} %add_convert_fusion), channel_id=1, replica_groups=mesh['x'=4,'z1'=2,'z0'=2,'c'=2,'y'=8,'z2'=2] {'x','z0'}, dimensions={0} | all-to-all | bytes 1327104 | tf_op jit(solution)/shard_map/all_to_all | solution.py:254
  (35 shorter events, 4.6 us)
Async XLA Ops:
  6.5 119.3 %copy-start = (f32[4608]{0:T(1024)S(1)}, f32[4608]{0:T(1024)}, u32[]{:S(2)}) copy-start(f32[4608]{0:T(1024)} %param.9) | copy-start | bytes 55300
  6.5 23.3 %copy-start.5 = (f32[144,576]{1,0:T(8,128)S(1)}, f32[144,576]{1,0:T(8,128)}, u32[]{:S(2)}) copy-start(f32[144,576]{1,0:T(8,128)} %rows.1) | copy-start | bytes 995332
  6.5 66.0 %all-gather.7.cloned.1.call-start = ((), (), s32[]{:S(2)}) async-start(), calls=%async_computation.8 | async-start | bytes 1658880 | tf_op jit(solution)/shard_map/all_gather | solution.py:211
  7.6 15.3 %collective-permute-start.1 = (bf16[144,576]{1,0:T(8,128)(2,1)S(1)}, bf16[144,576]{1,0:T(8,128)(2,1)S(1)}, u32[]{:S(2)}, u32[]{:S(2)}) collective-permute-start(bf16[144,576]{1,0:T(8,128)(2,1)S(1)} %convert_element_type.14), channel_id=1, source_target_pairs={{0,0},{1,16},{16,64},{17,80},{32,1},{33,17},{48,65},{49,81},{64,32... | collective-permute-start | bytes 497672 | tf_op jit(solution)/shard_map/ppermute | solution.py:209
  23.0 0.7 copy-start.8
  23.7 0.9 copy-start.6
  25.4 12.8 %all-to-all-start = ((bf16[4,72,288]{2,1,0:T(8,128)(2,1)}), bf16[4,72,288]{2,1,0:T(8,128)(2,1)S(1)}, u32[]{:S(2)}, u32[]{:S(2)}) async-start(bf16[4,72,288]{2,1,0:T(8,128)(2,1)} %shard_map.56), calls=%async_computation | async-start | bytes 442368 | tf_op jit(solution)/shard_map/all_to_all | solution.py:217
  29.9 86.0 %all-gather.5.cloned.1.call-start = ((), (), s32[]{:S(2)}) async-start(), calls=%async_computation.7 | async-start | bytes 1658880 | tf_op jit(solution)/shard_map/all_gather | solution.py:224
  31.0 7.3 %collective-permute-start = (bf16[2,72,576]{2,1,0:T(8,128)(2,1)S(1)}, bf16[2,72,576]{2,1,0:T(8,128)(2,1)S(1)}, u32[]{:S(2)}, u32[]{:S(2)}) collective-permute-start(bf16[2,72,576]{2,1,0:T(8,128)(2,1)S(1)} %shard_map.55), channel_id=1, source_target_pairs={{0,0},{2,64},{4,4},{6,68},{8,8},{10,72},{12,12},{14,76},{64,2},{66... | collective-permute-start | bytes 497672 | tf_op jit(solution)/shard_map/ppermute | solution.py:214
  38.3 21.9 %copy-start.7 = (bf16[2,72,576]{2,1,0:T(8,128)(2,1)}, bf16[2,72,576]{2,1,0:T(8,128)(2,1)S(1)}, u32[]{:S(2)}) copy-start(bf16[2,72,576]{2,1,0:T(8,128)(2,1)S(1)} %collective-permute-done) | copy-start | bytes 497668
  72.6 1.4 copy-start.3
  75.4 12.7 %collective-permute-start.2 = (bf16[72,576]{1,0:T(8,128)(2,1)S(1)}, bf16[72,576]{1,0:T(8,128)(2,1)S(1)}, u32[]{:S(2)}, u32[]{:S(2)}) collective-permute-start(bf16[72,576]{1,0:T(8,128)(2,1)S(1)} %get-tuple-element.22), channel_id=1, source_target_pairs={{0,1},{1,0},{64,65},{65,64},{2,3},{3,2},{66,67},{67,66},{4,5},{5,4... | collective-permute-start | bytes 248840 | tf_op jit(solution)/shard_map/ppermute | solution.py:127
  83.8 9.5 %collective-permute-start.3 = (bf16[72,576]{1,0:T(8,128)(2,1)S(1)}, bf16[72,576]{1,0:T(8,128)(2,1)S(1)}, u32[]{:S(2)}, u32[]{:S(2)}) collective-permute-start(bf16[72,576]{1,0:T(8,128)(2,1)S(1)} %get-tuple-element.23), channel_id=1, source_target_pairs={{0,64},{1,65},{64,0},{65,1},{2,66},{3,67},{66,2},{67,3},{4,68},{5,... | collective-permute-start | bytes 248840 | tf_op jit(solution)/shard_map/ppermute | solution.py:127
  86.2 8.2 %collective-permute-start.4 = (bf16[72,576]{1,0:T(8,128)(2,1)S(1)}, bf16[72,576]{1,0:T(8,128)(2,1)S(1)}, u32[]{:S(2)}, u32[]{:S(2)}) collective-permute-start(bf16[72,576]{1,0:T(8,128)(2,1)S(1)} %get-tuple-element.24), channel_id=1, source_target_pairs={{0,65},{1,64},{64,1},{65,0},{2,67},{3,66},{66,3},{67,2},{4,69},{5,... | collective-permute-start | bytes 248840 | tf_op jit(solution)/shard_map/ppermute | solution.py:127
  111.6 6.0 %collective-permute-start.5 = (bf16[8,72,576]{2,1,0:T(8,128)(2,1)S(1)}, bf16[8,72,576]{2,1,0:T(8,128)(2,1)S(1)}, u32[]{:S(2)}, u32[]{:S(2)}) collective-permute-start(bf16[8,72,576]{2,1,0:T(8,128)(2,1)S(1)} %all_to_all.36.own), channel_id=1, source_target_pairs={{0,16},{16,0},{1,17},{17,1},{2,18},{18,2},{3,19},{19,3},{4,20},{20... | collective-permute-start | bytes 1990664 | tf_op jit(solution)/shard_map/ppermute | solution.py:231
  117.7 1.4 copy-start.1
  121.0 27.1 %copy-start.4 = (bf16[1152,576]{1,0:T(8,128)(2,1)S(1)}, bf16[1152,576]{1,0:T(8,128)(2,1)}, u32[]{:S(2)}) copy-start(bf16[1152,576]{1,0:T(8,128)(2,1)} %all-gather.7.cloned.1.call-done) | copy-start | bytes 3981316
  121.0 13.6 %all-to-all-start.3 = ((bf16[4,72,576]{2,1,0:T(8,128)(2,1)}), bf16[4,72,576]{2,1,0:T(8,128)(2,1)S(1)}, u32[]{:S(2)}, u32[]{:S(2)}) async-start(bf16[4,72,576]{2,1,0:T(8,128)(2,1)} %shard_map.60), calls=%async_computation.3 | async-start | bytes 737280 | tf_op jit(solution)/shard_map/all_to_all | solution.py:235
  150.6 28.1 %copy-start.2 = (bf16[16,72,576]{2,1,0:T(8,128)(2,1)S(1)}, bf16[16,72,576]{2,1,0:T(8,128)(2,1)}, u32[]{:S(2)}) copy-start(bf16[16,72,576]{2,1,0:T(8,128)(2,1)} %all-gather.5.cloned.1.call-done) | copy-start | bytes 3981316
  171.3 7.4 %collective-permute-start.6 = (bf16[72,576]{1,0:T(8,128)(2,1)S(1)}, bf16[72,576]{1,0:T(8,128)(2,1)S(1)}, u32[]{:S(2)}, u32[]{:S(2)}) collective-permute-start(bf16[72,576]{1,0:T(8,128)(2,1)S(1)} %reduce_sum.12.mine), channel_id=1, source_target_pairs={{0,64},{64,0},{1,65},{65,1},{2,66},{66,2},{3,67},{67,3},{4,68},{68... | collective-permute-start | bytes 248840 | tf_op jit(solution)/shard_map/ppermute | solution.py:241
  182.0 13.4 %collective-permute-start.7 = (bf16[8,72,576]{2,1,0:T(8,128)(2,1)S(1)}, bf16[8,72,576]{2,1,0:T(8,128)(2,1)S(1)}, u32[]{:S(2)}, u32[]{:S(2)}) collective-permute-start(bf16[8,72,576]{2,1,0:T(8,128)(2,1)S(1)} %shard_map.64), channel_id=1, source_target_pairs={{0,16},{16,0},{1,17},{17,1},{2,18},{18,2},{3,19},{19,3},{4,20},{20... | collective-permute-start | bytes 1990664 | tf_op jit(solution)/shard_map/ppermute | solution.py:252
Sparse Core Ops, SparseCore 0:
  23.8 48.7 all-gather.6
  74.7 40.6 all-gather.4
